TPU v7x, 32 devices: a whole 2x2x4 slice. The times are simulated.
32 devices in a mesh: groups: 2 (over y), pts: 4 (over z), ffn: 2 (over x), sub: 2 (over core).
Axes of the slice: x: 2, y: 2, z: 4, core: 2. Of those that a mesh axis runs over, the one named last changes fastest.
Arguments:
- points: bfloat16 [32768, 512], P(('groups', 'pts', 'ffn', 'sub')), parts along dimension 0, may hold values from -24 to 24
- part_sizes: int32 [32], P('groups'), parts along dimension 0, may hold values from 1 to 1024, 8192 in all
- norm1_gain: float32 [512], replicated, may hold values from 0.4 to 1.6
- fx_weight: bfloat16 [512, 512], replicated, may hold values from -0.25 to 0.25
- x_weight: bfloat16 [512, 512], replicated, may hold values from -0.25 to 0.25
- slice_weight: bfloat16 [32, 256], replicated, may hold values from -80 to 80
- temp_vector: float32 [32], replicated, may hold values from -1 to 1
- q_weight: bfloat16 [32, 32], replicated, may hold values from -60 to 60
- k_weight: bfloat16 [32, 32], replicated, may hold values from -1 to 1
- v_weight: bfloat16 [32, 32], replicated, may hold values from -1 to 1
- out_weight: bfloat16 [512, 512], replicated, may hold values from -0.25 to 0.25
- norm2_gain: float32 [512], replicated, may hold values from 0.4 to 1.6
- up_weight: bfloat16 [512, 2048], P(None, 'ffn'), may hold values from -0.25 to 0.25
- down_weight: bfloat16 [2048, 512], P('ffn'), may hold values from -0.125 to 0.125
Outputs:
- mixed: bfloat16 [32768, 512], P(('groups', 'pts', 'ffn', 'sub')), parts along dimension 0
There are 2 independent parts, one for each index of `groups`. A program takes and returns all parts, laid end to end along the dimension named above; an argument that names none is the same for every part. Nothing has to cross between parts.
Inputs may be any that keep to these rules, and one draw needn't show every extreme that they name: part_sizes[d] live rows fill the first slots of device d's 1024 slots in the order of pts+ffn+sub; they sum to 8192.
All inputs are finite; a program needn't handle non-finite values.
Results may differ from a plain program's by a relative error of at most 0.007.
The roundings to bfloat16 on the way count: a program that leaves them out, or rounds other values in their place, can miss the bound.
Values may be sent and summed in bfloat16 or wider, within the bound.
No kernel may reach another device: no remote copies, remote signals or barrier semaphores. Data moves between devices by JAX's collectives and lax.ppermute only.
A program may use at most 64 MiB of HBM per device.

v0:
```python
import math

import jax
import jax.numpy as jnp
from jax import lax
from jax.sharding import PartitionSpec as P

BAL = 512


eps_norm = 1e-05
eps_mass = 1e-05
highest_precision = lax.Precision.HIGHEST


def layer_norm(values, gain):
    wide_values = values.astype(jnp.float32)
    centered = wide_values - jnp.mean(wide_values, axis=-1, keepdims=True)
    variance = jnp.mean(centered * centered, axis=-1, keepdims=True)
    return centered * lax.rsqrt(variance + eps_norm) * gain


def softmax_last(logits):
    shifted = logits - jnp.max(logits, axis=-1, keepdims=True)
    raised = jnp.exp(shifted)
    return raised / jnp.sum(raised, axis=-1, keepdims=True)


def token_mixing(token_sums, weight_sums, q_weight, k_weight, v_weight, head_size):
    tokens = (token_sums / (weight_sums[:, :, None] + eps_mass)).astype(jnp.bfloat16)
    queries = jnp.einsum("hgd,de->hge", tokens, q_weight, preferred_element_type=jnp.float32)
    keys_all = jnp.einsum("hgd,de->hge", tokens, k_weight, preferred_element_type=jnp.float32)
    values_all = jnp.einsum("hgd,de->hge", tokens, v_weight, preferred_element_type=jnp.float32)
    scores = jnp.einsum("hgd,hkd->hgk", queries, keys_all, precision=highest_precision) / math.sqrt(
        head_size
    )
    probs = softmax_last(scores).astype(jnp.bfloat16)
    mixed_tokens = jnp.einsum(
        "hgk,hkd->hgd", probs, values_all.astype(jnp.bfloat16), preferred_element_type=jnp.float32
    )
    return mixed_tokens.astype(jnp.bfloat16)


def per_device(
    points,
    part_sizes,
    norm1_gain,
    fx_weight,
    x_weight,
    slice_weight,
    temp_vector,
    q_weight,
    k_weight,
    v_weight,
    out_weight,
    norm2_gain,
    up_weight,
    down_weight,
):
    devices = lax.axis_size(("pts", "ffn", "sub"))
    position = lax.axis_index(("pts", "ffn", "sub"))
    slot_count, width = points.shape
    head_size = temp_vector.shape[0]
    head_count = width // head_size
    group_width = 4 * head_size
    layer_depth = slot_count // devices
    dealt = lax.all_to_all(
        points.reshape(layer_depth, devices, width),
        ("pts", "ffn", "sub"),
        split_axis=1,
        concat_axis=1,
        tiled=True,
    )
    flat_rows = dealt.reshape(slot_count, width)
    slot_numbers = jnp.arange(layer_depth, dtype=jnp.int32)[:, None] * devices + position
    live_slots = (slot_numbers < part_sizes[None, :]).reshape(slot_count)
    places = jnp.cumsum(live_slots.astype(jnp.int32)) - 1
    filled = places[-1] + 1
    buffer_rows = BAL + devices
    targets = jnp.where(live_slots, places, buffer_rows)
    sources = (
        jnp.zeros((buffer_rows,), jnp.int32)
        .at[targets]
        .set(jnp.arange(slot_count, dtype=jnp.int32), mode="drop")
    )
    packed = flat_rows[sources]
    packed_valid = jnp.arange(buffer_rows, dtype=jnp.int32) < filled
    row_total = packed.shape[0]
    normed = layer_norm(packed, norm1_gain).astype(jnp.bfloat16)
    features = jnp.dot(normed, fx_weight, preferred_element_type=jnp.float32).astype(jnp.bfloat16)
    middles = jnp.dot(normed, x_weight, preferred_element_type=jnp.float32).astype(jnp.bfloat16)
    valid_wide = packed_valid.astype(jnp.float32)[:, None, None]
    valid_narrow = packed_valid.astype(jnp.bfloat16)[:, None, None]
    stored = []
    sum_parts = []
    mass_parts = []
    for group_index in range(head_count // 4):
        lower = group_index * group_width
        middle_group = middles[:, lower : lower + group_width].reshape(row_total, 4, head_size)
        feature_group = features[:, lower : lower + group_width].reshape(row_total, 4, head_size)
        temps = 0.5 + jax.nn.softplus(
            jnp.einsum(
                "rhd,d->rh",
                middle_group.astype(jnp.float32),
                temp_vector,
                precision=highest_precision,
            )
        )
        logits = jnp.einsum(
            "rhd,dg->rhg", middle_group, slice_weight, preferred_element_type=jnp.float32
        )
        weights = softmax_last(logits / temps[:, :, None])
        group_mass = jnp.sum(weights * valid_wide, axis=0)
        narrow = weights.astype(jnp.bfloat16)
        stored.append(narrow)
        group_totals = jnp.einsum(
            "rhg,rhd->hgd", narrow * valid_narrow, feature_group, preferred_element_type=jnp.float32
        )
        sum_parts.append(group_totals)
        mass_parts.append(group_mass)
    token_sums = jnp.concatenate(sum_parts, 0)
    weight_sums = jnp.concatenate(mass_parts, 0)
    token_sums, weight_sums = lax.psum((token_sums, weight_sums), ("pts", "ffn", "sub"))
    mixed_tokens = token_mixing(token_sums, weight_sums, q_weight, k_weight, v_weight, head_size)
    spread_parts = []
    for group_index in range(head_count // 4):
        head_tokens = mixed_tokens[4 * group_index : 4 * group_index + 4]
        spread_group = jnp.einsum(
            "rhg,hgd->rhd", stored[group_index], head_tokens, preferred_element_type=jnp.float32
        )
        spread_parts.append(spread_group.astype(jnp.bfloat16).reshape(row_total, group_width))
    desliced = jnp.concatenate(spread_parts, 1)
    residual = packed.astype(jnp.float32) + jnp.dot(
        desliced, out_weight, preferred_element_type=jnp.float32
    )
    normed_late = layer_norm(residual, norm2_gain).astype(jnp.bfloat16)
    up_full = lax.all_gather(up_weight, "ffn", axis=1, tiled=True)
    down_full = lax.all_gather(down_weight, "ffn", axis=0, tiled=True)
    hidden = jax.nn.gelu(
        jnp.dot(normed_late, up_full, preferred_element_type=jnp.float32), approximate=False
    ).astype(jnp.bfloat16)
    update = jnp.dot(hidden, down_full, preferred_element_type=jnp.float32)
    finished = jnp.where(packed_valid[:, None], residual + update, 0.0).astype(jnp.bfloat16)
    unpacked = finished[jnp.clip(places, 0, buffer_rows - 1)]
    unpacked = jnp.where(live_slots[:, None], unpacked, jnp.zeros((), jnp.bfloat16))
    returned = lax.all_to_all(
        unpacked.reshape(layer_depth, devices, width),
        ("pts", "ffn", "sub"),
        split_axis=1,
        concat_axis=1,
        tiled=True,
    )
    return returned.reshape(slot_count, width)


def solution(mesh):
    return jax.shard_map(
        per_device,
        mesh=mesh,
        in_specs=(
            P(("groups", "pts", "ffn", "sub"), None),
            P("groups"),
            P(),
            P(),
            P(),
            P(),
            P(),
            P(),
            P(),
            P(),
            P(),
            P(),
            P(None, "ffn"),
            P("ffn", None),
        ),
        out_specs=P(("groups", "pts", "ffn", "sub"), None),
        check_vma=False,
    )
```

profile of v0, /device:TPU:1, one launch (start us, length us, event | category | flops | bytes accessed | tf_op | source)
XLA Modules:
  0.0 281.1 jit_solution(13280779587042761999)
XLA Ops:
  7.4 2.8 %copy.63 = bf16[64,16,512]{2,0,1:T(8,128)(2,1)} copy(bf16[64,16,512]{2,1,0:T(8,128)(2,1)} %bitcast.172) | data formatting | bytes 2097152 | tf_op jit(solution)/shard_map/reshape | solution.py:68
  10.2 7.3 %all-to-all-start = ((bf16[64,16,512]{2,0,1:T(8,128)(2,1)}), bf16[64,16,512]{2,0,1:T(8,128)(2,1)S(1)}, u32[]{:S(2)}, u32[]{:S(2)}) async-start(bf16[64,16,512]{2,0,1:T(8,128)(2,1)} %copy.63), calls=%async_computation | async-start | bytes 2097152 | tf_op jit(solution)/shard_map/all_to_all | solution.py:67
  18.6 0.6 slice.48
  19.3 4.3 %scatter_custom_fusion = s32[528]{0:T(1024)S(1)} fusion(s32[1024]{0:T(1024)S(1)} %bitcast.191, s32[1024]{0:T(1024)S(1)} %iota.37, s32[]{:T(128)} %constant.55.clone.1), kind=kCustom, calls=%fused_computation.154 | custom fusion | bytes 2116 | tf_op jit(solution)/shard_map/scatter | solution.py:84
  24.3 16.4 %all-to-all-done = bf16[64,16,512]{2,0,1:T(8,128)(2,1)S(1)} async-done(((bf16[64,16,512]{2,0,1:T(8,128)(2,1)}), bf16[64,16,512]{2,0,1:T(8,128)(2,1)S(1)}, u32[]{:S(2)}, u32[]{:S(2)}) %all-to-all-start) | async-done | bytes 1048608 | tf_op jit(solution)/shard_map/all_to_all | solution.py:67
  40.7 0.6 copy.64
  41.3 2.9 %gather_fusion = bf16[528,512]{1,0:T(8,128)(2,1)S(1)} fusion(bf16[1024,512]{1,0:T(8,128)(2,1)S(1)} %bitcast.170, s32[1024]{0:T(1024)S(1)} %pad_clamp_fusion), kind=kCustom, calls=%fused_computation | custom fusion | bytes 1083456 | tf_op jit(solution)/shard_map/gather | solution.py:86
  45.5 0.7 fusion.104
  46.9 0.7 fusion.102
  48.0 2.3 fusion.151
  50.3 2.3 fusion.154
  52.8 0.7 fusion.106
  54.0 2.3 fusion.148
  56.4 0.7 fusion.108
  57.6 2.3 fusion.145
  61.2 5.1 %multiply_reduce_fusion.3 = (f32[4,256]{1,0:T(4,128)S(1)}, f32[4,256]{1,0:T(4,128)S(1)}, f32[4,256]{1,0:T(4,128)S(1)}, f32[4,256]{1,0:T(4,128)S(1)}, bf16[528,4,...) fusion(f32[528]{0:T(1024)S(1)} %get-tuple-element.33, ...), kind=kLoop, calls=%fused_computation.29 | loop fusion | flops 8646656 | bytes 13028416 | tf_op jit(solution)/shard_map/reduce_sum | solution.py:113
  68.0 0.8 pad_maximum_fusion
  68.9 0.5 all-gather.3.cloned.1.call-update
  69.5 0.5 all-gather.5.cloned.1.call-update
  70.2 58.8 %psum.15 = f32[16,256]{1,0:T(8,128)S(1)} all-reduce(f32[16,256]{1,0:T(8,128)S(1)} %pad_maximum_fusion.1), channel_id=1, replica_groups=mesh['groups'=2,'pts'=4,'ffn'=2,'sub'=2] {'pts','ffn','sub'}, use_global_device_ids=true, to_apply=%region_18.19 | all-reduce | flops 4096 | bytes 32768 | tf_op jit(solution)/shard_map/psum | solution.py:123
  129.0 68.1 %all-reduce.2.cloned.1.call-done = f32[16,256,32]{1,2,0:T(8,128)} async-done(((f32[16,256,32]{1,2,0:T(8,128)}), f32[16,256,32]{1,2,0:T(8,128)}) %all-reduce.2.cloned.1.call-update) | async-done | bytes 524304 | tf_op jit(solution)/shard_map/psum | solution.py:123
  197.1 1.1 divide_convert_fusion
  198.7 5.0 %convolution_multiply_fusion = f32[16,256,256]{2,1,0:T(8,128)} fusion(f32[16,256,32]{1,2,0:T(8,128)S(1)} %fusion.88, f32[16,256,32]{1,2,0:T(8,128)S(1)} %fusion.86), kind=kOutput, calls=%fused_computation.35 | convolution fusion | flops 403701760 | bytes 5242880 | tf_op jit(solution)/shard_map/hgd,hkd->hgk/dot_general | solution.py:34
  203.8 1.9 fusion.84
  205.7 12.7 %online-softmax = f32[16,256,32]{2,1,0:T(8,128)} custom-call(f32[16,256,256]{2,1,0:T(8,128)} %convolution_multiply_fusion, f32[16,256,32]{2,1,0:T(8,128)} %fusion.84), custom_call_target="tpu_custom_call" | custom-call | tf_op online-softmax
  218.3 1.9 convert_element_type.106
  222.5 0.6 fusion.157
  223.5 13.2 %fusion.24 = bf16[528,512]{1,0:T(8,128)(2,1)S(1)} fusion(f32[528,512]{1,0:T(8,128)S(1)} %get-tuple-element.32, bf16[2048,512]{1,0:T(8,128)(2,1)} %all-gather.5.cloned.1.call-done, bf16[512,2048]{1,0:T(8,128)(2,1)} %all-gather.3.cloned.1.call-done, f32[512]{0:T(512)S(1)} %copy-done.16, f32[528]{0:T(1024)S(1)} %add_rsqrt_fusion, ...), kind=kOutput, calls=%fused_computation.49 | convolution fusion | flops 2286772224 | bytes 5823120 | tf_op jit(solution)/shard_map/dot_general | solution.py:142
  236.7 4.0 %gather_fusion.1 = bf16[1024,512]{1,0:T(8,128)(2,1)S(1)} fusion(bf16[528,512]{1,0:T(8,128)(2,1)S(1)} %fusion.24, s32[1024]{0:T(1024)S(1)} %broadcast_clamp_fusion), kind=kCustom, calls=%fused_computation.1 | custom fusion | bytes 2101248 | tf_op jit(solution)/shard_map/gather | solution.py:144
  240.7 1.2 copy_select_fusion
  241.9 30.2 %all_to_all.10 = bf16[64,16,512]{2,0,1:T(8,128)(2,1)S(1)} all-to-all(bf16[64,16,512]{2,0,1:T(8,128)(2,1)S(1)} %copy_select_fusion), channel_id=1, replica_groups=mesh['groups'=2,'pts'=4,'ffn'=2,'sub'=2] {'pts','ffn','sub'}, dimensions={1} | all-to-all | bytes 2097152 | tf_op jit(solution)/shard_map/all_to_all | solution.py:146
  272.1 1.5 copy.82
  (102 shorter events, 10.9 us)
Async XLA Ops:
  7.4 215.1 %copy-start = (bf16[512,512]{1,0:T(8,128)(2,1)S(1)}, bf16[512,512]{1,0:T(8,128)(2,1)}, u32[]{:S(2)}) copy-start(bf16[512,512]{1,0:T(8,128)(2,1)} %param.24) | copy-start | bytes 1572868
  7.4 10.4 %copy-start.11 = (s32[16]{0:T(128)S(1)}, s32[16]{0:T(128)}, u32[]{:S(2)}) copy-start(s32[16]{0:T(128)} %param.15) | copy-start | bytes 196
  10.2 30.5 %all-to-all-start = ((bf16[64,16,512]{2,0,1:T(8,128)(2,1)}), bf16[64,16,512]{2,0,1:T(8,128)(2,1)S(1)}, u32[]{:S(2)}, u32[]{:S(2)}) async-start(bf16[64,16,512]{2,0,1:T(8,128)(2,1)} %copy.63), calls=%async_computation | async-start | bytes 2097152 | tf_op jit(solution)/shard_map/all_to_all | solution.py:67
  17.5 179.5 %all-reduce.2.cloned.1.call-start = ((), (), s32[]{:S(2)}) async-start(), calls=%async_computation.2 | async-start | bytes 1048576 | tf_op jit(solution)/shard_map/psum | solution.py:123
  41.3 3.5 %copy-start.12 = (bf16[512,512]{1,0:T(8,128)(2,1)S(1)}, bf16[512,512]{1,0:T(8,128)(2,1)}, u32[]{:S(2)}) copy-start(bf16[512,512]{1,0:T(8,128)(2,1)} %param.18) | copy-start | bytes 1572868
  41.3 3.5 %copy-start.15 = (f32[512]{0:T(512)S(1)}, f32[512]{0:T(512)}, u32[]{:S(2)}) copy-start(f32[512]{0:T(512)} %param.16) | copy-start | bytes 6148
  44.4 1.2 copy-start.10
  46.3 1.8 copy-start.14
  57.6 2.3 copy-start.13
  66.2 1.7 copy-start.1
  66.2 1.8 copy-start.3
  66.3 1.8 copy-start.5
  68.0 130.2 %copy-start.7 = (bf16[32,32]{1,0:T(8,128)(2,1)S(1)}, bf16[32,32]{1,0:T(8,128)(2,1)}, u32[]{:S(2)}) copy-start(bf16[32,32]{1,0:T(8,128)(2,1)} %param.22) | copy-start | bytes 6148
  68.9 129.6 %copy-start.8 = (bf16[32,32]{1,0:T(8,128)(2,1)S(1)}, bf16[32,32]{1,0:T(8,128)(2,1)}, u32[]{:S(2)}) copy-start(bf16[32,32]{1,0:T(8,128)(2,1)} %param.21) | copy-start | bytes 6148
  68.9 154.6 %all-gather.3.cloned.1.call-start = ((), (), s32[]{:S(2)}) async-start(), calls=%async_computation.3 | async-start | bytes 3145728 | tf_op jit(solution)/shard_map/all_gather | solution.py:137
  69.5 154.0 %all-gather.5.cloned.1.call-start = ((), (), s32[]{:S(2)}) async-start(), calls=%async_computation.4 | async-start | bytes 3145728 | tf_op jit(solution)/shard_map/all_gather | solution.py:138
  198.7 5.1 %copy-start.9 = (bf16[32,32]{1,0:T(8,128)(2,1)S(1)}, bf16[32,32]{1,0:T(8,128)(2,1)}, u32[]{:S(2)}) copy-start(bf16[32,32]{1,0:T(8,128)(2,1)} %param.23) | copy-start | bytes 6148
  218.3 1.9 copy-start.6
  218.3 2.4 copy-start.4
  220.3 1.3 copy-start.2
  222.5 1.0 copy-start.16
Sparse Core Ops, SparseCore 0:
  69.0 128.0 all-reduce.1
Sparse Core Ops, SparseCore 1:
  70.9 35.0 all-gather.2
  107.4 33.4 all-gather.4
where the time goes:
time: 282 us; the launch traced here: 281 us
  blocking collectives  89 us (32%)
  waiting for transfers between devices  85.6 us (30%)
  matrix products  37.8 us (13%)
  local copies, waits for them, and re-layouts  20.9 us (7%)
  between operations  16 us (6%)
  Pallas kernels  12.7 us (5%)
  other arithmetic  11.7 us (4%)
  starting transfers between devices  7.44 us (3%)
    psum x1, waiting for transfers between devices, per_device(): lax.psum((token_sums, weight_sums), ('pts', 'ffn', 'sub'))  68.1 us
    psum x1, blocking collectives, per_device(): lax.psum((token_sums, weight_sums), ('pts', 'ffn', 'sub'))  58.8 us
    all_to_all x1, blocking collectives, per_device(): lax.all_to_all(unpacked.reshape(layer_depth, devices, width), ('pts', 'ff...  30.2 us
    all_to_all x1, waiting for transfers between devices, per_device(): lax.all_to_all(points.reshape(layer_depth, devices, width), ('pts', 'ffn'...  16.4 us
    dot_general x1, matrix products, per_device(): update = jnp.dot(hidden, down_full, preferred_element_type=jnp.float32)  13.2 us
    unnamed x1, Pallas kernels  12.7 us
    sub x4, matrix products, softmax_last(): shifted = logits - jnp.max(logits, axis=-1, keepdims=True)  9.23 us
    all_to_all x1, starting transfers between devices, per_device(): lax.all_to_all(points.reshape(layer_depth, devices, width), ('pts', 'ffn'...  7.32 us
  transfers between devices with their start and end apart: 4, of which 2 were waited for; matrix products, arithmetic and copies ran while one was open for 7% of the time, Pallas kernels for 5%

commit v1 on v0

v1 whole, which is shorter than its diff:
```python
import functools
import math

import jax
import jax.numpy as jnp
from jax import lax
from jax.experimental import pallas as pl
from jax.experimental.pallas import tpu as pltpu
from jax.sharding import PartitionSpec as P

eps_norm = 1e-05
eps_mass = 1e-05
f32 = jnp.float32
bf16 = jnp.bfloat16
MIB = 1024 * 1024
ROWS = 256


def dot(a, b):
    return jnp.dot(a, b, preferred_element_type=f32)


def layer_norm(wide, gain):
    centered = wide - jnp.mean(wide, axis=-1, keepdims=True)
    variance = jnp.mean(centered * centered, axis=-1, keepdims=True)
    return (centered * lax.rsqrt(variance + eps_norm) * gain).astype(bf16)


def gelu(x):
    z = jnp.clip(x * math.sqrt(0.5), -3.7439211627767994, 3.7439211627767994)
    q = z * z
    num = 0.00022905065861350646
    for c in (
        0.0034082910107109506,
        0.050955695062380861,
        0.18520832239976145,
        1.128379143519084,
    ):
        num = num * q + c
    den = -1.1791602954361697e-7
    for c in (
        0.000023547966471313185,
        0.0010179625278914885,
        0.014070470171167667,
        0.11098505178285362,
        0.49746925110067538,
        1.0,
    ):
        den = den * q + c
    return 0.5 * x * (1.0 + z * num / den)


def front_kernel(
    meta,
    points,
    gain,
    fx_weight,
    x_weight,
    slice_weight,
    temp_vector,
    stored,
    keep,
    send,
    slice_wide,
    temp_wide,
    totals,
):
    heads, head_size, slices = 16, slice_weight.shape[0], slice_weight.shape[1]
    heads = points.shape[1] // head_size
    per_tile = 128 // head_size
    half = heads // 2
    step = pl.program_id(0)

    @pl.when(step == 0)
    def _():
        totals[...] = jnp.zeros_like(totals)
        slice_wide[...] = jnp.zeros_like(slice_wide)
        for j in range(per_tile):
            slice_wide[j, j * head_size : (j + 1) * head_size, :] = slice_weight[...]
        row = lax.broadcasted_iota(jnp.int32, (head_size, head_size), 0)
        col = lax.broadcasted_iota(jnp.int32, (head_size, head_size), 1)
        spread = jnp.where(row == col, jnp.broadcast_to(temp_vector[...], (head_size, head_size)), 0.0)
        column = jnp.sum(spread, axis=1, keepdims=True)
        first = column.astype(bf16).astype(f32)
        second = (column - first).astype(bf16).astype(f32)
        third = column - first - second
        lane = lax.broadcasted_iota(jnp.int32, (head_size, 128), 1)
        for h in range(heads):
            block = jnp.where(lane == h, first, 0.0)
            block = jnp.where(lane == heads + h, second, block)
            block = jnp.where(lane == 2 * heads + h, third, block)
            temp_wide[h * head_size : (h + 1) * head_size, :] = block.astype(bf16)

    @pl.when(step * ROWS < meta[0])
    def _():
        normed = layer_norm(points[...].astype(f32), gain[...])
        features = dot(normed, fx_weight[...])
        middles = dot(normed, x_weight[...]).astype(bf16)
        features_t = features.T.astype(bf16)
        t = dot(middles, temp_wide[...])
        t = t + pltpu.roll(t, 128 - heads, 1) + pltpu.roll(t, 128 - 2 * heads, 1)
        temps = 0.5 + jnp.maximum(t, 0.0) + jnp.log(1.0 + jnp.exp(-jnp.abs(t)))
        scales = math.log2(math.e) / temps
        row = lax.broadcasted_iota(jnp.int32, (ROWS, 1), 0) + step * ROWS
        valid = jnp.where(row < meta[0], 1.0, 0.0)
        for h in range(heads):
            tile = (h // per_tile) * 128
            logits = dot(middles[:, tile : tile + 128], slice_wide[h % per_tile])
            logits = logits * scales[:, h : h + 1]
            top = jnp.max(logits, axis=-1, keepdims=True)
            raised = jnp.exp2(logits - top)
            weights = raised * (valid / jnp.sum(raised, axis=-1, keepdims=True))
            narrow = weights.astype(bf16)
            stored[:, h * slices : (h + 1) * slices] = narrow
            side, at = h // half, h % half
            totals[side, half * head_size + at : half * head_size + at + 1, :] += jnp.sum(
                weights, axis=0, keepdims=True
            )
            totals[side, at * head_size : (at + 1) * head_size, :] += dot(
                features_t[h * head_size : (h + 1) * head_size, :], narrow
            )

    @pl.when(step == pl.num_programs(0) - 1)
    def _():
        keep[...] = totals[meta[1]]
        send[...] = totals[1 - meta[1]]


def mix_kernel(first, second, q_weight, k_weight, v_weight, out):
    head_size = q_weight.shape[0]
    width = first.shape[1]
    half = (first.shape[0]) // (head_size + 1)
    slices = width
    span = half * head_size
    sums = first[...] + second[...]
    parts = []
    for h in range(half):
        mass = sums[span + h : span + h + 1, :] + eps_mass
        parts.append(sums[h * head_size : (h + 1) * head_size, :] / mass)
    tokens = jnp.concatenate(parts, 0).T.astype(bf16)
    total = jnp.zeros((slices, span), f32)
    lane = lax.broadcasted_iota(jnp.int32, (slices, span), 1)
    for h in range(half):
        own = tokens[:, h * head_size : (h + 1) * head_size]
        queries = dot(own, q_weight[...])
        keys = dot(own, k_weight[...])
        values = dot(own, v_weight[...]).astype(bf16)
        scores = lax.dot_general(
            queries,
            keys,
            (((1,), (1,)), ((), ())),
            precision=lax.Precision.HIGHEST,
            preferred_element_type=f32,
        ) / math.sqrt(head_size)
        top = jnp.max(scores, axis=-1, keepdims=True)
        raised = jnp.exp(scores - top)
        probs = (raised / jnp.sum(raised, axis=-1, keepdims=True)).astype(bf16)
        wide = jnp.concatenate([values.astype(f32)] * half, 1)
        wide = jnp.where(lax.div(lane, head_size) == h, wide, 0.0).astype(bf16)
        total = total + dot(probs, wide)
    out[...] = total.astype(bf16)


def back_kernel(
    meta, stored, points, mine, theirs, out_weight, gain, up, down, mixed, spread
):
    slices = mine.shape[0]
    half_width = mine.shape[1]
    width = points.shape[1]
    heads = stored.shape[1] // slices
    head_size = width // heads
    half = heads // 2
    step = pl.program_id(0)
    live = meta[0]

    @pl.when(step == 0)
    def _():
        lane = lax.broadcasted_iota(jnp.int32, (slices, half_width), 1)
        low = meta[1] == 0
        own = mine[...].astype(f32)
        other = theirs[...].astype(f32)
        for side in range(2):
            if side == 0:
                block = jnp.where(low, own, other)
            else:
                block = jnp.where(low, other, own)
            for h in range(half):
                at = (side * half + h) * slices
                spread[at : at + slices, :] = jnp.where(lax.div(lane, head_size) == h, block, 0.0).astype(bf16)

    @pl.when(step * ROWS < live)
    def _():
        middle = half * slices
        left = dot(stored[:, :middle], spread[:middle, :])
        right = dot(stored[:, middle:], spread[middle:, :])
        desliced = jnp.concatenate([left, right], 1).astype(bf16)
        residual = points[...].astype(f32) + dot(desliced, out_weight[...])
        late = layer_norm(residual, gain[...])
        total = residual
        chunk = 512
        for j in range(up.shape[0]):
            for c in range(up.shape[2] // chunk):
                hidden = gelu(dot(late, up[j, :, c * chunk : (c + 1) * chunk])).astype(bf16)
                total = total + dot(hidden, down[j, c * chunk : (c + 1) * chunk, :])
        row = lax.broadcasted_iota(jnp.int32, (ROWS, 1), 0) + step * ROWS
        mixed[...] = jnp.where(row < live, total, 0.0).astype(bf16)

    @pl.when(step * ROWS >= live)
    def _():
        mixed[...] = jnp.zeros_like(mixed)


def whole(shape):
    return pl.BlockSpec(shape, lambda i, m: (0,) * len(shape))


def per_device(
    mesh_shape,
    points,
    part_sizes,
    norm1_gain,
    fx_weight,
    x_weight,
    slice_weight,
    temp_vector,
    q_weight,
    k_weight,
    v_weight,
    out_weight,
    norm2_gain,
    up_weight,
    down_weight,
):
    axes = ("pts", "ffn", "sub")
    devices = math.prod(mesh_shape[a] for a in axes)
    position = lax.axis_index(axes)
    core = lax.axis_index("sub")
    rows, width = points.shape
    head_size, slices = slice_weight.shape
    heads = width // head_size
    half = heads // 2
    live = part_sizes[position]
    meta = jnp.stack([live, core.astype(jnp.int32)])
    steps = rows // ROWS
    up = lax.all_gather(up_weight, "ffn", axis=0)
    down = lax.all_gather(down_weight, "ffn", axis=0)

    sums_rows = half * (head_size + 1)
    last = lambda i, m: jnp.minimum(i, lax.div(m[0] - 1, ROWS))
    stored, keep, send = pl.pallas_call(
        front_kernel,
        grid_spec=pltpu.PrefetchScalarGridSpec(
            num_scalar_prefetch=1,
            grid=(steps,),
            in_specs=[
                pl.BlockSpec((ROWS, width), lambda i, m: (last(i, m), 0)),
                whole((1, width)),
                whole((width, width)),
                whole((width, width)),
                whole((head_size, slices)),
                whole((1, head_size)),
            ],
            out_specs=[
                pl.BlockSpec((ROWS, heads * slices), lambda i, m: (last(i, m), 0)),
                whole((sums_rows, slices)),
                whole((sums_rows, slices)),
            ],
            scratch_shapes=[
                pltpu.VMEM((128 // head_size, 128, slices), bf16),
                pltpu.VMEM((width, 128), bf16),
                pltpu.VMEM((2, sums_rows, slices), f32),
            ],
        ),
        out_shape=[
            jax.ShapeDtypeStruct((rows, heads * slices), bf16),
            jax.ShapeDtypeStruct((sums_rows, slices), f32),
            jax.ShapeDtypeStruct((sums_rows, slices), f32),
        ],
        compiler_params=pltpu.CompilerParams(vmem_limit_bytes=40 * MIB),
        name="front",
    )(
        meta,
        points,
        norm1_gain[None, :],
        fx_weight,
        x_weight,
        slice_weight,
        temp_vector[None, :],
    )

    received = lax.ppermute(send, "sub", [(0, 1), (1, 0)])
    chips = devices // 2
    bits = [2 << b for b in range(chips.bit_length() - 1)]
    turned = bits[1:] + bits[:1]
    sums = keep
    for even, odd in zip(bits, turned):
        sums = sums + received
        received = lax.ppermute(
            sums, axes, [(i, i ^ (odd if i & 1 else even)) for i in range(devices)]
        )
    mine = pl.pallas_call(
        mix_kernel,
        out_shape=jax.ShapeDtypeStruct((slices, half * head_size), bf16),
        compiler_params=pltpu.CompilerParams(vmem_limit_bytes=40 * MIB),
        name="mix",
    )(sums, received, q_weight, k_weight, v_weight)
    theirs = lax.ppermute(mine, "sub", [(0, 1), (1, 0)])

    return pl.pallas_call(
        back_kernel,
        grid_spec=pltpu.PrefetchScalarGridSpec(
            num_scalar_prefetch=1,
            grid=(steps,),
            in_specs=[
                pl.BlockSpec((ROWS, heads * slices), lambda i, m: (last(i, m), 0)),
                pl.BlockSpec((ROWS, width), lambda i, m: (last(i, m), 0)),
                whole(mine.shape),
                whole(mine.shape),
                whole((width, width)),
                whole((1, width)),
                whole(up.shape),
                whole(down.shape),
            ],
            out_specs=pl.BlockSpec((ROWS, width), lambda i, m: (i, 0)),
            scratch_shapes=[pltpu.VMEM((heads * slices, half * head_size), bf16)],
        ),
        out_shape=jax.ShapeDtypeStruct((rows, width), bf16),
        compiler_params=pltpu.CompilerParams(vmem_limit_bytes=48 * MIB),
        name="back",
    )(
        meta,
        stored,
        points,
        mine,
        theirs,
        out_weight,
        norm2_gain[None, :],
        up,
        down,
    )


def solution(mesh):
    return jax.shard_map(
        functools.partial(per_device, dict(mesh.shape)),
        mesh=mesh,
        in_specs=(
            P(("groups", "pts", "ffn", "sub"), None),
            P("groups"),
            P(),
            P(),
            P(),
            P(),
            P(),
            P(),
            P(),
            P(),
            P(),
            P(),
            P(None, "ffn"),
            P("ffn", None),
        ),
        out_specs=P(("groups", "pts", "ffn", "sub"), None),
        check_vma=False,
    )
```

time: 282 us -> 113 us (0.40)
  the two profiles are of different devices: /device:TPU:1 before, /device:TPU:5 now
where the time goes in v1:
time: 113 us; the launch traced here: 112 us
  Pallas kernels  55.9 us (49%)
  waiting for transfers between devices  31 us (27%)
  between operations  13.5 us (12%)
  local copies, waits for them, and re-layouts  7.09 us (6%)
  starting transfers between devices  4.2 us (4%)
    pallas_call x1, Pallas kernels, per_device(): pl.pallas_call(front_kernel, grid_spec=pltpu.PrefetchScalarGridSpec(num_s...  28.5 us
    ppermute x3, waiting for transfers between devices, per_device(): lax.ppermute(sums, axes, [(i, i ^ (odd if i & 1 else even)) for i in rang...  22.6 us
    pallas_call x1, Pallas kernels, per_device(): pl.pallas_call(back_kernel, grid_spec=pltpu.PrefetchScalarGridSpec(num_sc...  20.9 us
    unnamed x30, local copies, waits for them, and re-layouts  6.5 us
    pallas_call x1, Pallas kernels, per_device(): pl.pallas_call(mix_kernel, out_shape=jax.ShapeDtypeStruct((slices, half *...  6.46 us
    all_gather x1, waiting for transfers between devices, per_device(): down = lax.all_gather(down_weight, 'ffn', axis=0)  4.17 us
    ppermute x3, starting transfers between devices, per_device(): lax.ppermute(sums, axes, [(i, i ^ (odd if i & 1 else even)) for i in rang...  4.08 us
  transfers between devices with their start and end apart: 7, of which 6 were waited for; matrix products, arithmetic and copies ran while one was open for 1% of the time, Pallas kernels for 31%

profile of v1, /device:TPU:5, one launch (start us, length us, event | category | flops | bytes accessed | tf_op | source)
XLA Modules:
  0.0 112.5 jit_solution(13146695411899167002)
XLA Ops:
  6.5 0.0 copy-start.4
  6.6 0.0 copy-start.11
  6.6 0.0 all-gather.5.cloned.1.call-start
  6.6 0.7 all-gather.5.cloned.1.call-update
  7.3 0.0 all-gather.7.cloned.1.call-start
  7.3 0.7 all-gather.7.cloned.1.call-update
  8.1 0.0 copy-done.14
  8.1 0.6 dynamic_slice.3
  8.7 0.6 pad_add_fusion.meta
  9.3 0.0 copy-done.1
  9.3 0.0 copy-done.13
  9.3 0.0 copy-start.8
  9.4 0.0 copy-start.9
  9.4 0.0 copy-start.10
  9.4 28.5 %front.1 = (bf16[1024,4096]{1,0:T(8,128)(2,1)S(1)}, f32[264,256]{1,0:T(8,128)S(1)}, f32[264,256]{1,0:T(8,128)S(1)}) custom-call(s32[2]{0:T(128)S(1)} %pad_add_fusion.meta, bf16[1024,512]{1,0:T(8,128)(2,1)S(1)} %copy-done.1, f32[1,512]{1,0:T(1,128)S(1)} %bitcast.8, bf16[512,512]{1,0:T(8,128)(2,1)S(1)} %copy-done.4, bf16[512,512]{1,0:T(8,128)(2,1)S(1)} %copy-done.5, ...), custom_call_target="tpu_custom_call" | custom-call | tf_op jit(solution)/shard_map/front/pallas_call | solution.py:250
  37.9 3.3 %copy-done = bf16[1024,4096]{1,0:T(8,128)(2,1)} copy-done((bf16[1024,4096]{1,0:T(8,128)(2,1)}, bf16[1024,4096]{1,0:T(8,128)(2,1)S(1)}, u32[]{:S(2)}) %copy-start) | copy-done | bytes 8388632
  41.2 0.0 collective-permute-start
  41.2 1.5 %collective-permute-done = f32[264,256]{1,0:T(8,128)S(1)} collective-permute-done((f32[264,256]{1,0:T(8,128)S(1)}, f32[264,256]{1,0:T(8,128)S(1)}, u32[]{:S(2)}, u32[]{:S(2)}) %collective-permute-start) | collective-permute-done | bytes 270368 | tf_op jit(solution)/shard_map/ppermute | solution.py:291
  42.8 0.1 collective-permute-start.1
  42.9 5.6 %collective-permute-done.1 = f32[264,256]{1,0:T(8,128)S(1)} collective-permute-done((f32[264,256]{1,0:T(8,128)S(1)}, f32[264,256]{1,0:T(8,128)S(1)}, u32[]{:S(2)}, u32[]{:S(2)}) %collective-permute-start.1) | collective-permute-done | bytes 270368 | tf_op jit(solution)/shard_map/ppermute | solution.py:298
  48.5 2.7 %collective-permute-start.2 = (f32[264,256]{1,0:T(8,128)S(1)}, f32[264,256]{1,0:T(8,128)S(1)}, u32[]{:S(2)}, u32[]{:S(2)}) collective-permute-start(f32[264,256]{1,0:T(8,128)S(1)} %add.22), channel_id=1, source_target_pairs={{0,4},{1,9},{2,6},{3,11},{4,0},{5,13},{6,2},{7,15},{8,12},{9,1},{1... | collective-permute-start | bytes 811016 | tf_op jit(solution)/shard_map/ppermute | solution.py:298
  51.2 6.8 %collective-permute-done.2 = f32[264,256]{1,0:T(8,128)S(1)} collective-permute-done((f32[264,256]{1,0:T(8,128)S(1)}, f32[264,256]{1,0:T(8,128)S(1)}, u32[]{:S(2)}, u32[]{:S(2)}) %collective-permute-start.2) | collective-permute-done | bytes 270368 | tf_op jit(solution)/shard_map/ppermute | solution.py:298
  58.0 1.3 %collective-permute-start.3 = (f32[264,256]{1,0:T(8,128)S(1)}, f32[264,256]{1,0:T(8,128)S(1)}, u32[]{:S(2)}, u32[]{:S(2)}) collective-permute-start(f32[264,256]{1,0:T(8,128)S(1)} %add.23.first), channel_id=1, source_target_pairs={{0,8},{1,3},{2,10},{3,1},{4,12},{5,7},{6,14},{7,5},{8,0},{9,11},{1... | collective-permute-start | bytes 811016 | tf_op jit(solution)/shard_map/ppermute | solution.py:298
  59.3 10.2 %collective-permute-done.3.second = f32[264,256]{1,0:T(8,128)S(1)} collective-permute-done((f32[264,256]{1,0:T(8,128)S(1)}, f32[264,256]{1,0:T(8,128)S(1)}, u32[]{:S(2)}, u32[]{:S(2)}) %collective-permute-start.3) | collective-permute-done | bytes 270368 | tf_op jit(solution)/shard_map/ppermute | solution.py:298
  69.5 0.0 copy-done.9
  69.5 6.5 %mix.1.mine = bf16[256,256]{1,0:T(8,128)(2,1)S(1)} custom-call(f32[264,256]{1,0:T(8,128)S(1)} %add.23.first, f32[264,256]{1,0:T(8,128)S(1)} %collective-permute-done.3.second, bf16[32,32]{1,0:T(8,128)(2,1)S(1)} %copy-done.8, bf16[32,32]{1,0:T(8,128)(2,1)S(1)} %copy-done.9, bf16[32,32]{1,0:T(8,128)(2,1)S(1)} %copy-done.10), custom_call_target="tpu_custom_call" | custom-call | tf_op jit(solution)/shard_map/mix/pallas_call | solution.py:301
  76.0 0.0 collective-permute-start.4
  76.0 1.3 %collective-permute-done.4.theirs = bf16[256,256]{1,0:T(8,128)(2,1)S(1)} collective-permute-done((bf16[256,256]{1,0:T(8,128)(2,1)S(1)}, bf16[256,256]{1,0:T(8,128)(2,1)S(1)}, u32[]{:S(2)}, u32[]{:S(2)}) %collective-permute-start.4) | collective-permute-done | bytes 131104 | tf_op jit(solution)/shard_map/ppermute | solution.py:307
  77.4 4.2 %all-gather.7.cloned.1.call-done = bf16[2048,512]{1,0:T(8,128)(2,1)} async-done(((bf16[1024,512]{1,0:T(8,128)(2,1)}), bf16[2048,512]{1,0:T(8,128)(2,1)}) %all-gather.7.cloned.1.call-update) | async-done | bytes 2097168 | tf_op jit(solution)/shard_map/all_gather | solution.py:246
  81.5 1.6 %copy-done.2 = bf16[1024,1024]{1,0:T(8,128)(2,1)S(1)} copy-done((bf16[1024,1024]{1,0:T(8,128)(2,1)S(1)}, bf16[1024,1024]{1,0:T(8,128)(2,1)}, u32[]{:S(2)}) %copy-start.2) | copy-done | bytes 2097176
  83.1 1.6 %copy-done.3 = bf16[2048,512]{1,0:T(8,128)(2,1)S(1)} copy-done((bf16[2048,512]{1,0:T(8,128)(2,1)S(1)}, bf16[2048,512]{1,0:T(8,128)(2,1)}, u32[]{:S(2)}) %copy-start.3) | copy-done | bytes 2097176
  84.7 20.9 %back.1 = bf16[1024,512]{1,0:T(8,128)(2,1)} custom-call(s32[2]{0:T(128)S(1)} %pad_add_fusion.meta, bf16[1024,4096]{1,0:T(8,128)(2,1)} %copy-done, bf16[1024,512]{1,0:T(8,128)(2,1)S(1)} %copy-done.1, bf16[256,256]{1,0:T(8,128)(2,1)S(1)} %mix.1.mine, bf16[256,256]{1,0:T(8,128)(2,1)S(1)} %collective-permute-done.4.theirs, bf16[512,512]{1,0:T(8,128)(2,1)S(1)} %copy-done.6, ...), custom_call_target="tpu_custom_call" | custom-call | tf_op jit(solution)/shard_map/back/pallas_call | solution.py:309
  (22 shorter events, 0.1 us)
Async XLA Ops:
  6.5 1.5 %copy-start.14 = (s32[16]{0:T(128)S(1)}, s32[16]{0:T(128)}, u32[]{:S(2)}) copy-start(s32[16]{0:T(128)} %param.15) | copy-start | bytes 196
  6.5 2.8 %copy-start.1 = (bf16[1024,512]{1,0:T(8,128)(2,1)S(1)}, bf16[1024,512]{1,0:T(8,128)(2,1)}, u32[]{:S(2)}) copy-start(bf16[1024,512]{1,0:T(8,128)(2,1)} %points.3) | copy-start | bytes 3145732
  6.5 2.8 %copy-start.13 = (f32[32]{0:T(128)S(1)}, f32[32]{0:T(128)}, u32[]{:S(2)}) copy-start(f32[32]{0:T(128)} %param.20) | copy-start | bytes 388
  6.5 2.8 %copy-start.7 = (bf16[32,256]{1,0:T(8,128)(2,1)S(1)}, bf16[32,256]{1,0:T(8,128)(2,1)}, u32[]{:S(2)}) copy-start(bf16[32,256]{1,0:T(8,128)(2,1)} %slice_weight.1) | copy-start | bytes 49156
  6.5 2.8 %copy-start.5 = (bf16[512,512]{1,0:T(8,128)(2,1)S(1)}, bf16[512,512]{1,0:T(8,128)(2,1)}, u32[]{:S(2)}) copy-start(bf16[512,512]{1,0:T(8,128)(2,1)} %x_weight.1) | copy-start | bytes 1572868
  6.5 2.8 %copy-start.4 = (bf16[512,512]{1,0:T(8,128)(2,1)S(1)}, bf16[512,512]{1,0:T(8,128)(2,1)}, u32[]{:S(2)}) copy-start(bf16[512,512]{1,0:T(8,128)(2,1)} %fx_weight.1) | copy-start | bytes 1572868
  6.6 2.8 %copy-start.11 = (f32[512]{0:T(512)S(1)}, f32[512]{0:T(512)}, u32[]{:S(2)}) copy-start(f32[512]{0:T(512)} %param.16) | copy-start | bytes 6148
  6.6 70.8 %all-gather.5.cloned.1.call-start = ((), (), s32[]{:S(2)}) async-start(), calls=%async_computation | async-start | bytes 3145728 | tf_op jit(solution)/shard_map/all_gather | solution.py:245
  7.3 74.2 %all-gather.7.cloned.1.call-start = ((), (), s32[]{:S(2)}) async-start(), calls=%async_computation.1 | async-start | bytes 3145728 | tf_op jit(solution)/shard_map/all_gather | solution.py:246
  9.3 60.2 %copy-start.8 = (bf16[32,32]{1,0:T(8,128)(2,1)S(1)}, bf16[32,32]{1,0:T(8,128)(2,1)}, u32[]{:S(2)}) copy-start(bf16[32,32]{1,0:T(8,128)(2,1)} %q_weight.1) | copy-start | bytes 6148
  9.4 60.1 %copy-start.9 = (bf16[32,32]{1,0:T(8,128)(2,1)S(1)}, bf16[32,32]{1,0:T(8,128)(2,1)}, u32[]{:S(2)}) copy-start(bf16[32,32]{1,0:T(8,128)(2,1)} %k_weight.1) | copy-start | bytes 6148
  9.4 60.1 %copy-start.10 = (bf16[32,32]{1,0:T(8,128)(2,1)S(1)}, bf16[32,32]{1,0:T(8,128)(2,1)}, u32[]{:S(2)}) copy-start(bf16[32,32]{1,0:T(8,128)(2,1)} %v_weight.1) | copy-start | bytes 6148
  37.9 3.3 %copy-start = (bf16[1024,4096]{1,0:T(8,128)(2,1)}, bf16[1024,4096]{1,0:T(8,128)(2,1)S(1)}, u32[]{:S(2)}) copy-start(bf16[1024,4096]{1,0:T(8,128)(2,1)S(1)} %get-tuple-element.8.stored) | copy-start | bytes 25165828
  41.2 40.3 %copy-start.6 = (bf16[512,512]{1,0:T(8,128)(2,1)S(1)}, bf16[512,512]{1,0:T(8,128)(2,1)}, u32[]{:S(2)}) copy-start(bf16[512,512]{1,0:T(8,128)(2,1)} %out_weight.1) | copy-start | bytes 1572868
  41.2 40.4 %copy-start.12 = (f32[512]{0:T(512)S(1)}, f32[512]{0:T(512)}, u32[]{:S(2)}) copy-start(f32[512]{0:T(512)} %param.25) | copy-start | bytes 6148
  41.2 1.5 %collective-permute-start = (f32[264,256]{1,0:T(8,128)S(1)}, f32[264,256]{1,0:T(8,128)S(1)}, u32[]{:S(2)}, u32[]{:S(2)}) collective-permute-start(f32[264,256]{1,0:T(8,128)S(1)} %get-tuple-element.10), channel_id=1, source_target_pairs={{0,1},{1,0},{2,3},{3,2},{4,5},{5,4},{6,7},{7,6},{8,9},{9,8},{10,11... | collective-permute-start | bytes 811016 | tf_op jit(solution)/shard_map/ppermute | solution.py:291
  42.8 5.7 %collective-permute-start.1 = (f32[264,256]{1,0:T(8,128)S(1)}, f32[264,256]{1,0:T(8,128)S(1)}, u32[]{:S(2)}, u32[]{:S(2)}) collective-permute-start(f32[264,256]{1,0:T(8,128)S(1)} %add.21), channel_id=1, source_target_pairs={{0,2},{1,5},{2,0},{3,7},{4,6},{5,1},{6,4},{7,3},{8,10},{9,13},{10,... | collective-permute-start | bytes 811016 | tf_op jit(solution)/shard_map/ppermute | solution.py:298
  48.5 9.4 %collective-permute-start.2 = (f32[264,256]{1,0:T(8,128)S(1)}, f32[264,256]{1,0:T(8,128)S(1)}, u32[]{:S(2)}, u32[]{:S(2)}) collective-permute-start(f32[264,256]{1,0:T(8,128)S(1)} %add.22), channel_id=1, source_target_pairs={{0,4},{1,9},{2,6},{3,11},{4,0},{5,13},{6,2},{7,15},{8,12},{9,1},{1... | collective-permute-start | bytes 811016 | tf_op jit(solution)/shard_map/ppermute | solution.py:298
  58.0 11.5 %collective-permute-start.3 = (f32[264,256]{1,0:T(8,128)S(1)}, f32[264,256]{1,0:T(8,128)S(1)}, u32[]{:S(2)}, u32[]{:S(2)}) collective-permute-start(f32[264,256]{1,0:T(8,128)S(1)} %add.23.first), channel_id=1, source_target_pairs={{0,8},{1,3},{2,10},{3,1},{4,12},{5,7},{6,14},{7,5},{8,0},{9,11},{1... | collective-permute-start | bytes 811016 | tf_op jit(solution)/shard_map/ppermute | solution.py:298
  76.0 1.4 %collective-permute-start.4 = (bf16[256,256]{1,0:T(8,128)(2,1)S(1)}, bf16[256,256]{1,0:T(8,128)(2,1)S(1)}, u32[]{:S(2)}, u32[]{:S(2)}) collective-permute-start(bf16[256,256]{1,0:T(8,128)(2,1)S(1)} %mix.1.mine), channel_id=1, source_target_pairs={{0,1},{1,0},{2,3},{3,2},{4,5},{5,4},{6,7},{7,6},{8,9},{9,8},{10,11... | collective-permute-start | bytes 393224 | tf_op jit(solution)/shard_map/ppermute | solution.py:307
  81.5 1.6 %copy-start.2 = (bf16[1024,1024]{1,0:T(8,128)(2,1)S(1)}, bf16[1024,1024]{1,0:T(8,128)(2,1)}, u32[]{:S(2)}) copy-start(bf16[1024,1024]{1,0:T(8,128)(2,1)} %all-gather.5.cloned.1.call-done) | copy-start | bytes 6291460
  83.1 1.6 %copy-start.3 = (bf16[2048,512]{1,0:T(8,128)(2,1)S(1)}, bf16[2048,512]{1,0:T(8,128)(2,1)}, u32[]{:S(2)}) copy-start(bf16[2048,512]{1,0:T(8,128)(2,1)} %all-gather.7.cloned.1.call-done) | copy-start | bytes 6291460
Sparse Core Ops, SparseCore 0:
  8.9 34.3 all-gather.4
  44.9 36.5 all-gather.6

commit v2 on v0

v2 whole, which is shorter than its diff:
```python
import functools
import math

import jax
import jax.numpy as jnp
from jax import lax
from jax.experimental import pallas as pl
from jax.experimental.pallas import tpu as pltpu
from jax.sharding import PartitionSpec as P

eps_norm = 1e-05
eps_mass = 1e-05
f32 = jnp.float32
bf16 = jnp.bfloat16
MIB = 1024 * 1024
FRONT_ROWS = 256
BACK_ROWS = 512


def dot(a, b):
    return jnp.dot(a, b, preferred_element_type=f32)


def layer_norm(wide, gain):
    centered = wide - jnp.mean(wide, axis=-1, keepdims=True)
    variance = jnp.mean(centered * centered, axis=-1, keepdims=True)
    return (centered * lax.rsqrt(variance + eps_norm) * gain).astype(bf16)


def dot_nt(a, b):
    return lax.dot_general(a, b, (((1,), (1,)), ((), ())), preferred_element_type=f32)


def split3(x):
    first = x.astype(bf16)
    rest = x - first.astype(f32)
    second = rest.astype(bf16)
    third = (rest - second.astype(f32)).astype(bf16)
    return first, second, third


def gelu(x):
    halved = 0.5 * x
    return halved + halved * lax.erf(x * math.sqrt(0.5))


def head_tile(weight, copies):
    size = weight.shape[0]
    wide = jnp.concatenate([weight] * copies, 1)
    tall = jnp.concatenate([wide] * copies, 0)
    row = lax.broadcasted_iota(jnp.int32, tall.shape, 0)
    col = lax.broadcasted_iota(jnp.int32, tall.shape, 1)
    return jnp.where(lax.div(row, size) == lax.div(col, size), tall, 0.0)


def front_kernel(
    sizes,
    place,
    points,
    gain,
    fx_weight,
    x_weight,
    slice_weight,
    temp_vector,
    stored,
    keep,
    send,
    fx_t,
    x_t,
    slice_t,
    temp_t,
    feats,
    mids,
    masses,
    totals,
):
    head_size, slices = slice_weight.shape
    width = points.shape[1]
    heads = width // head_size
    half = heads // 2
    span = half * head_size
    step = pl.program_id(0)
    live = sizes[place[0]]
    core = place[0] % 2

    @pl.when(step == 0)
    def _():
        totals[...] = jnp.zeros_like(totals)
        masses[...] = jnp.zeros_like(masses)
        fx_t[...] = fx_weight[...].astype(f32).T.astype(bf16)
        x_t[...] = x_weight[...].astype(f32).T.astype(bf16)
        slice_t[...] = slice_weight[...].astype(f32).T.astype(bf16)
        wide = jnp.concatenate([temp_vector[...]] * heads, 1)
        row = lax.broadcasted_iota(jnp.int32, (heads, width), 0)
        col = lax.broadcasted_iota(jnp.int32, (heads, width), 1)
        block = jnp.where(lax.div(col, head_size) == row, jnp.broadcast_to(wide, (heads, width)), 0.0)
        for i, part in enumerate(split3(block)):
            temp_t[i * heads : (i + 1) * heads, :] = part

    @pl.when(step * FRONT_ROWS < live)
    def _():
        normed = layer_norm(points[...].astype(f32), gain[...])
        mids[...] = dot_nt(x_t[...], normed).astype(bf16)
        feats[...] = dot_nt(fx_t[...], normed).astype(bf16)
        t = dot(temp_t[...], mids[...])
        t = t[:heads] + t[heads : 2 * heads] + t[2 * heads : 3 * heads]
        temps = 0.5 + jnp.maximum(t, 0.0) + jnp.log(1.0 + jnp.exp(-jnp.abs(t)))
        scales = math.log2(math.e) / temps
        col = lax.broadcasted_iota(jnp.int32, (1, FRONT_ROWS), 1) + step * FRONT_ROWS
        valid = jnp.where(col < live, 1.0, 0.0)
        own = lambda h: slice(h * head_size, (h + 1) * head_size)
        logits = dot(slice_t[...], mids[own(0), :])
        before = None
        for h in range(heads):
            rows = slice(h * slices, (h + 1) * slices)
            ahead = dot(slice_t[...], mids[own(h + 1), :]) if h + 1 < heads else None
            mass, parts = None, []
            for c in range(FRONT_ROWS // 128):
                lanes = slice(c * 128, (c + 1) * 128)
                l = logits[:, lanes]
                top = jnp.max(l, axis=0, keepdims=True)
                raised = jnp.exp2((l - top) * scales[h : h + 1, lanes])
                total = jnp.sum(raised, axis=0, keepdims=True)
                weights = raised * (valid[:, lanes] * pltpu.reciprocal(total, approx=True))
                parts.append(weights.astype(bf16))
                mass = weights if mass is None else mass + weights
            masses[rows, :] += mass
            before = jnp.concatenate(parts, 1)
            stored[rows, :] = before
            logits = ahead
        for h in range(heads):
            side, at = h // half, h % half
            totals[side, at * head_size : (at + 1) * head_size, :] += dot_nt(feats[own(h), :], stored[h * slices : (h + 1) * slices, :])

    @pl.when(step == pl.num_programs(0) - 1)
    def _():
        for h in range(heads):
            mass = jnp.sum(masses[h * slices : (h + 1) * slices, :].T, axis=0, keepdims=True)
            totals[h // half, span + h % half : span + h % half + 1, :] = mass
        keep[...] = totals[core]
        send[...] = totals[1 - core]


def mix_kernel(first, second, q_weight, k_weight, v_weight, out, spread, queries, scores, probs):
    head_size = q_weight.shape[0]
    slices = first.shape[1]
    half = first.shape[0] // (head_size + 1)
    span = half * head_size
    sums = first[...] + second[...]
    parts = []
    for h in range(half):
        mass = sums[span + h : span + h + 1, :] + eps_mass
        parts.append(sums[h * head_size : (h + 1) * head_size, :] / mass)
    tokens_wide = jnp.concatenate(parts, 0).astype(bf16)
    crossed = head_tile(dot_nt(k_weight[...], q_weight[...]), half)
    asked = sum(dot(part, tokens_wide) for part in split3(crossed))
    for i, part in enumerate(split3(asked * (math.log2(math.e) / math.sqrt(head_size)))):
        for h in range(half):
            queries[h, i * head_size : (i + 1) * head_size, :] = part[h * head_size : (h + 1) * head_size, :]
    for h in range(half):
        queries[h, 3 * head_size :, :] = jnp.zeros_like(queries[h, 3 * head_size :, :])
    values = dot(head_tile(v_weight[...].astype(f32), half).T.astype(bf16), tokens_wide).astype(bf16)
    row = lax.broadcasted_iota(jnp.int32, (span, half * 128), 0)
    col = lax.broadcasted_iota(jnp.int32, (span, half * 128), 1)
    same = (lax.div(row, head_size) == lax.div(col, 128)) & (lax.rem(row, head_size) == lax.rem(col, head_size))
    repeat = jnp.where(same, 1.0, 0.0).astype(bf16)
    tokens = tokens_wide.astype(f32).T.astype(bf16)
    spread[...] = dot(tokens, repeat).astype(bf16)
    for h in range(half):
        scores[h] = dot(spread[:, h * 128 : (h + 1) * 128], queries[h])
    for h in range(half):
        top = jnp.max(scores[h], axis=0, keepdims=True)
        raised = jnp.exp2(scores[h] - top)
        total = jnp.sum(raised, axis=0, keepdims=True)
        probs[h] = (raised * pltpu.reciprocal(total, approx=True)).astype(bf16)
    for h in range(half):
        own = slice(h * head_size, (h + 1) * head_size)
        out[own, :] = dot(values[own, :], probs[h]).astype(bf16)


def back_kernel(sizes, place, stored, points, mine, theirs, out_weight, gain, up, down, *refs):
    extra = len(refs) - 6
    sent, (mixed, spread, desliced, ups, downs, arrived) = refs[:extra], refs[extra:]
    span, slices = mine.shape
    width = points.shape[1]
    heads = stored.shape[0] // slices
    head_size = width // heads
    piece = ups.shape[2]
    step = pl.program_id(0)
    live = sizes[place[0]]
    low = place[0] % 2 == 0

    sources = [
        (up.at[:, pl.ds(c * piece, piece)], down.at[pl.ds(c * piece, piece), :]) for c in range(2)
    ]
    if piece == width:
        sources += [(r.at[pl.ds(0, width), :], r.at[pl.ds(width, piece), :]) for r in sent]
    else:
        sources += [(sent[2 * i], sent[2 * i + 1]) for i in range(extra // 2)]

    def copies(n):
        return (
            pltpu.make_async_copy(sources[n][0], ups.at[n], arrived.at[2 * n]),
            pltpu.make_async_copy(sources[n][1], downs.at[n], arrived.at[2 * n + 1]),
        )

    @pl.when(step == 0)
    def _():
        for n in range(len(sources)):
            for copy in copies(n):
                copy.start()
        own = mine[...].astype(f32)
        other = theirs[...].astype(f32)
        spread[:span, :] = jnp.where(low, own, other).astype(bf16)
        spread[span:, :] = jnp.where(low, other, own).astype(bf16)

    @pl.when(step * BACK_ROWS < live)
    def _():
        for h in range(heads):
            own = slice(h * head_size, (h + 1) * head_size)
            desliced[own, :] = dot(spread[own, :], stored[h * slices : (h + 1) * slices, :])
        picked = desliced[...].T.astype(bf16)
        residual = points[...].astype(f32) + dot(picked, out_weight[...])
        late = layer_norm(residual, gain[...])
        total = residual

        @pl.when(step == 0)
        def _():
            for n in range(len(sources)):
                for copy in copies(n):
                    copy.wait()

        raw = dot(late, ups[0])
        for n in range(len(sources)):
            now = raw
            if n + 1 < len(sources):
                raw = dot(late, ups[n + 1])
            total = total + dot(gelu(now).astype(bf16), downs[n])
        row = lax.broadcasted_iota(jnp.int32, (BACK_ROWS, 1), 0) + step * BACK_ROWS
        mixed[...] = jnp.where(row < live, total, 0.0).astype(bf16)

    @pl.when(step * BACK_ROWS >= live)
    def _():
        mixed[...] = jnp.zeros_like(mixed)


def whole(shape):
    return pl.BlockSpec(shape, lambda i, s, p: (0,) * len(shape))


def front_call(sizes, place, points, gain, fx_weight, x_weight, slice_weight, temp_vector):
    rows, width = points.shape
    head_size, slices = slice_weight.shape
    heads = width // head_size
    sums_rows = heads // 2 * (head_size + 1)
    last = lambda i, s, p: jnp.minimum(i, lax.div(s[p[0]] - 1, FRONT_ROWS))
    return pl.pallas_call(
        front_kernel,
        grid_spec=pltpu.PrefetchScalarGridSpec(
            num_scalar_prefetch=2,
            grid=(rows // FRONT_ROWS,),
            in_specs=[
                pl.BlockSpec((FRONT_ROWS, width), lambda i, s, p: (last(i, s, p), 0)),
                whole((1, width)),
                whole((width, width)),
                whole((width, width)),
                whole((head_size, slices)),
                whole((1, head_size)),
            ],
            out_specs=[
                pl.BlockSpec((heads * slices, FRONT_ROWS), lambda i, s, p: (0, last(i, s, p))),
                whole((sums_rows, slices)),
                whole((sums_rows, slices)),
            ],
            scratch_shapes=[
                pltpu.VMEM((width, width), bf16),
                pltpu.VMEM((width, width), bf16),
                pltpu.VMEM((slices, head_size), bf16),
                pltpu.VMEM((3 * heads, width), bf16),
                pltpu.VMEM((width, FRONT_ROWS), bf16),
                pltpu.VMEM((width, FRONT_ROWS), bf16),
                pltpu.VMEM((heads * slices, 128), f32),
                pltpu.VMEM((2, sums_rows, slices), f32),
            ],
        ),
        out_shape=[
            jax.ShapeDtypeStruct((heads * slices, rows), bf16),
            jax.ShapeDtypeStruct((sums_rows, slices), f32),
            jax.ShapeDtypeStruct((sums_rows, slices), f32),
        ],
        compiler_params=pltpu.CompilerParams(vmem_limit_bytes=60 * MIB),
        name="front",
    )(
        sizes,
        place,
        points,
        gain[None, :],
        fx_weight,
        x_weight,
        slice_weight,
        temp_vector[None, :],
    )


def mix_call(first, second, q_weight, k_weight, v_weight):
    head_size = q_weight.shape[0]
    slices = first.shape[1]
    half = first.shape[0] // (head_size + 1)
    return pl.pallas_call(
        mix_kernel,
        out_shape=jax.ShapeDtypeStruct((half * head_size, slices), bf16),
        scratch_shapes=[
            pltpu.VMEM((slices, half * 128), bf16),
            pltpu.VMEM((half, 128, slices), bf16),
            pltpu.VMEM((half, slices, slices), f32),
            pltpu.VMEM((half, slices, slices), bf16),
        ],
        compiler_params=pltpu.CompilerParams(vmem_limit_bytes=60 * MIB),
        name="mix",
    )(first, second, q_weight, k_weight, v_weight)


def back_call(sizes, place, stored, points, mine, theirs, out_weight, gain, up, down, sent):
    rows, width = points.shape
    tall = stored.shape[0]
    piece = up.shape[1] // 2
    pieces = 2 + (len(sent) if piece == width else len(sent) // 2)
    last = lambda i, s, p: jnp.minimum(i, lax.div(s[p[0]] - 1, BACK_ROWS))
    return pl.pallas_call(
        back_kernel,
        grid_spec=pltpu.PrefetchScalarGridSpec(
            num_scalar_prefetch=2,
            grid=(rows // BACK_ROWS,),
            in_specs=[
                pl.BlockSpec((tall, BACK_ROWS), lambda i, s, p: (0, last(i, s, p))),
                pl.BlockSpec((BACK_ROWS, width), lambda i, s, p: (last(i, s, p), 0)),
                whole(mine.shape),
                whole(mine.shape),
                whole((width, width)),
                whole((1, width)),
            ]
            + [pl.BlockSpec(memory_space=pl.ANY)] * (2 + len(sent)),
            out_specs=pl.BlockSpec((BACK_ROWS, width), lambda i, s, p: (i, 0)),
            scratch_shapes=[
                pltpu.VMEM((width, mine.shape[1]), bf16),
                pltpu.VMEM((width, BACK_ROWS), f32),
                pltpu.VMEM((pieces, width, piece), bf16),
                pltpu.VMEM((pieces, piece, width), bf16),
                pltpu.SemaphoreType.DMA((2 * pieces,)),
            ],
        ),
        out_shape=jax.ShapeDtypeStruct((rows, width), bf16),
        compiler_params=pltpu.CompilerParams(vmem_limit_bytes=60 * MIB),
        name="back",
    )(sizes, place, stored, points, mine, theirs, out_weight, gain[None, :], up, down, *sent)


def per_device(
    mesh_shape,
    points,
    part_sizes,
    norm1_gain,
    fx_weight,
    x_weight,
    slice_weight,
    temp_vector,
    q_weight,
    k_weight,
    v_weight,
    out_weight,
    norm2_gain,
    up_weight,
    down_weight,
):
    axes = ("pts", "ffn", "sub")
    devices = math.prod(mesh_shape[a] for a in axes)
    shards = mesh_shape["ffn"]
    place = lax.axis_index(axes).astype(jnp.int32).reshape(1)

    piece = up_weight.shape[1] // 2
    core = lax.axis_index("sub")
    halves = (
        lax.dynamic_slice_in_dim(up_weight, core * piece, piece, 1),
        lax.dynamic_slice_in_dim(down_weight, core * piece, piece, 0),
    )
    if piece == up_weight.shape[0]:
        halves = (jnp.concatenate(halves, 0),)
    far_pieces = [
        lax.ppermute(half, "ffn", [(i, (i + turn) % shards) for i in range(shards)])
        for turn in range(1, shards)
        for half in halves
    ]
    stored, keep, send = front_call(
        part_sizes, place, points, norm1_gain, fx_weight, x_weight, slice_weight, temp_vector
    )
    received = lax.ppermute(send, "sub", [(0, 1), (1, 0)])
    bits = [2 << b for b in range((devices // 2).bit_length() - 1)]
    sums = keep
    hops = None
    for even, odd in zip(bits, bits[1:] + bits[:1]):
        sums = sums + received
        if even == bits[2]:
            ready = lax.optimization_barrier((tuple(far_pieces), sums))[0]
            hops = [lax.ppermute(piece, "sub", [(0, 1), (1, 0)]) for piece in ready]
        received = lax.ppermute(
            sums, axes, [(i, i ^ (odd if i & 1 else even)) for i in range(devices)]
        )
    mine = mix_call(sums, received, q_weight, k_weight, v_weight)
    theirs = lax.ppermute(mine, "sub", [(0, 1), (1, 0)])
    return back_call(
        part_sizes,
        place,
        stored,
        points,
        mine,
        theirs,
        out_weight,
        norm2_gain,
        up_weight,
        down_weight,
        far_pieces + hops,
    )


def solution(mesh):
    return jax.shard_map(
        functools.partial(per_device, dict(mesh.shape)),
        mesh=mesh,
        in_specs=(
            P(("groups", "pts", "ffn", "sub"), None),
            P("groups"),
            P(),
            P(),
            P(),
            P(),
            P(),
            P(),
            P(),
            P(),
            P(),
            P(),
            P(None, "ffn"),
            P("ffn", None),
        ),
        out_specs=P(("groups", "pts", "ffn", "sub"), None),
        check_vma=False,
    )
```

time: 282 us -> 69.2 us (0.25)
  blocking collectives: 89 us -> 0 us
  waiting for transfers between devices: 85.6 us -> 20.2 us
  matrix products: 37.8 us -> 0 us
  Pallas kernels: 12.7 us -> 32.7 us
  local copies, waits for them, and re-layouts: 20.9 us -> 2.97 us
  between operations: 16 us -> 0.07 us
  other arithmetic: 11.7 us -> 1.13 us
  starting transfers between devices: 7.44 us -> 12.2 us
    psum x1 -> x0, waiting for transfers between devices: 68.1 us -> none  [per_device(): lax.psum((token_sums, weight_sums), ('pts', 'ffn', 'sub'))]
    psum x1 -> x0, blocking collectives: 58.8 us -> none  [per_device(): lax.psum((token_sums, weight_sums), ('pts', 'ffn', 'sub'))]
    pallas_call x0 -> x3, Pallas kernels: none -> 32.7 us  [the longest x1 16.6 us: front_call(): pl.pallas_call(front_kernel, grid_spec=pltpu.PrefetchScalarGridSpec(num_s...]
    all_to_all x1 -> x0, blocking collectives: 30.2 us -> none  [per_device(): lax.all_to_all(unpacked.reshape(layer_depth, devices, width), ('pts', 'ff...]
    dot_general x20 -> x0, matrix products: 28.6 us -> none  [the longest x1 13.2 us: per_device(): update = jnp.dot(hidden, down_full, preferred_element_type=jnp.float32)]
    ppermute x0 -> x7, waiting for transfers between devices: none -> 20.2 us  [the longest x3 17.3 us: per_device(): lax.ppermute(sums, axes, [(i, i ^ (odd if i & 1 else even)) for i in rang...]
    all_to_all x1 -> x0, waiting for transfers between devices: 16.4 us -> none  [per_device(): lax.all_to_all(points.reshape(layer_depth, devices, width), ('pts', 'ffn'...]
    unnamed x1 -> x0, Pallas kernels: 12.7 us -> none
  transfers between devices with their start and end apart: 4 -> 7, of which waited for: 2 -> 5; matrix products, arithmetic and copies ran while one was open for 7% -> 2% of each run, Pallas kernels for 5% -> 28%
where the time goes in v2:
time: 69.2 us; the launch traced here: 69.3 us
  Pallas kernels  32.7 us (47%)
  waiting for transfers between devices  20.2 us (29%)
  starting transfers between devices  12.2 us (18%)
  local copies, waits for them, and re-layouts  2.97 us (4%)
  other arithmetic  1.13 us (2%)
    ppermute x3, waiting for transfers between devices, per_device(): lax.ppermute(sums, axes, [(i, i ^ (odd if i & 1 else even)) for i in rang...  17.3 us
    pallas_call x1, Pallas kernels, front_call(): pl.pallas_call(front_kernel, grid_spec=pltpu.PrefetchScalarGridSpec(num_s...  16.6 us
    pallas_call x1, Pallas kernels, back_call(): pl.pallas_call(back_kernel, grid_spec=pltpu.PrefetchScalarGridSpec(num_sc...  13.1 us
    ppermute x1, starting transfers between devices, per_device(): theirs = lax.ppermute(mine, 'sub', [(0, 1), (1, 0)])  4.73 us
    ppermute x3, starting transfers between devices, per_device(): lax.ppermute(sums, axes, [(i, i ^ (odd if i & 1 else even)) for i in rang...  3.55 us
    pallas_call x1, Pallas kernels, mix_call(): pl.pallas_call(mix_kernel, out_shape=jax.ShapeDtypeStruct((half * head_si...  2.99 us
    ppermute x1, starting transfers between devices, per_device(): lax.ppermute(half, 'ffn', [(i, (i + turn) % shards) for i in range(shards)])  2.11 us
    ppermute x1, starting transfers between devices, per_device(): hops = [lax.ppermute(piece, 'sub', [(0, 1), (1, 0)]) for piece in ready]  1.85 us
  transfers between devices with their start and end apart: 7, of which 5 were waited for; matrix products, arithmetic and copies ran while one was open for 2% of the time, Pallas kernels for 28%

profile of v2, /device:TPU:1, one launch (start us, length us, event | category | flops | bytes accessed | tf_op | source)
XLA Modules:
  0.0 69.3 jit_solution(273997128176949726)
XLA Ops:
  0.0 1.3 %constant_dynamic-slice_fusion = (bf16[512,512]{1,0:T(8,128)(2,1)S(1)}, bf16[512,512]{1,0:T(8,128)(2,1)S(1)}) fusion(bf16[1024,512]{1,0:T(8,128)(2,1)} %down.1, s32[]{:T(128)S(6)} %select_n.4, bf16[512,1024]{1,0:T(8,128)(2,1)} %up.1), kind=kLoop, calls=%fused_computation.1 | loop fusion | bytes 2097156 | tf_op jit(solution)/shard_map/dynamic_slice | solution.py:384
  1.3 0.1 pad_maximum_fusion
  1.3 2.1 %collective-permute-start.5 = (bf16[1024,512]{1,0:T(8,128)(2,1)S(1)}, bf16[1024,512]{1,0:T(8,128)(2,1)S(1)}, u32[]{:S(2)}, u32[]{:S(2)}) collective-permute-start(bf16[1024,512]{1,0:T(8,128)(2,1)S(1)} %pad_maximum_fusion), channel_id=1, source_target_pairs={{0,2},{2,0},{1,3},{3,1},{4,6},{6,4},{5,7},{7,5},{8,10},{10,8},{9,1... | collective-permute-start | bytes 3145736 | tf_op jit(solution)/shard_map/ppermute | solution.py:389
  3.5 16.6 %front.1 = (bf16[4096,1024]{1,0:T(8,128)(2,1)}, f32[264,256]{1,0:T(8,128)}, f32[264,256]{1,0:T(8,128)}) custom-call(s32[16]{0:T(128)} %sizes.3, s32[1]{0:T(128)} %bitcast.place, bf16[1024,512]{1,0:T(8,128)(2,1)} %points.3, f32[1,512]{1,0:T(1,128)} %bitcast.4, bf16[512,512]{1,0:T(8,128)(2,1)} %fx_weight.1, bf16[512,512]{1,0:T(8,128)(2,1)} %x_weight.1, ...), custom_call_target="tpu_custom_call" | custom-call | tf_op jit(solution)/shard_map/front/pallas_call | solution.py:257
  20.0 0.0 collective-permute-start
  20.1 1.8 %collective-permute-done = f32[264,256]{1,0:T(8,128)S(1)} collective-permute-done((f32[264,256]{1,0:T(8,128)}, f32[264,256]{1,0:T(8,128)S(1)}, u32[]{:S(2)}, u32[]{:S(2)}) %collective-permute-start) | collective-permute-done | bytes 270368 | tf_op jit(solution)/shard_map/ppermute | solution.py:396
  21.8 1.0 %add.21 = f32[264,256]{1,0:T(8,128)S(1)} add(f32[264,256]{1,0:T(8,128)} %get-tuple-element.10, f32[264,256]{1,0:T(8,128)S(1)} %collective-permute-done) | non-fusion elementwise | flops 67584 | bytes 811008 | tf_op jit(solution)/shard_map/add | solution.py:401
  22.8 0.1 collective-permute-start.1
  22.9 5.6 %collective-permute-done.1 = f32[264,256]{1,0:T(8,128)S(1)} collective-permute-done((f32[264,256]{1,0:T(8,128)S(1)}, f32[264,256]{1,0:T(8,128)S(1)}, u32[]{:S(2)}, u32[]{:S(2)}) %collective-permute-start.1) | collective-permute-done | bytes 270368 | tf_op jit(solution)/shard_map/ppermute | solution.py:405
  28.5 3.0 %collective-permute-start.2 = (f32[264,256]{1,0:T(8,128)S(1)}, f32[264,256]{1,0:T(8,128)S(1)}, u32[]{:S(2)}, u32[]{:S(2)}) collective-permute-start(f32[264,256]{1,0:T(8,128)S(1)} %add.22), channel_id=1, source_target_pairs={{0,4},{1,9},{2,6},{3,11},{4,0},{5,13},{6,2},{7,15},{8,12},{9,1},{1... | collective-permute-start | bytes 811016 | tf_op jit(solution)/shard_map/ppermute | solution.py:405
  31.5 6.6 %collective-permute-done.2 = f32[264,256]{1,0:T(8,128)S(1)} collective-permute-done((f32[264,256]{1,0:T(8,128)S(1)}, f32[264,256]{1,0:T(8,128)S(1)}, u32[]{:S(2)}, u32[]{:S(2)}) %collective-permute-start.2) | collective-permute-done | bytes 270368 | tf_op jit(solution)/shard_map/ppermute | solution.py:405
  38.1 0.0 copy-start
  38.1 0.0 collective-permute-done.5.refs_0_
  38.1 0.0 copy-start.1
  38.1 1.9 %collective-permute-start.6 = (bf16[1024,512]{1,0:T(8,128)(2,1)S(1)}, bf16[1024,512]{1,0:T(8,128)(2,1)S(1)}, u32[]{:S(2)}, u32[]{:S(2)}) collective-permute-start(bf16[1024,512]{1,0:T(8,128)(2,1)S(1)} %collective-permute-done.5.refs_0_), channel_id=1, source_target_pairs={{0,1},{1,0},{2,3},{3,2},{4,5},{5,4},{6,7},{7,6},{8,9},{9,8},{10,11... | collective-permute-start | bytes 3145736 | tf_op jit(solution)/shard_map/ppermute | solution.py:404
  40.0 0.5 collective-permute-start.3
  40.5 5.1 %collective-permute-done.3.second = f32[264,256]{1,0:T(8,128)S(1)} collective-permute-done((f32[264,256]{1,0:T(8,128)S(1)}, f32[264,256]{1,0:T(8,128)S(1)}, u32[]{:S(2)}, u32[]{:S(2)}) %collective-permute-start.3) | collective-permute-done | bytes 270368 | tf_op jit(solution)/shard_map/ppermute | solution.py:405
  45.6 0.0 copy-done
  45.6 0.0 copy-start.3
  45.6 0.7 %copy-done.3 = f32[264,256]{1,0:T(8,128)} copy-done((f32[264,256]{1,0:T(8,128)}, f32[264,256]{1,0:T(8,128)S(1)}, u32[]{:S(2)}) %copy-start.3) | copy-done | bytes 270360
  46.3 3.0 %mix.1.mine = bf16[256,256]{1,0:T(8,128)(2,1)} custom-call(f32[264,256]{1,0:T(8,128)} %copy-done, f32[264,256]{1,0:T(8,128)} %copy-done.3, bf16[32,32]{1,0:T(8,128)(2,1)} %q_weight.1, bf16[32,32]{1,0:T(8,128)(2,1)} %k_weight.1, bf16[32,32]{1,0:T(8,128)(2,1)} %v_weight.1), custom_call_target="tpu_custom_call" | custom-call | tf_op jit(solution)/shard_map/mix/pallas_call | solution.py:309
  49.3 4.7 %collective-permute-start.4 = (bf16[256,256]{1,0:T(8,128)(2,1)}, bf16[256,256]{1,0:T(8,128)(2,1)S(1)}, u32[]{:S(2)}, u32[]{:S(2)}) collective-permute-start(bf16[256,256]{1,0:T(8,128)(2,1)} %mix.1.mine), channel_id=1, source_target_pairs={{0,1},{1,0},{2,3},{3,2},{4,5},{5,4},{6,7},{7,6},{8,9},{9,8},{10,11... | collective-permute-start | bytes 393224 | tf_op jit(solution)/shard_map/ppermute | solution.py:409
  54.0 1.2 %collective-permute-done.4.theirs = bf16[256,256]{1,0:T(8,128)(2,1)S(1)} collective-permute-done((bf16[256,256]{1,0:T(8,128)(2,1)}, bf16[256,256]{1,0:T(8,128)(2,1)S(1)}, u32[]{:S(2)}, u32[]{:S(2)}) %collective-permute-start.4) | collective-permute-done | bytes 131104 | tf_op jit(solution)/shard_map/ppermute | solution.py:409
  55.2 0.0 copy-start.4
  55.2 0.0 collective-permute-done.6.refs_1_
  55.2 0.0 copy-start.2
  55.2 0.0 copy-done.1
  55.2 0.6 copy-done.4
  55.8 0.3 copy-done.2
  56.2 13.1 %back.1 = bf16[1024,512]{1,0:T(8,128)(2,1)} custom-call(s32[16]{0:T(128)} %sizes.3, s32[1]{0:T(128)} %bitcast.place, bf16[4096,1024]{1,0:T(8,128)(2,1)} %get-tuple-element.9.stored, bf16[1024,512]{1,0:T(8,128)(2,1)} %points.3, bf16[256,256]{1,0:T(8,128)(2,1)} %mix.1.mine, bf16[256,256]{1,0:T(8,128)(2,1)} %copy-done.4, bf16[512,512]{1,0:T(8,128)(2,1)} %out_weight.1, ...), custom_call_target="tpu_custom_call" | custom-call | tf_op jit(solution)/shard_map/back/pallas_call | solution.py:329
  (2 shorter events, 0.1 us)
Async XLA Ops:
  1.3 36.7 %collective-permute-start.5 = (bf16[1024,512]{1,0:T(8,128)(2,1)S(1)}, bf16[1024,512]{1,0:T(8,128)(2,1)S(1)}, u32[]{:S(2)}, u32[]{:S(2)}) collective-permute-start(bf16[1024,512]{1,0:T(8,128)(2,1)S(1)} %pad_maximum_fusion), channel_id=1, source_target_pairs={{0,2},{2,0},{1,3},{3,1},{4,6},{6,4},{5,7},{7,5},{8,10},{10,8},{9,1... | collective-permute-start | bytes 3145736 | tf_op jit(solution)/shard_map/ppermute | solution.py:389
  20.0 1.8 %collective-permute-start = (f32[264,256]{1,0:T(8,128)}, f32[264,256]{1,0:T(8,128)S(1)}, u32[]{:S(2)}, u32[]{:S(2)}) collective-permute-start(f32[264,256]{1,0:T(8,128)} %get-tuple-element.11), channel_id=1, source_target_pairs={{0,1},{1,0},{2,3},{3,2},{4,5},{5,4},{6,7},{7,6},{8,9},{9,8},{10,11... | collective-permute-start | bytes 811016 | tf_op jit(solution)/shard_map/ppermute | solution.py:396
  22.8 5.7 %collective-permute-start.1 = (f32[264,256]{1,0:T(8,128)S(1)}, f32[264,256]{1,0:T(8,128)S(1)}, u32[]{:S(2)}, u32[]{:S(2)}) collective-permute-start(f32[264,256]{1,0:T(8,128)S(1)} %add.21), channel_id=1, source_target_pairs={{0,2},{1,5},{2,0},{3,7},{4,6},{5,1},{6,4},{7,3},{8,10},{9,13},{10,... | collective-permute-start | bytes 811016 | tf_op jit(solution)/shard_map/ppermute | solution.py:405
  28.5 9.5 %collective-permute-start.2 = (f32[264,256]{1,0:T(8,128)S(1)}, f32[264,256]{1,0:T(8,128)S(1)}, u32[]{:S(2)}, u32[]{:S(2)}) collective-permute-start(f32[264,256]{1,0:T(8,128)S(1)} %add.22), channel_id=1, source_target_pairs={{0,4},{1,9},{2,6},{3,11},{4,0},{5,13},{6,2},{7,15},{8,12},{9,1},{1... | collective-permute-start | bytes 811016 | tf_op jit(solution)/shard_map/ppermute | solution.py:405
  38.1 7.5 %copy-start = (f32[264,256]{1,0:T(8,128)}, f32[264,256]{1,0:T(8,128)S(1)}, u32[]{:S(2)}) copy-start(f32[264,256]{1,0:T(8,128)S(1)} %add.23.first) | copy-start | bytes 811012
  38.1 17.1 %copy-start.1 = (bf16[1024,512]{1,0:T(8,128)(2,1)}, bf16[1024,512]{1,0:T(8,128)(2,1)S(1)}, u32[]{:S(2)}) copy-start(bf16[1024,512]{1,0:T(8,128)(2,1)S(1)} %collective-permute-done.5.refs_0_) | copy-start | bytes 3145732
  38.1 17.1 %collective-permute-start.6 = (bf16[1024,512]{1,0:T(8,128)(2,1)S(1)}, bf16[1024,512]{1,0:T(8,128)(2,1)S(1)}, u32[]{:S(2)}, u32[]{:S(2)}) collective-permute-start(bf16[1024,512]{1,0:T(8,128)(2,1)S(1)} %collective-permute-done.5.refs_0_), channel_id=1, source_target_pairs={{0,1},{1,0},{2,3},{3,2},{4,5},{5,4},{6,7},{7,6},{8,9},{9,8},{10,11... | collective-permute-start | bytes 3145736 | tf_op jit(solution)/shard_map/ppermute | solution.py:404
  40.0 5.6 %collective-permute-start.3 = (f32[264,256]{1,0:T(8,128)S(1)}, f32[264,256]{1,0:T(8,128)S(1)}, u32[]{:S(2)}, u32[]{:S(2)}) collective-permute-start(f32[264,256]{1,0:T(8,128)S(1)} %add.23.first), channel_id=1, source_target_pairs={{0,8},{1,3},{2,10},{3,1},{4,12},{5,7},{6,14},{7,5},{8,0},{9,11},{1... | collective-permute-start | bytes 811016 | tf_op jit(solution)/shard_map/ppermute | solution.py:405
  45.6 0.7 %copy-start.3 = (f32[264,256]{1,0:T(8,128)}, f32[264,256]{1,0:T(8,128)S(1)}, u32[]{:S(2)}) copy-start(f32[264,256]{1,0:T(8,128)S(1)} %collective-permute-done.3.second) | copy-start | bytes 811012
  49.3 5.9 %collective-permute-start.4 = (bf16[256,256]{1,0:T(8,128)(2,1)}, bf16[256,256]{1,0:T(8,128)(2,1)S(1)}, u32[]{:S(2)}, u32[]{:S(2)}) collective-permute-start(bf16[256,256]{1,0:T(8,128)(2,1)} %mix.1.mine), channel_id=1, source_target_pairs={{0,1},{1,0},{2,3},{3,2},{4,5},{5,4},{6,7},{7,6},{8,9},{9,8},{10,11... | collective-permute-start | bytes 393224 | tf_op jit(solution)/shard_map/ppermute | solution.py:409
  55.2 0.6 copy-start.4
  55.2 1.0 %copy-start.2 = (bf16[1024,512]{1,0:T(8,128)(2,1)}, bf16[1024,512]{1,0:T(8,128)(2,1)S(1)}, u32[]{:S(2)}) copy-start(bf16[1024,512]{1,0:T(8,128)(2,1)S(1)} %collective-permute-done.6.refs_1_) | copy-start | bytes 3145732

commit v3 on v2

v3 whole, which is shorter than its diff:
```python
import functools
import math

import jax
import jax.numpy as jnp
from jax import lax
from jax.experimental import pallas as pl
from jax.experimental.pallas import tpu as pltpu
from jax.sharding import PartitionSpec as P

eps_norm = 1e-05
eps_mass = 1e-05
f32 = jnp.float32
bf16 = jnp.bfloat16
MIB = 1024 * 1024
FRONT_ROWS = 512
BACK_ROWS = 512


def dot(a, b):
    return jnp.dot(a, b, preferred_element_type=f32)


def dot_nt(a, b):
    return lax.dot_general(a, b, (((1,), (1,)), ((), ())), preferred_element_type=f32)


def split3(x):
    first = x.astype(bf16)
    rest = x - first.astype(f32)
    second = rest.astype(bf16)
    third = (rest - second.astype(f32)).astype(bf16)
    return first, second, third


def layer_norm(wide, gain):
    centered = wide - jnp.mean(wide, axis=-1, keepdims=True)
    variance = jnp.mean(centered * centered, axis=-1, keepdims=True)
    return (centered * lax.rsqrt(variance + eps_norm) * gain).astype(bf16)


def gelu(x):
    halved = 0.5 * x
    return halved + halved * lax.erf(x * math.sqrt(0.5))


def head_tile(weight, copies):
    size = weight.shape[0]
    wide = jnp.concatenate([weight] * copies, 1)
    tall = jnp.concatenate([wide] * copies, 0)
    row = lax.broadcasted_iota(jnp.int32, tall.shape, 0)
    col = lax.broadcasted_iota(jnp.int32, tall.shape, 1)
    return jnp.where(lax.div(row, size) == lax.div(col, size), tall, 0.0)


def front_kernel(
    sizes,
    place,
    gain,
    slice_weight,
    temp_vector,
    points,
    fx_weight,
    x_weight,
    stored,
    keep,
    send,
    fx_t,
    x_t,
    slice_t,
    temp_t,
    feats,
    mids,
    totals,
):
    head_size, slices = slice_weight.shape
    width = points.shape[1]
    heads = width // head_size
    half = heads // 2
    span = half * head_size
    live = sizes[place[0]]
    core = place[0] % 2
    totals[...] = jnp.zeros_like(totals)
    slice_t[...] = slice_weight[...].astype(f32).T.astype(bf16)
    wide = jnp.concatenate([temp_vector[...]] * heads, 1)
    row = lax.broadcasted_iota(jnp.int32, (heads, width), 0)
    col = lax.broadcasted_iota(jnp.int32, (heads, width), 1)
    block = jnp.where(lax.div(col, head_size) == row, jnp.broadcast_to(wide, (heads, width)), 0.0)
    for i, part in enumerate(split3(block)):
        temp_t[i * heads : (i + 1) * heads, :] = part
    x_t[...] = x_weight[...].astype(f32).T.astype(bf16)
    fx_t[...] = fx_weight[...].astype(f32).T.astype(bf16)

    def own(h):
        return slice(h * head_size, (h + 1) * head_size)

    def step(i, carry):
        here = points[pl.ds(pl.multiple_of(i * FRONT_ROWS, FRONT_ROWS), FRONT_ROWS), :]
        normed = layer_norm(here.astype(f32), gain[...])
        mids[...] = dot_nt(x_t[...], normed).astype(bf16)
        feats[...] = dot_nt(fx_t[...], normed).astype(bf16)
        t = dot(temp_t[...], mids[...])
        t = t[:heads] + t[heads : 2 * heads] + t[2 * heads : 3 * heads]
        temps = 0.5 + jnp.maximum(t, 0.0) + jnp.log(1.0 + jnp.exp(-jnp.abs(t)))
        scales = math.log2(math.e) / temps
        col = lax.broadcasted_iota(jnp.int32, (1, FRONT_ROWS), 1) + i * FRONT_ROWS
        valid = jnp.where(col < live, 1.0, 0.0)
        for q in range(0, heads, 2):
            group = range(q, q + 2)
            logits = [dot(slice_t[...], mids[own(h), :]) for h in group]
            tops = [jnp.max(l, axis=0, keepdims=True) for l in logits]
            raised = [
                jnp.exp2((l - top) * scales[h : h + 1, :]) for h, l, top in zip(group, logits, tops)
            ]
            shares = [valid * pltpu.reciprocal(jnp.sum(r, axis=0, keepdims=True), approx=True) for r in raised]
            for h, r, share in zip(group, raised, shares):
                rows = slice(h * slices, (h + 1) * slices)
                weights = r * share
                stored[i, rows, :] = weights.astype(bf16)
                mass = weights[:, :128]
                for c in range(1, FRONT_ROWS // 128):
                    mass = mass + weights[:, c * 128 : (c + 1) * 128]
                mass_row = jnp.sum(mass.T, axis=0, keepdims=True)
                totals[h // half, span + h % half : span + h % half + 1, :] += mass_row
        for h in range(heads):
            side, at = h // half, h % half
            totals[side, own(at), :] += dot_nt(
                feats[own(h), :], stored[i, h * slices : (h + 1) * slices, :]
            )
        return carry

    lax.fori_loop(0, lax.div(live + FRONT_ROWS - 1, FRONT_ROWS), step, 0)
    keep[...] = totals[core]
    send[...] = totals[1 - core]


def back_kernel(
    sizes, place, stored, mine, theirs, q_weight, k_weight, v_weight, gain, points, out_weight, up, down, *refs
):
    extra = len(refs) - 11
    sent = refs[:extra]
    (
        mixed,
        finished,
        spread,
        desliced,
        crossed,
        value_t,
        repeat,
        tokens,
        queries,
        scores,
        arrived,
    ) = refs[extra:]
    head_size = q_weight.shape[0]
    slices = mine.shape[1]
    half = mine.shape[0] // (head_size + 1)
    span = half * head_size
    heads = 2 * half
    rows, width = points.shape
    piece = up.shape[1] // 2
    live = sizes[place[0]]
    low = place[0] % 2 == 0
    blocks = rows // BACK_ROWS
    def leave(i):
        here = pl.ds(pl.multiple_of(i * BACK_ROWS, BACK_ROWS), BACK_ROWS)
        return pltpu.make_async_copy(finished.at[i], mixed.at[here, :], arrived.at[i])

    def own(h):
        return slice(h * head_size, (h + 1) * head_size)

    tiled = head_tile(dot_nt(k_weight[...], q_weight[...]), half)
    for i, part in enumerate(split3(tiled)):
        crossed[i] = part
    value_t[...] = head_tile(v_weight[...].astype(f32), half).T.astype(bf16)
    row = lax.broadcasted_iota(jnp.int32, (span, half * 128), 0)
    col = lax.broadcasted_iota(jnp.int32, (span, half * 128), 1)
    same = (lax.div(row, head_size) == lax.div(col, 128)) & (
        lax.rem(row, head_size) == lax.rem(col, head_size)
    )
    repeat[...] = jnp.where(same, 1.0, 0.0).astype(bf16)
    queries[...] = jnp.zeros_like(queries)
    for side in range(2):
        sums = jnp.where(low, mine[...], theirs[...]) if side == 0 else jnp.where(low, theirs[...], mine[...])
        parts = []
        for h in range(half):
            mass = sums[span + h : span + h + 1, :] + eps_mass
            parts.append(sums[own(h), :] / mass)
        wide = jnp.concatenate(parts, 0)
        narrow = wide.astype(bf16)
        asked = dot(crossed[0], narrow) + dot(crossed[1], narrow) + dot(crossed[2], narrow)
        for i, part in enumerate(split3(asked * (math.log2(math.e) / math.sqrt(head_size)))):
            for h in range(half):
                queries[side * half + h, own(i), :] = part[own(h), :]
        values = dot(value_t[...], narrow).astype(bf16)
        tokens[...] = dot(narrow.astype(f32).T.astype(bf16), repeat[...]).astype(bf16)
        for h in range(half):
            scores[h] = dot(tokens[:, h * 128 : (h + 1) * 128], queries[side * half + h])
        for h in range(half):
            top = jnp.max(scores[h], axis=0, keepdims=True)
            raised = jnp.exp2(scores[h] - top)
            total = jnp.sum(raised, axis=0, keepdims=True)
            probs = (raised * pltpu.reciprocal(total, approx=True)).astype(bf16)
            spread[own(side * half + h), :] = dot(values[own(h), :], probs).astype(bf16)

    pieces = [
        (up[:, c * piece : (c + 1) * piece], down[c * piece : (c + 1) * piece, :]) for c in range(2)
    ]
    if piece == width:
        pieces += [(r[:width, :], r[width:, :]) for r in sent]
    else:
        pieces += [(sent[2 * i][...], sent[2 * i + 1][...]) for i in range(extra // 2)]

    def step(i, carry):
        per = BACK_ROWS // FRONT_ROWS
        for p in range(per):
            lanes = slice(p * FRONT_ROWS, (p + 1) * FRONT_ROWS)
            for h in range(heads):
                desliced[own(h), lanes] = dot(
                    spread[own(h), :], stored[i * per + p, h * slices : (h + 1) * slices, :]
                )
        picked = desliced[...].T.astype(bf16)
        here = points[pl.ds(pl.multiple_of(i * BACK_ROWS, BACK_ROWS), BACK_ROWS), :]
        residual = here.astype(f32) + dot(picked, out_weight[...])
        late = layer_norm(residual, gain[...])
        total = residual
        raw = dot(late, pieces[0][0])
        for n in range(len(pieces)):
            now = raw
            if n + 1 < len(pieces):
                raw = dot(late, pieces[n + 1][0])
            total = total + dot(gelu(now).astype(bf16), pieces[n][1])
        row = lax.broadcasted_iota(jnp.int32, (BACK_ROWS, 1), 0) + i * BACK_ROWS
        finished[i] = jnp.where(row < live, total, 0.0).astype(bf16)
        leave(i).start()
        return carry

    busy = lax.div(live + BACK_ROWS - 1, BACK_ROWS)
    lax.fori_loop(0, busy, step, 0)
    for i in range(blocks):

        @pl.when(i >= busy)
        def _():
            finished[i] = jnp.zeros_like(finished[i])
            leave(i).start()

    for i in range(blocks):
        leave(i).wait()


SMEM = pl.BlockSpec(memory_space=pltpu.SMEM)
VMEM = pl.BlockSpec(memory_space=pltpu.VMEM)
HBM = pl.BlockSpec(memory_space=pltpu.HBM)


def front_call(sizes, place, points, gain, fx_weight, x_weight, slice_weight, temp_vector):
    rows, width = points.shape
    head_size, slices = slice_weight.shape
    heads = width // head_size
    sums_rows = heads // 2 * (head_size + 1)
    return pl.pallas_call(
        front_kernel,
        in_specs=[SMEM, SMEM] + [VMEM] * 6,
        out_specs=[VMEM, VMEM, VMEM],
        out_shape=[
            jax.ShapeDtypeStruct((rows // FRONT_ROWS, heads * slices, FRONT_ROWS), bf16),
            jax.ShapeDtypeStruct((sums_rows, slices), f32),
            jax.ShapeDtypeStruct((sums_rows, slices), f32),
        ],
        scratch_shapes=[
            pltpu.VMEM((width, width), bf16),
            pltpu.VMEM((width, width), bf16),
            pltpu.VMEM((slices, head_size), bf16),
            pltpu.VMEM((3 * heads, width), bf16),
            pltpu.VMEM((width, FRONT_ROWS), bf16),
            pltpu.VMEM((width, FRONT_ROWS), bf16),
            pltpu.VMEM((2, sums_rows, slices), f32),
        ],
        compiler_params=pltpu.CompilerParams(vmem_limit_bytes=32 * MIB),
        name="front",
    )(
        sizes,
        place,
        gain[None, :],
        slice_weight,
        temp_vector[None, :],
        points,
        fx_weight,
        x_weight,
    )


def back_call(
    sizes, place, stored, mine, theirs, q_weight, k_weight, v_weight, gain, points, out_weight, up, down, sent
):
    rows, width = points.shape
    head_size = q_weight.shape[0]
    slices = mine.shape[1]
    half = mine.shape[0] // (head_size + 1)
    span = half * head_size
    blocks = rows // BACK_ROWS
    return pl.pallas_call(
        back_kernel,
        in_specs=[SMEM, SMEM] + [VMEM] * (11 + len(sent)),
        out_specs=HBM,
        out_shape=jax.ShapeDtypeStruct((rows, width), bf16),
        scratch_shapes=[
            pltpu.VMEM((blocks, BACK_ROWS, width), bf16),
            pltpu.VMEM((2 * span, slices), bf16),
            pltpu.VMEM((width, BACK_ROWS), f32),
            pltpu.VMEM((3, span, span), bf16),
            pltpu.VMEM((span, span), bf16),
            pltpu.VMEM((span, half * 128), bf16),
            pltpu.VMEM((slices, half * 128), bf16),
            pltpu.VMEM((2 * half, 128, slices), bf16),
            pltpu.VMEM((half, slices, slices), f32),
            pltpu.SemaphoreType.DMA((blocks,)),
        ],
        compiler_params=pltpu.CompilerParams(vmem_limit_bytes=36 * MIB),
        name="back",
    )(
        sizes,
        place,
        stored,
        mine,
        theirs,
        q_weight,
        k_weight,
        v_weight,
        gain[None, :],
        points,
        out_weight,
        up,
        down,
        *sent,
    )


def per_device(
    mesh_shape,
    points,
    part_sizes,
    norm1_gain,
    fx_weight,
    x_weight,
    slice_weight,
    temp_vector,
    q_weight,
    k_weight,
    v_weight,
    out_weight,
    norm2_gain,
    up_weight,
    down_weight,
):
    axes = ("pts", "ffn", "sub")
    devices = math.prod(mesh_shape[a] for a in axes)
    shards = mesh_shape["ffn"]
    place = lax.axis_index(axes).astype(jnp.int32).reshape(1)

    piece = up_weight.shape[1] // 2
    core = lax.axis_index("sub")
    halves = (
        lax.dynamic_slice_in_dim(up_weight, core * piece, piece, 1),
        lax.dynamic_slice_in_dim(down_weight, core * piece, piece, 0),
    )
    if piece == up_weight.shape[0]:
        halves = (jnp.concatenate(halves, 0),)
    far_pieces = [
        lax.ppermute(half, "ffn", [(i, (i + turn) % shards) for i in range(shards)])
        for turn in range(1, shards)
        for half in halves
    ]
    stored, keep, send = front_call(
        part_sizes, place, points, norm1_gain, fx_weight, x_weight, slice_weight, temp_vector
    )
    received = lax.ppermute(send, "sub", [(0, 1), (1, 0)])
    bits = [2 << b for b in range((devices // 2).bit_length() - 1)]
    zs = [b for b in bits if b >= 2 * shards]
    xs = [b for b in bits if b < 2 * shards]
    even_order, odd_order = zs[1:] + xs + zs[:1], zs + xs
    sums = keep + received
    for n, (even, odd) in enumerate(zip(even_order, odd_order)):
        if n == 2:
            ready = lax.optimization_barrier((tuple(far_pieces), sums))[0]
            hops = [lax.ppermute(piece, "sub", [(0, 1), (1, 0)]) for piece in ready]
        sums = sums + lax.ppermute(
            sums, axes, [(i, i ^ (odd if i & 1 else even)) for i in range(devices)]
        )
    theirs = lax.ppermute(sums, "sub", [(0, 1), (1, 0)])
    return back_call(
        part_sizes,
        place,
        stored,
        sums,
        theirs,
        q_weight,
        k_weight,
        v_weight,
        norm2_gain,
        points,
        out_weight,
        up_weight,
        down_weight,
        far_pieces + hops,
    )


def solution(mesh):
    return jax.shard_map(
        functools.partial(per_device, dict(mesh.shape)),
        mesh=mesh,
        in_specs=(
            P(("groups", "pts", "ffn", "sub"), None),
            P("groups"),
            P(),
            P(),
            P(),
            P(),
            P(),
            P(),
            P(),
            P(),
            P(),
            P(),
            P(None, "ffn"),
            P("ffn", None),
        ),
        out_specs=P(("groups", "pts", "ffn", "sub"), None),
        check_vma=False,
    )
```

time: 69.2 us -> 54.7 us (0.79)
  the two profiles are of different devices: /device:TPU:1 before, /device:TPU:0 now
where the time goes in v3:
time: 54.7 us; the launch traced here: 54.4 us
  waiting for transfers between devices  23.3 us (43%)
  Pallas kernels  22 us (40%)
  starting transfers between devices  6.17 us (11%)
  local copies, waits for them, and re-layouts  1.49 us (3%)
  other arithmetic  1.18 us (2%)
    ppermute x3, waiting for transfers between devices, per_device(): lax.ppermute(sums, axes, [(i, i ^ (odd if i & 1 else even)) for i in rang...  20.2 us
    pallas_call x1, Pallas kernels, back_call(): pl.pallas_call(back_kernel, in_specs=[SMEM, SMEM] + [VMEM] * (11 + len(se...  11.4 us
    pallas_call x1, Pallas kernels, front_call(): pl.pallas_call(front_kernel, in_specs=[SMEM, SMEM] + [VMEM] * 6, out_spec...  10.7 us
    ppermute x3, starting transfers between devices, per_device(): lax.ppermute(sums, axes, [(i, i ^ (odd if i & 1 else even)) for i in rang...  3 us
    ppermute x1, starting transfers between devices, per_device(): lax.ppermute(half, 'ffn', [(i, (i + turn) % shards) for i in range(shards)])  2.95 us
    ppermute x1, waiting for transfers between devices, per_device(): theirs = lax.ppermute(sums, 'sub', [(0, 1), (1, 0)])  1.53 us
    ppermute x1, waiting for transfers between devices, per_device(): received = lax.ppermute(send, 'sub', [(0, 1), (1, 0)])  1.53 us
    dynamic_slice x1, local copies, waits for them, and re-layouts, per_device(): lax.dynamic_slice_in_dim(down_weight, core * piece, piece, 0)  1.42 us
  transfers between devices with their start and end apart: 7, of which 5 were waited for; matrix products, arithmetic and copies ran while one was open for 0% of the time, Pallas kernels for 20%

profile of v3, /device:TPU:0, one launch (start us, length us, event | category | flops | bytes accessed | tf_op | source)
XLA Modules:
  0.0 54.4 jit_solution(13371390486372103248)
XLA Ops:
  0.0 0.0 copy-start.11
  0.0 0.0 copy-start.13
  0.0 1.4 %constant_dynamic-slice_fusion = (bf16[512,512]{1,0:T(8,128)(2,1)S(1)}, bf16[512,512]{1,0:T(8,128)(2,1)S(1)}) fusion(bf16[1024,512]{1,0:T(8,128)(2,1)} %down.1, s32[]{:T(128)S(6)} %select_n.4, bf16[512,1024]{1,0:T(8,128)(2,1)} %up.1), kind=kLoop, calls=%fused_computation.1 | loop fusion | bytes 2097156 | tf_op jit(solution)/shard_map/dynamic_slice | solution.py:365
  1.5 1.0 %pad_maximum_fusion = bf16[1024,512]{1,0:T(8,128)(2,1)} fusion(bf16[512,512]{1,0:T(8,128)(2,1)S(1)} %get-tuple-element.13, bf16[512,512]{1,0:T(8,128)(2,1)S(1)} %get-tuple-element.14), kind=kLoop, calls=%fused_computation | loop fusion | flops 2097152 | bytes 2097152 | tf_op jit(solution)/shard_map/concatenate | solution.py:368
  2.5 3.0 %collective-permute-start.5 = (bf16[1024,512]{1,0:T(8,128)(2,1)}, bf16[1024,512]{1,0:T(8,128)(2,1)S(1)}, u32[]{:S(2)}, u32[]{:S(2)}) collective-permute-start(bf16[1024,512]{1,0:T(8,128)(2,1)} %pad_maximum_fusion), channel_id=1, source_target_pairs={{0,2},{2,0},{1,3},{3,1},{4,6},{6,4},{5,7},{7,5},{8,10},{10,8},{9,1... | collective-permute-start | bytes 3145736 | tf_op jit(solution)/shard_map/ppermute | solution.py:370
  5.4 0.0 copy-done
  5.4 0.0 copy-done.3
  5.4 0.0 copy-done.4
  5.5 0.0 copy-done.6
  5.5 10.7 %front.1 = (bf16[2,4096,512]{2,1,0:T(8,128)(2,1)S(1)}, f32[264,256]{1,0:T(8,128)S(1)}, f32[264,256]{1,0:T(8,128)S(1)}) custom-call(s32[16]{0:T(128)S(1)} %copy-done.11, s32[1]{0:T(128)} %bitcast.place, f32[1,512]{1,0:T(1,128)S(1)} %bitcast.4, bf16[32,256]{1,0:T(8,128)(2,1)S(1)} %copy-done.6, f32[1,32]{1,0:T(1,128)S(1)} %bitcast.6, ...), custom_call_target="tpu_custom_call" | custom-call | tf_op jit(solution)/shard_map/front/pallas_call | solution.py:261
  16.2 0.0 copy-start.1
  16.2 0.0 copy-start.2
  16.2 0.0 copy-start.5
  16.2 0.0 copy-start.7
  16.2 0.0 copy-start.8
  16.2 0.0 copy-start.9
  16.2 0.0 copy-start.12
  16.2 0.1 collective-permute-start
  16.3 1.5 %collective-permute-done = f32[264,256]{1,0:T(8,128)S(1)} collective-permute-done((f32[264,256]{1,0:T(8,128)S(1)}, f32[264,256]{1,0:T(8,128)S(1)}, u32[]{:S(2)}, u32[]{:S(2)}) %collective-permute-start) | collective-permute-done | bytes 270368 | tf_op jit(solution)/shard_map/ppermute | solution.py:377
  17.9 2.6 %collective-permute-start.1 = (f32[264,256]{1,0:T(8,128)S(1)}, f32[264,256]{1,0:T(8,128)S(1)}, u32[]{:S(2)}, u32[]{:S(2)}) collective-permute-start(f32[264,256]{1,0:T(8,128)S(1)} %add.24), channel_id=1, source_target_pairs={{0,8},{1,5},{2,10},{3,7},{4,12},{5,1},{6,14},{7,3},{8,0},{9,13},{1... | collective-permute-start | bytes 811016 | tf_op jit(solution)/shard_map/ppermute | solution.py:387
  20.5 7.5 %collective-permute-done.1 = f32[264,256]{1,0:T(8,128)S(1)} collective-permute-done((f32[264,256]{1,0:T(8,128)S(1)}, f32[264,256]{1,0:T(8,128)S(1)}, u32[]{:S(2)}, u32[]{:S(2)}) %collective-permute-start.1) | collective-permute-done | bytes 270368 | tf_op jit(solution)/shard_map/ppermute | solution.py:387
  28.1 0.1 collective-permute-start.2
  28.2 6.4 %collective-permute-done.2 = f32[264,256]{1,0:T(8,128)S(1)} collective-permute-done((f32[264,256]{1,0:T(8,128)S(1)}, f32[264,256]{1,0:T(8,128)S(1)}, u32[]{:S(2)}, u32[]{:S(2)}) %collective-permute-start.2) | collective-permute-done | bytes 270368 | tf_op jit(solution)/shard_map/ppermute | solution.py:387
  34.7 0.0 collective-permute-done.5.refs_0_
  34.7 0.1 collective-permute-start.6
  34.8 0.3 collective-permute-start.3
  35.1 6.2 %collective-permute-done.3 = f32[264,256]{1,0:T(8,128)S(1)} collective-permute-done((f32[264,256]{1,0:T(8,128)S(1)}, f32[264,256]{1,0:T(8,128)S(1)}, u32[]{:S(2)}, u32[]{:S(2)}) %collective-permute-start.3) | collective-permute-done | bytes 270368 | tf_op jit(solution)/shard_map/ppermute | solution.py:387
  41.3 0.1 collective-permute-start.4
  41.4 1.5 %collective-permute-done.4.theirs = f32[264,256]{1,0:T(8,128)S(1)} collective-permute-done((f32[264,256]{1,0:T(8,128)S(1)}, f32[264,256]{1,0:T(8,128)S(1)}, u32[]{:S(2)}, u32[]{:S(2)}) %collective-permute-start.4) | collective-permute-done | bytes 270368 | tf_op jit(solution)/shard_map/ppermute | solution.py:390
  42.9 0.0 collective-permute-done.6.refs_1_
  43.0 0.0 copy-done.2
  43.0 11.4 %back.1 = bf16[1024,512]{1,0:T(8,128)(2,1)} custom-call(s32[16]{0:T(128)S(1)} %copy-done.11, s32[1]{0:T(128)} %bitcast.place, bf16[2,4096,512]{2,1,0:T(8,128)(2,1)S(1)} %get-tuple-element.9.stored, f32[264,256]{1,0:T(8,128)S(1)} %add.27.mine, f32[264,256]{1,0:T(8,128)S(1)} %collective-permute-done.4.theirs, bf16[32,32]{1,0:T(8,128)(2,1)S(1)} %copy-done.7, ...), custom_call_target="tpu_custom_call" | custom-call | tf_op jit(solution)/shard_map/back/pallas_call | solution.py:302
  (18 shorter events, 0.2 us)
Async XLA Ops:
  0.0 5.4 %copy-start = (bf16[1024,512]{1,0:T(8,128)(2,1)S(1)}, bf16[1024,512]{1,0:T(8,128)(2,1)}, u32[]{:S(2)}) copy-start(bf16[1024,512]{1,0:T(8,128)(2,1)} %points.3) | copy-start | bytes 3145732
  0.0 5.4 %copy-start.3 = (bf16[512,512]{1,0:T(8,128)(2,1)S(1)}, bf16[512,512]{1,0:T(8,128)(2,1)}, u32[]{:S(2)}) copy-start(bf16[512,512]{1,0:T(8,128)(2,1)} %fx_weight.1) | copy-start | bytes 1572868
  0.0 5.4 %copy-start.4 = (bf16[512,512]{1,0:T(8,128)(2,1)S(1)}, bf16[512,512]{1,0:T(8,128)(2,1)}, u32[]{:S(2)}) copy-start(bf16[512,512]{1,0:T(8,128)(2,1)} %x_weight.1) | copy-start | bytes 1572868
  0.0 5.4 %copy-start.6 = (bf16[32,256]{1,0:T(8,128)(2,1)S(1)}, bf16[32,256]{1,0:T(8,128)(2,1)}, u32[]{:S(2)}) copy-start(bf16[32,256]{1,0:T(8,128)(2,1)} %slice_weight.1) | copy-start | bytes 49156
  0.0 5.5 %copy-start.10 = (f32[512]{0:T(512)S(1)}, f32[512]{0:T(512)}, u32[]{:S(2)}) copy-start(f32[512]{0:T(512)} %param.16) | copy-start | bytes 6148
  0.0 5.5 %copy-start.11 = (s32[16]{0:T(128)S(1)}, s32[16]{0:T(128)}, u32[]{:S(2)}) copy-start(s32[16]{0:T(128)} %sizes.3) | copy-start | bytes 196
  0.0 5.5 %copy-start.13 = (f32[32]{0:T(128)S(1)}, f32[32]{0:T(128)}, u32[]{:S(2)}) copy-start(f32[32]{0:T(128)} %param.20) | copy-start | bytes 388
  2.5 32.2 %collective-permute-start.5 = (bf16[1024,512]{1,0:T(8,128)(2,1)}, bf16[1024,512]{1,0:T(8,128)(2,1)S(1)}, u32[]{:S(2)}, u32[]{:S(2)}) collective-permute-start(bf16[1024,512]{1,0:T(8,128)(2,1)} %pad_maximum_fusion), channel_id=1, source_target_pairs={{0,2},{2,0},{1,3},{3,1},{4,6},{6,4},{5,7},{7,5},{8,10},{10,8},{9,1... | collective-permute-start | bytes 3145736 | tf_op jit(solution)/shard_map/ppermute | solution.py:370
  16.2 26.8 %copy-start.1 = (bf16[512,1024]{1,0:T(8,128)(2,1)S(1)}, bf16[512,1024]{1,0:T(8,128)(2,1)}, u32[]{:S(2)}) copy-start(bf16[512,1024]{1,0:T(8,128)(2,1)} %up.1) | copy-start | bytes 3145732
  16.2 26.8 %copy-start.2 = (bf16[1024,512]{1,0:T(8,128)(2,1)S(1)}, bf16[1024,512]{1,0:T(8,128)(2,1)}, u32[]{:S(2)}) copy-start(bf16[1024,512]{1,0:T(8,128)(2,1)} %down.1) | copy-start | bytes 3145732
  16.2 26.8 %copy-start.5 = (bf16[512,512]{1,0:T(8,128)(2,1)S(1)}, bf16[512,512]{1,0:T(8,128)(2,1)}, u32[]{:S(2)}) copy-start(bf16[512,512]{1,0:T(8,128)(2,1)} %out_weight.1) | copy-start | bytes 1572868
  16.2 26.8 %copy-start.7 = (bf16[32,32]{1,0:T(8,128)(2,1)S(1)}, bf16[32,32]{1,0:T(8,128)(2,1)}, u32[]{:S(2)}) copy-start(bf16[32,32]{1,0:T(8,128)(2,1)} %q_weight.1) | copy-start | bytes 6148
  16.2 26.8 %copy-start.8 = (bf16[32,32]{1,0:T(8,128)(2,1)S(1)}, bf16[32,32]{1,0:T(8,128)(2,1)}, u32[]{:S(2)}) copy-start(bf16[32,32]{1,0:T(8,128)(2,1)} %k_weight.1) | copy-start | bytes 6148
  16.2 26.8 %copy-start.9 = (bf16[32,32]{1,0:T(8,128)(2,1)S(1)}, bf16[32,32]{1,0:T(8,128)(2,1)}, u32[]{:S(2)}) copy-start(bf16[32,32]{1,0:T(8,128)(2,1)} %v_weight.1) | copy-start | bytes 6148
  16.2 26.8 %copy-start.12 = (f32[512]{0:T(512)S(1)}, f32[512]{0:T(512)}, u32[]{:S(2)}) copy-start(f32[512]{0:T(512)} %param.25) | copy-start | bytes 6148
  16.2 1.6 %collective-permute-start = (f32[264,256]{1,0:T(8,128)S(1)}, f32[264,256]{1,0:T(8,128)S(1)}, u32[]{:S(2)}, u32[]{:S(2)}) collective-permute-start(f32[264,256]{1,0:T(8,128)S(1)} %get-tuple-element.11), channel_id=1, source_target_pairs={{0,1},{1,0},{2,3},{3,2},{4,5},{5,4},{6,7},{7,6},{8,9},{9,8},{10,11... | collective-permute-start | bytes 811016 | tf_op jit(solution)/shard_map/ppermute | solution.py:377
  17.9 10.2 %collective-permute-start.1 = (f32[264,256]{1,0:T(8,128)S(1)}, f32[264,256]{1,0:T(8,128)S(1)}, u32[]{:S(2)}, u32[]{:S(2)}) collective-permute-start(f32[264,256]{1,0:T(8,128)S(1)} %add.24), channel_id=1, source_target_pairs={{0,8},{1,5},{2,10},{3,7},{4,12},{5,1},{6,14},{7,3},{8,0},{9,13},{1... | collective-permute-start | bytes 811016 | tf_op jit(solution)/shard_map/ppermute | solution.py:387
  28.1 6.5 %collective-permute-start.2 = (f32[264,256]{1,0:T(8,128)S(1)}, f32[264,256]{1,0:T(8,128)S(1)}, u32[]{:S(2)}, u32[]{:S(2)}) collective-permute-start(f32[264,256]{1,0:T(8,128)S(1)} %add.25), channel_id=1, source_target_pairs={{0,2},{1,9},{2,0},{3,11},{4,6},{5,13},{6,4},{7,15},{8,10},{9,1},{1... | collective-permute-start | bytes 811016 | tf_op jit(solution)/shard_map/ppermute | solution.py:387
  34.7 8.3 %collective-permute-start.6 = (bf16[1024,512]{1,0:T(8,128)(2,1)S(1)}, bf16[1024,512]{1,0:T(8,128)(2,1)S(1)}, u32[]{:S(2)}, u32[]{:S(2)}) collective-permute-start(bf16[1024,512]{1,0:T(8,128)(2,1)S(1)} %collective-permute-done.5.refs_0_), channel_id=1, source_target_pairs={{0,1},{1,0},{2,3},{3,2},{4,5},{5,4},{6,7},{7,6},{8,9},{9,8},{10,11... | collective-permute-start | bytes 3145736 | tf_op jit(solution)/shard_map/ppermute | solution.py:386
  34.8 6.5 %collective-permute-start.3 = (f32[264,256]{1,0:T(8,128)S(1)}, f32[264,256]{1,0:T(8,128)S(1)}, u32[]{:S(2)}, u32[]{:S(2)}) collective-permute-start(f32[264,256]{1,0:T(8,128)S(1)} %add.26), channel_id=1, source_target_pairs={{0,4},{1,3},{2,6},{3,1},{4,0},{5,7},{6,2},{7,5},{8,12},{9,11},{10,... | collective-permute-start | bytes 811016 | tf_op jit(solution)/shard_map/ppermute | solution.py:387
  41.3 1.6 %collective-permute-start.4 = (f32[264,256]{1,0:T(8,128)S(1)}, f32[264,256]{1,0:T(8,128)S(1)}, u32[]{:S(2)}, u32[]{:S(2)}) collective-permute-start(f32[264,256]{1,0:T(8,128)S(1)} %add.27.mine), channel_id=1, source_target_pairs={{0,1},{1,0},{2,3},{3,2},{4,5},{5,4},{6,7},{7,6},{8,9},{9,8},{10,11... | collective-permute-start | bytes 811016 | tf_op jit(solution)/shard_map/ppermute | solution.py:390

commit v4 on v3

--- a/solution.py
+++ b/solution.py
@@ -94,6 +94,11 @@
     def own(h):
         return slice(h * head_size, (h + 1) * head_size)
 
+    def add_sums(i, h):
+        totals[h // half, own(h % half), :] += dot_nt(
+            feats[own(h), :], stored[i, h * slices : (h + 1) * slices, :]
+        )
+
     def step(i, carry):
         here = points[pl.ds(pl.multiple_of(i * FRONT_ROWS, FRONT_ROWS), FRONT_ROWS), :]
         normed = layer_norm(here.astype(f32), gain[...])
@@ -108,25 +113,24 @@
         for q in range(0, heads, 2):
             group = range(q, q + 2)
             logits = [dot(slice_t[...], mids[own(h), :]) for h in group]
+            if q:
+                add_sums(i, q - 2)
+                add_sums(i, q - 1)
             tops = [jnp.max(l, axis=0, keepdims=True) for l in logits]
             raised = [
                 jnp.exp2((l - top) * scales[h : h + 1, :]) for h, l, top in zip(group, logits, tops)
             ]
             shares = [valid * pltpu.reciprocal(jnp.sum(r, axis=0, keepdims=True), approx=True) for r in raised]
             for h, r, share in zip(group, raised, shares):
-                rows = slice(h * slices, (h + 1) * slices)
                 weights = r * share
-                stored[i, rows, :] = weights.astype(bf16)
+                stored[i, h * slices : (h + 1) * slices, :] = weights.astype(bf16)
                 mass = weights[:, :128]
                 for c in range(1, FRONT_ROWS // 128):
                     mass = mass + weights[:, c * 128 : (c + 1) * 128]
                 mass_row = jnp.sum(mass.T, axis=0, keepdims=True)
                 totals[h // half, span + h % half : span + h % half + 1, :] += mass_row
-        for h in range(heads):
-            side, at = h // half, h % half
-            totals[side, own(at), :] += dot_nt(
-                feats[own(h), :], stored[i, h * slices : (h + 1) * slices, :]
-            )
+        add_sums(i, heads - 2)
+        add_sums(i, heads - 1)
         return carry
 
     lax.fori_loop(0, lax.div(live + FRONT_ROWS - 1, FRONT_ROWS), step, 0)
@@ -134,15 +138,85 @@
     send[...] = totals[1 - core]
 
 
+def mix_tokens(sums, crossed, value_t, repeat, tokens, queries, scores, probs, spread, at):
+    slices = sums.shape[1]
+    span = value_t.shape[0]
+    half = scores.shape[0]
+    head_size = span // half
+
+    def own(h):
+        return slice(h * head_size, (h + 1) * head_size)
+
+    parts = []
+    for h in range(half):
+        mass = sums[span + h : span + h + 1, :] + eps_mass
+        parts.append(sums[own(h), :] / mass)
+    wide = jnp.concatenate(parts, 0)
+    narrow = wide.astype(bf16)
+    asked = dot(crossed[0], narrow) + dot(crossed[1], narrow) + dot(crossed[2], narrow)
+    for i, part in enumerate(split3(asked * (math.log2(math.e) / math.sqrt(head_size)))):
+        for h in range(half):
+            queries[h, own(i), :] = part[own(h), :]
+    values = dot(value_t[...], narrow).astype(bf16)
+    tokens[...] = dot(narrow.astype(f32).T.astype(bf16), repeat[...]).astype(bf16)
+    for h in range(half):
+        scores[h] = dot(tokens[:, h * 128 : (h + 1) * 128], queries[h])
+    for h in range(half):
+        top = jnp.max(scores[h], axis=0, keepdims=True)
+        raised = jnp.exp2(scores[h] - top)
+        total = jnp.sum(raised, axis=0, keepdims=True)
+        probs[h] = (raised * pltpu.reciprocal(total, approx=True)).astype(bf16)
+        if h:
+            spread[at + (h - 1) * head_size : at + h * head_size, :] = dot(
+                values[own(h - 1), :], probs[h - 1]
+            ).astype(bf16)
+    spread[at + span - head_size : at + span, :] = dot(values[own(half - 1), :], probs[half - 1]).astype(bf16)
+
+
+def mix_weights(q_weight, k_weight, v_weight, crossed, value_t, repeat, queries):
+    half, head_size = queries.shape[0], q_weight.shape[0]
+    span = half * head_size
+    tiled = head_tile(dot_nt(k_weight[...], q_weight[...]), half)
+    for i, part in enumerate(split3(tiled)):
+        crossed[i] = part
+    value_t[...] = head_tile(v_weight[...].astype(f32), half).T.astype(bf16)
+    row = lax.broadcasted_iota(jnp.int32, (span, half * 128), 0)
+    col = lax.broadcasted_iota(jnp.int32, (span, half * 128), 1)
+    same = (lax.div(row, head_size) == lax.div(col, 128)) & (
+        lax.rem(row, head_size) == lax.rem(col, head_size)
+    )
+    repeat[...] = jnp.where(same, 1.0, 0.0).astype(bf16)
+    queries[...] = jnp.zeros_like(queries)
+
+
+def mix_kernel(sums, q_weight, k_weight, v_weight, out, crossed, value_t, repeat, tokens, queries, scores, probs):
+    mix_weights(q_weight, k_weight, v_weight, crossed, value_t, repeat, queries)
+    mix_tokens(sums, crossed, value_t, repeat, tokens, queries, scores, probs, out, 0)
+
+
+def mix_scratch(half, head_size, slices):
+    span = half * head_size
+    return [
+        pltpu.VMEM((3, span, span), bf16),
+        pltpu.VMEM((span, span), bf16),
+        pltpu.VMEM((span, half * 128), bf16),
+        pltpu.VMEM((slices, half * 128), bf16),
+        pltpu.VMEM((half, 128, slices), bf16),
+        pltpu.VMEM((half, slices, slices), f32),
+        pltpu.VMEM((half, slices, slices), bf16),
+    ]
+
+
 def back_kernel(
     sizes, place, stored, mine, theirs, q_weight, k_weight, v_weight, gain, points, out_weight, up, down, *refs
 ):
-    extra = len(refs) - 11
+    extra = len(refs) - 13
     sent = refs[:extra]
     (
         mixed,
         finished,
         spread,
+        mixed_here,
         desliced,
         crossed,
         value_t,
@@ -150,12 +224,13 @@
         tokens,
         queries,
         scores,
+        probs,
         arrived,
     ) = refs[extra:]
     head_size = q_weight.shape[0]
     slices = mine.shape[1]
-    half = mine.shape[0] // (head_size + 1)
-    span = half * head_size
+    span = mine.shape[0]
+    half = span // head_size
     heads = 2 * half
     rows, width = points.shape
     piece = up.shape[1] // 2
@@ -169,47 +244,19 @@
     def own(h):
         return slice(h * head_size, (h + 1) * head_size)
 
-    tiled = head_tile(dot_nt(k_weight[...], q_weight[...]), half)
-    for i, part in enumerate(split3(tiled)):
-        crossed[i] = part
-    value_t[...] = head_tile(v_weight[...].astype(f32), half).T.astype(bf16)
-    row = lax.broadcasted_iota(jnp.int32, (span, half * 128), 0)
-    col = lax.broadcasted_iota(jnp.int32, (span, half * 128), 1)
-    same = (lax.div(row, head_size) == lax.div(col, 128)) & (
-        lax.rem(row, head_size) == lax.rem(col, head_size)
-    )
-    repeat[...] = jnp.where(same, 1.0, 0.0).astype(bf16)
-    queries[...] = jnp.zeros_like(queries)
-    for side in range(2):
-        sums = jnp.where(low, mine[...], theirs[...]) if side == 0 else jnp.where(low, theirs[...], mine[...])
-        parts = []
-        for h in range(half):
-            mass = sums[span + h : span + h + 1, :] + eps_mass
-            parts.append(sums[own(h), :] / mass)
-        wide = jnp.concatenate(parts, 0)
-        narrow = wide.astype(bf16)
-        asked = dot(crossed[0], narrow) + dot(crossed[1], narrow) + dot(crossed[2], narrow)
-        for i, part in enumerate(split3(asked * (math.log2(math.e) / math.sqrt(head_size)))):
-            for h in range(half):
-                queries[side * half + h, own(i), :] = part[own(h), :]
-        values = dot(value_t[...], narrow).astype(bf16)
-        tokens[...] = dot(narrow.astype(f32).T.astype(bf16), repeat[...]).astype(bf16)
-        for h in range(half):
-            scores[h] = dot(tokens[:, h * 128 : (h + 1) * 128], queries[side * half + h])
-        for h in range(half):
-            top = jnp.max(scores[h], axis=0, keepdims=True)
-            raised = jnp.exp2(scores[h] - top)
-            total = jnp.sum(raised, axis=0, keepdims=True)
-            probs = (raised * pltpu.reciprocal(total, approx=True)).astype(bf16)
-            spread[own(side * half + h), :] = dot(values[own(h), :], probs).astype(bf16)
+    mix_weights(q_weight, k_weight, v_weight, crossed, value_t, repeat, queries)
+    mix_tokens(theirs, crossed, value_t, repeat, tokens, queries, scores, probs, mixed_here, 0)
+    own_side, other_side = mine[...].astype(f32), mixed_here[...].astype(f32)
+    spread[:span, :] = jnp.where(low, own_side, other_side).astype(bf16)
+    spread[span:, :] = jnp.where(low, other_side, own_side).astype(bf16)
 
     pieces = [
-        (up[:, c * piece : (c + 1) * piece], down[c * piece : (c + 1) * piece, :]) for c in range(2)
+        (up.at[:, pl.ds(c * piece, piece)], down.at[pl.ds(c * piece, piece), :]) for c in range(2)
     ]
     if piece == width:
-        pieces += [(r[:width, :], r[width:, :]) for r in sent]
+        pieces += [(r.at[pl.ds(0, width), :], r.at[pl.ds(width, piece), :]) for r in sent]
     else:
-        pieces += [(sent[2 * i][...], sent[2 * i + 1][...]) for i in range(extra // 2)]
+        pieces += [(sent[2 * i], sent[2 * i + 1]) for i in range(extra // 2)]
 
     def step(i, carry):
         per = BACK_ROWS // FRONT_ROWS
@@ -224,12 +271,12 @@
         residual = here.astype(f32) + dot(picked, out_weight[...])
         late = layer_norm(residual, gain[...])
         total = residual
-        raw = dot(late, pieces[0][0])
+        raw = dot(late, pieces[0][0][...])
         for n in range(len(pieces)):
             now = raw
             if n + 1 < len(pieces):
-                raw = dot(late, pieces[n + 1][0])
-            total = total + dot(gelu(now).astype(bf16), pieces[n][1])
+                raw = dot(late, pieces[n + 1][0][...])
+            total = total + dot(gelu(now).astype(bf16), pieces[n][1][...])
         row = lax.broadcasted_iota(jnp.int32, (BACK_ROWS, 1), 0) + i * BACK_ROWS
         finished[i] = jnp.where(row < live, total, 0.0).astype(bf16)
         leave(i).start()
@@ -290,14 +337,30 @@
     )
 
 
+def mix_call(sums, q_weight, k_weight, v_weight):
+    head_size = q_weight.shape[0]
+    slices = sums.shape[1]
+    half = sums.shape[0] // (head_size + 1)
+    return pl.pallas_call(
+        mix_kernel,
+        in_specs=[VMEM] * 4,
+        out_specs=VMEM,
+        out_shape=jax.ShapeDtypeStruct((half * head_size, slices), bf16),
+        scratch_shapes=mix_scratch(half, head_size, slices),
+        compiler_params=pltpu.CompilerParams(vmem_limit_bytes=12 * MIB),
+        cost_estimate=pl.CostEstimate(flops=300_000_000, bytes_accessed=500_000, transcendentals=600_000),
+        name="mix",
+    )(sums, q_weight, k_weight, v_weight)
+
+
 def back_call(
     sizes, place, stored, mine, theirs, q_weight, k_weight, v_weight, gain, points, out_weight, up, down, sent
 ):
     rows, width = points.shape
     head_size = q_weight.shape[0]
     slices = mine.shape[1]
-    half = mine.shape[0] // (head_size + 1)
-    span = half * head_size
+    span = mine.shape[0]
+    half = span // head_size
     blocks = rows // BACK_ROWS
     return pl.pallas_call(
         back_kernel,
@@ -307,13 +370,9 @@
         scratch_shapes=[
             pltpu.VMEM((blocks, BACK_ROWS, width), bf16),
             pltpu.VMEM((2 * span, slices), bf16),
+            pltpu.VMEM((span, slices), bf16),
             pltpu.VMEM((width, BACK_ROWS), f32),
-            pltpu.VMEM((3, span, span), bf16),
-            pltpu.VMEM((span, span), bf16),
-            pltpu.VMEM((span, half * 128), bf16),
-            pltpu.VMEM((slices, half * 128), bf16),
-            pltpu.VMEM((2 * half, 128, slices), bf16),
-            pltpu.VMEM((half, slices, slices), f32),
+            *mix_scratch(half, head_size, slices),
             pltpu.SemaphoreType.DMA((blocks,)),
         ],
         compiler_params=pltpu.CompilerParams(vmem_limit_bytes=36 * MIB),
@@ -388,11 +447,12 @@
             sums, axes, [(i, i ^ (odd if i & 1 else even)) for i in range(devices)]
         )
     theirs = lax.ppermute(sums, "sub", [(0, 1), (1, 0)])
+    mine = mix_call(sums, q_weight, k_weight, v_weight)
     return back_call(
         part_sizes,
         place,
         stored,
-        sums,
+        mine,
         theirs,
         q_weight,
         k_weight,

time: 54.7 us -> 52.1 us (0.952)
  the two profiles are of different devices: /device:TPU:0 before, /device:TPU:1 now
where the time goes in v4:
time: 52.1 us
  Pallas kernels  21.6 us (41%)
  waiting for transfers between devices  19.2 us (37%)
  starting transfers between devices  8.44 us (16%)
  local copies, waits for them, and re-layouts  1.47 us (3%)
  other arithmetic  1.18 us (2%)
    ppermute x3, waiting for transfers between devices, per_device(): lax.ppermute(sums, axes, [(i, i ^ (odd if i & 1 else even)) for i in rang...  17.7 us
    pallas_call x1, Pallas kernels, back_call(): pl.pallas_call(back_kernel, in_specs=[SMEM, SMEM] + [VMEM] * (11 + len(se...  10.2 us
    pallas_call x1, Pallas kernels, front_call(): pl.pallas_call(front_kernel, in_specs=[SMEM, SMEM] + [VMEM] * 6, out_spec...  10.1 us
    ppermute x3, starting transfers between devices, per_device(): lax.ppermute(sums, axes, [(i, i ^ (odd if i & 1 else even)) for i in rang...  4.9 us
    ppermute x1, starting transfers between devices, per_device(): lax.ppermute(half, 'ffn', [(i, (i + turn) % shards) for i in range(shards)])  2.04 us
    ppermute x1, waiting for transfers between devices, per_device(): received = lax.ppermute(send, 'sub', [(0, 1), (1, 0)])  1.53 us
    dynamic_slice x1, local copies, waits for them, and re-layouts, per_device(): lax.dynamic_slice_in_dim(down_weight, core * piece, piece, 0)  1.41 us
    ppermute x1, starting transfers between devices, per_device(): theirs = lax.ppermute(sums, 'sub', [(0, 1), (1, 0)])  1.35 us
  transfers between devices with their start and end apart: 7, of which 4 were waited for; matrix products, arithmetic and copies ran while one was open for 0% of the time, Pallas kernels for 22%

profile of v4, /device:TPU:1, one launch (start us, length us, event | category | flops | bytes accessed | tf_op | source)
XLA Modules:
  0.0 52.1 jit_solution(4706129950341497777)
XLA Ops:
  0.0 0.0 copy-start.6
  0.0 0.0 copy-start.10
  0.0 0.0 copy-start.12
  0.0 0.0 copy-start.13
  0.0 1.4 %constant_dynamic-slice_fusion = (bf16[512,512]{1,0:T(8,128)(2,1)S(1)}, bf16[512,512]{1,0:T(8,128)(2,1)S(1)}) fusion(bf16[1024,512]{1,0:T(8,128)(2,1)} %down.1, s32[]{:T(128)S(6)} %select_n.4, bf16[512,1024]{1,0:T(8,128)(2,1)} %up.1), kind=kLoop, calls=%fused_computation.1 | loop fusion | bytes 2097156 | tf_op jit(solution)/shard_map/dynamic_slice | solution.py:424
  1.5 1.0 %pad_maximum_fusion = bf16[1024,512]{1,0:T(8,128)(2,1)} fusion(bf16[512,512]{1,0:T(8,128)(2,1)S(1)} %get-tuple-element.13, bf16[512,512]{1,0:T(8,128)(2,1)S(1)} %get-tuple-element.14), kind=kLoop, calls=%fused_computation | loop fusion | flops 2097152 | bytes 2097152 | tf_op jit(solution)/shard_map/concatenate | solution.py:427
  2.5 2.0 %collective-permute-start.5 = (bf16[1024,512]{1,0:T(8,128)(2,1)}, bf16[1024,512]{1,0:T(8,128)(2,1)S(1)}, u32[]{:S(2)}, u32[]{:S(2)}) collective-permute-start(bf16[1024,512]{1,0:T(8,128)(2,1)} %pad_maximum_fusion), channel_id=1, source_target_pairs={{0,2},{2,0},{1,3},{3,1},{4,6},{6,4},{5,7},{7,5},{8,10},{10,8},{9,1... | collective-permute-start | bytes 3145736 | tf_op jit(solution)/shard_map/ppermute | solution.py:429
  4.5 0.0 copy-done
  4.6 0.0 copy-done.6
  4.6 0.0 copy-done.10
  4.6 0.0 copy-done.12
  4.6 0.0 copy-done.13
  4.6 10.1 %front.1 = (bf16[2,4096,512]{2,1,0:T(8,128)(2,1)S(1)}, f32[264,256]{1,0:T(8,128)S(1)}, f32[264,256]{1,0:T(8,128)S(1)}) custom-call(s32[16]{0:T(128)S(1)} %copy-done.12, s32[1]{0:T(128)} %bitcast.place, f32[1,512]{1,0:T(1,128)S(1)} %bitcast.4, bf16[32,256]{1,0:T(8,128)(2,1)S(1)} %copy-done.6, f32[1,32]{1,0:T(1,128)S(1)} %bitcast.6, ...), custom_call_target="tpu_custom_call" | custom-call | tf_op jit(solution)/shard_map/front/pallas_call | solution.py:308
  14.7 0.0 copy-start.7
  14.7 0.0 copy-start.8
  14.7 0.0 copy-start.9
  14.7 0.1 collective-permute-start
  14.8 1.5 %collective-permute-done = f32[264,256]{1,0:T(8,128)S(1)} collective-permute-done((f32[264,256]{1,0:T(8,128)S(1)}, f32[264,256]{1,0:T(8,128)S(1)}, u32[]{:S(2)}, u32[]{:S(2)}) %collective-permute-start) | collective-permute-done | bytes 270368 | tf_op jit(solution)/shard_map/ppermute | solution.py:436
  16.4 0.1 collective-permute-start.1
  16.5 7.3 %collective-permute-done.1 = f32[264,256]{1,0:T(8,128)S(1)} collective-permute-done((f32[264,256]{1,0:T(8,128)S(1)}, f32[264,256]{1,0:T(8,128)S(1)}, u32[]{:S(2)}, u32[]{:S(2)}) %collective-permute-start.1) | collective-permute-done | bytes 270368 | tf_op jit(solution)/shard_map/ppermute | solution.py:446
  23.8 3.8 %collective-permute-start.2 = (f32[264,256]{1,0:T(8,128)S(1)}, f32[264,256]{1,0:T(8,128)S(1)}, u32[]{:S(2)}, u32[]{:S(2)}) collective-permute-start(f32[264,256]{1,0:T(8,128)S(1)} %add.25), channel_id=1, source_target_pairs={{0,2},{1,9},{2,0},{3,11},{4,6},{5,13},{6,4},{7,15},{8,10},{9,1},{1... | collective-permute-start | bytes 811016 | tf_op jit(solution)/shard_map/ppermute | solution.py:446
  27.6 5.7 %collective-permute-done.2 = f32[264,256]{1,0:T(8,128)S(1)} collective-permute-done((f32[264,256]{1,0:T(8,128)S(1)}, f32[264,256]{1,0:T(8,128)S(1)}, u32[]{:S(2)}, u32[]{:S(2)}) %collective-permute-start.2) | collective-permute-done | bytes 270368 | tf_op jit(solution)/shard_map/ppermute | solution.py:446
  33.4 0.0 collective-permute-done.5.refs_0_
  33.4 0.1 collective-permute-start.6
  33.5 1.0 %collective-permute-start.3 = (f32[264,256]{1,0:T(8,128)S(1)}, f32[264,256]{1,0:T(8,128)S(1)}, u32[]{:S(2)}, u32[]{:S(2)}) collective-permute-start(f32[264,256]{1,0:T(8,128)S(1)} %add.26), channel_id=1, source_target_pairs={{0,4},{1,3},{2,6},{3,1},{4,0},{5,7},{6,2},{7,5},{8,12},{9,11},{10,... | collective-permute-start | bytes 811016 | tf_op jit(solution)/shard_map/ppermute | solution.py:446
  34.5 4.6 %collective-permute-done.3 = f32[264,256]{1,0:T(8,128)S(1)} collective-permute-done((f32[264,256]{1,0:T(8,128)S(1)}, f32[264,256]{1,0:T(8,128)S(1)}, u32[]{:S(2)}, u32[]{:S(2)}) %collective-permute-start.3) | collective-permute-done | bytes 270368 | tf_op jit(solution)/shard_map/ppermute | solution.py:446
  39.2 1.4 %collective-permute-start.4 = (f32[264,256]{1,0:T(8,128)S(1)}, f32[264,256]{1,0:T(8,128)S(1)}, u32[]{:S(2)}, u32[]{:S(2)}) collective-permute-start(f32[264,256]{1,0:T(8,128)S(1)} %add.27.sums), channel_id=1, source_target_pairs={{0,1},{1,0},{2,3},{3,2},{4,5},{5,4},{6,7},{7,6},{8,9},{9,8},{10,11... | collective-permute-start | bytes 811016 | tf_op jit(solution)/shard_map/ppermute | solution.py:449
  40.5 0.0 copy-done.8
  40.6 1.3 %mix.1.mine = bf16[256,256]{1,0:T(8,128)(2,1)S(1)} custom-call(f32[264,256]{1,0:T(8,128)S(1)} %add.27.sums, bf16[32,32]{1,0:T(8,128)(2,1)S(1)} %copy-done.7, bf16[32,32]{1,0:T(8,128)(2,1)S(1)} %copy-done.8, bf16[32,32]{1,0:T(8,128)(2,1)S(1)} %copy-done.9), custom_call_target="tpu_custom_call" | custom-call | flops 300000000 | bytes 500000 | tf_op jit(solution)/shard_map/mix/pallas_call | solution.py:344
  41.8 0.0 collective-permute-done.4.theirs
  41.8 0.0 collective-permute-done.6.refs_1_
  41.9 10.2 %back.1 = bf16[1024,512]{1,0:T(8,128)(2,1)} custom-call(s32[16]{0:T(128)S(1)} %copy-done.12, s32[1]{0:T(128)} %bitcast.place, bf16[2,4096,512]{2,1,0:T(8,128)(2,1)S(1)} %get-tuple-element.9.stored, bf16[256,256]{1,0:T(8,128)(2,1)S(1)} %mix.1.mine, f32[264,256]{1,0:T(8,128)S(1)} %collective-permute-done.4.theirs, bf16[32,32]{1,0:T(8,128)(2,1)S(1)} %copy-done.7, ...), custom_call_target="tpu_custom_call" | custom-call | tf_op jit(solution)/shard_map/back/pallas_call | solution.py:365
  (19 shorter events, 0.2 us)
Async XLA Ops:
  0.0 4.5 %copy-start = (bf16[1024,512]{1,0:T(8,128)(2,1)S(1)}, bf16[1024,512]{1,0:T(8,128)(2,1)}, u32[]{:S(2)}) copy-start(bf16[1024,512]{1,0:T(8,128)(2,1)} %points.3) | copy-start | bytes 3145732
  0.0 4.5 %copy-start.3 = (bf16[512,512]{1,0:T(8,128)(2,1)S(1)}, bf16[512,512]{1,0:T(8,128)(2,1)}, u32[]{:S(2)}) copy-start(bf16[512,512]{1,0:T(8,128)(2,1)} %fx_weight.1) | copy-start | bytes 1572868
  0.0 4.5 %copy-start.4 = (bf16[512,512]{1,0:T(8,128)(2,1)S(1)}, bf16[512,512]{1,0:T(8,128)(2,1)}, u32[]{:S(2)}) copy-start(bf16[512,512]{1,0:T(8,128)(2,1)} %x_weight.1) | copy-start | bytes 1572868
  0.0 4.5 %copy-start.6 = (bf16[32,256]{1,0:T(8,128)(2,1)S(1)}, bf16[32,256]{1,0:T(8,128)(2,1)}, u32[]{:S(2)}) copy-start(bf16[32,256]{1,0:T(8,128)(2,1)} %slice_weight.1) | copy-start | bytes 49156
  0.0 4.5 %copy-start.10 = (f32[512]{0:T(512)S(1)}, f32[512]{0:T(512)}, u32[]{:S(2)}) copy-start(f32[512]{0:T(512)} %param.16) | copy-start | bytes 6148
  0.0 4.5 %copy-start.12 = (s32[16]{0:T(128)S(1)}, s32[16]{0:T(128)}, u32[]{:S(2)}) copy-start(s32[16]{0:T(128)} %sizes.3) | copy-start | bytes 196
  0.0 4.5 %copy-start.13 = (f32[32]{0:T(128)S(1)}, f32[32]{0:T(128)}, u32[]{:S(2)}) copy-start(f32[32]{0:T(128)} %param.20) | copy-start | bytes 388
  2.5 30.9 %collective-permute-start.5 = (bf16[1024,512]{1,0:T(8,128)(2,1)}, bf16[1024,512]{1,0:T(8,128)(2,1)S(1)}, u32[]{:S(2)}, u32[]{:S(2)}) collective-permute-start(bf16[1024,512]{1,0:T(8,128)(2,1)} %pad_maximum_fusion), channel_id=1, source_target_pairs={{0,2},{2,0},{1,3},{3,1},{4,6},{6,4},{5,7},{7,5},{8,10},{10,8},{9,1... | collective-permute-start | bytes 3145736 | tf_op jit(solution)/shard_map/ppermute | solution.py:429
  14.7 25.9 %copy-start.7 = (bf16[32,32]{1,0:T(8,128)(2,1)S(1)}, bf16[32,32]{1,0:T(8,128)(2,1)}, u32[]{:S(2)}) copy-start(bf16[32,32]{1,0:T(8,128)(2,1)} %q_weight.3) | copy-start | bytes 6148
  14.7 25.9 %copy-start.8 = (bf16[32,32]{1,0:T(8,128)(2,1)S(1)}, bf16[32,32]{1,0:T(8,128)(2,1)}, u32[]{:S(2)}) copy-start(bf16[32,32]{1,0:T(8,128)(2,1)} %k_weight.3) | copy-start | bytes 6148
  14.7 25.8 %copy-start.9 = (bf16[32,32]{1,0:T(8,128)(2,1)S(1)}, bf16[32,32]{1,0:T(8,128)(2,1)}, u32[]{:S(2)}) copy-start(bf16[32,32]{1,0:T(8,128)(2,1)} %v_weight.3) | copy-start | bytes 6148
  14.7 1.6 %collective-permute-start = (f32[264,256]{1,0:T(8,128)S(1)}, f32[264,256]{1,0:T(8,128)S(1)}, u32[]{:S(2)}, u32[]{:S(2)}) collective-permute-start(f32[264,256]{1,0:T(8,128)S(1)} %get-tuple-element.11), channel_id=1, source_target_pairs={{0,1},{1,0},{2,3},{3,2},{4,5},{5,4},{6,7},{7,6},{8,9},{9,8},{10,11... | collective-permute-start | bytes 811016 | tf_op jit(solution)/shard_map/ppermute | solution.py:436
  16.3 25.5 %copy-start.1 = (bf16[512,1024]{1,0:T(8,128)(2,1)S(1)}, bf16[512,1024]{1,0:T(8,128)(2,1)}, u32[]{:S(2)}) copy-start(bf16[512,1024]{1,0:T(8,128)(2,1)} %up.1) | copy-start | bytes 3145732
  16.3 25.5 %copy-start.2 = (bf16[1024,512]{1,0:T(8,128)(2,1)S(1)}, bf16[1024,512]{1,0:T(8,128)(2,1)}, u32[]{:S(2)}) copy-start(bf16[1024,512]{1,0:T(8,128)(2,1)} %down.1) | copy-start | bytes 3145732
  16.3 25.6 %copy-start.5 = (bf16[512,512]{1,0:T(8,128)(2,1)S(1)}, bf16[512,512]{1,0:T(8,128)(2,1)}, u32[]{:S(2)}) copy-start(bf16[512,512]{1,0:T(8,128)(2,1)} %out_weight.1) | copy-start | bytes 1572868
  16.3 25.6 %copy-start.11 = (f32[512]{0:T(512)S(1)}, f32[512]{0:T(512)}, u32[]{:S(2)}) copy-start(f32[512]{0:T(512)} %param.25) | copy-start | bytes 6148
  16.4 7.4 %collective-permute-start.1 = (f32[264,256]{1,0:T(8,128)S(1)}, f32[264,256]{1,0:T(8,128)S(1)}, u32[]{:S(2)}, u32[]{:S(2)}) collective-permute-start(f32[264,256]{1,0:T(8,128)S(1)} %add.24), channel_id=1, source_target_pairs={{0,8},{1,5},{2,10},{3,7},{4,12},{5,1},{6,14},{7,3},{8,0},{9,13},{1... | collective-permute-start | bytes 811016 | tf_op jit(solution)/shard_map/ppermute | solution.py:446
  23.8 9.5 %collective-permute-start.2 = (f32[264,256]{1,0:T(8,128)S(1)}, f32[264,256]{1,0:T(8,128)S(1)}, u32[]{:S(2)}, u32[]{:S(2)}) collective-permute-start(f32[264,256]{1,0:T(8,128)S(1)} %add.25), channel_id=1, source_target_pairs={{0,2},{1,9},{2,0},{3,11},{4,6},{5,13},{6,4},{7,15},{8,10},{9,1},{1... | collective-permute-start | bytes 811016 | tf_op jit(solution)/shard_map/ppermute | solution.py:446
  33.4 8.4 %collective-permute-start.6 = (bf16[1024,512]{1,0:T(8,128)(2,1)S(1)}, bf16[1024,512]{1,0:T(8,128)(2,1)S(1)}, u32[]{:S(2)}, u32[]{:S(2)}) collective-permute-start(bf16[1024,512]{1,0:T(8,128)(2,1)S(1)} %collective-permute-done.5.refs_0_), channel_id=1, source_target_pairs={{0,1},{1,0},{2,3},{3,2},{4,5},{5,4},{6,7},{7,6},{8,9},{9,8},{10,11... | collective-permute-start | bytes 3145736 | tf_op jit(solution)/shard_map/ppermute | solution.py:445
  33.5 5.7 %collective-permute-start.3 = (f32[264,256]{1,0:T(8,128)S(1)}, f32[264,256]{1,0:T(8,128)S(1)}, u32[]{:S(2)}, u32[]{:S(2)}) collective-permute-start(f32[264,256]{1,0:T(8,128)S(1)} %add.26), channel_id=1, source_target_pairs={{0,4},{1,3},{2,6},{3,1},{4,0},{5,7},{6,2},{7,5},{8,12},{9,11},{10,... | collective-permute-start | bytes 811016 | tf_op jit(solution)/shard_map/ppermute | solution.py:446
  39.2 2.6 %collective-permute-start.4 = (f32[264,256]{1,0:T(8,128)S(1)}, f32[264,256]{1,0:T(8,128)S(1)}, u32[]{:S(2)}, u32[]{:S(2)}) collective-permute-start(f32[264,256]{1,0:T(8,128)S(1)} %add.27.sums), channel_id=1, source_target_pairs={{0,1},{1,0},{2,3},{3,2},{4,5},{5,4},{6,7},{7,6},{8,9},{9,8},{10,11... | collective-permute-start | bytes 811016 | tf_op jit(solution)/shard_map/ppermute | solution.py:449

commit v5 on v4

--- a/solution.py
+++ b/solution.py
@@ -54,6 +54,7 @@
 
 
 def front_kernel(
+    zunit,
     sizes,
     place,
     gain,
@@ -76,10 +77,9 @@
     head_size, slices = slice_weight.shape
     width = points.shape[1]
     heads = width // head_size
-    half = heads // 2
-    span = half * head_size
+    quarter = heads // 4
     live = sizes[place[0]]
-    core = place[0] % 2
+    core, turn = place[0] % 2, lax.div(place[0], zunit) % 2
     totals[...] = jnp.zeros_like(totals)
     slice_t[...] = slice_weight[...].astype(f32).T.astype(bf16)
     wide = jnp.concatenate([temp_vector[...]] * heads, 1)
@@ -95,7 +95,7 @@
         return slice(h * head_size, (h + 1) * head_size)
 
     def add_sums(i, h):
-        totals[h // half, own(h % half), :] += dot_nt(
+        totals[h // quarter, own(h % quarter), :] += dot_nt(
             feats[own(h), :], stored[i, h * slices : (h + 1) * slices, :]
         )
 
@@ -110,12 +110,12 @@
         scales = math.log2(math.e) / temps
         col = lax.broadcasted_iota(jnp.int32, (1, FRONT_ROWS), 1) + i * FRONT_ROWS
         valid = jnp.where(col < live, 1.0, 0.0)
-        for q in range(0, heads, 2):
-            group = range(q, q + 2)
+        for q in range(0, heads, 1):
+            group = range(q, q + 1)
             logits = [dot(slice_t[...], mids[own(h), :]) for h in group]
             if q:
-                add_sums(i, q - 2)
-                add_sums(i, q - 1)
+                for h in range(q - 1, q):
+                    add_sums(i, h)
             tops = [jnp.max(l, axis=0, keepdims=True) for l in logits]
             raised = [
                 jnp.exp2((l - top) * scales[h : h + 1, :]) for h, l, top in zip(group, logits, tops)
@@ -128,14 +128,16 @@
                 for c in range(1, FRONT_ROWS // 128):
                     mass = mass + weights[:, c * 128 : (c + 1) * 128]
                 mass_row = jnp.sum(mass.T, axis=0, keepdims=True)
-                totals[h // half, span + h % half : span + h % half + 1, :] += mass_row
-        add_sums(i, heads - 2)
-        add_sums(i, heads - 1)
+                at = quarter * head_size + h % quarter
+                totals[h // quarter, at : at + 1, :] += mass_row
+        for h in range(heads - 1, heads):
+            add_sums(i, h)
         return carry
 
     lax.fori_loop(0, lax.div(live + FRONT_ROWS - 1, FRONT_ROWS), step, 0)
-    keep[...] = totals[core]
-    send[...] = totals[1 - core]
+    for n in range(2):
+        keep[n] = totals[2 * core + (turn if n == 0 else 1 - turn)]
+        send[n] = totals[2 * (1 - core) + (turn if n == 0 else 1 - turn)]
 
 
 def mix_tokens(sums, crossed, value_t, repeat, tokens, queries, scores, probs, spread, at):
@@ -208,34 +210,19 @@
 
 
 def back_kernel(
-    sizes, place, stored, mine, theirs, q_weight, k_weight, v_weight, gain, points, out_weight, up, down, *refs
+    zunit, sizes, place, stored, mine, across, along, corner, gain, points, out_weight, up, down, *refs
 ):
-    extra = len(refs) - 13
+    extra = len(refs) - 5
     sent = refs[:extra]
-    (
-        mixed,
-        finished,
-        spread,
-        mixed_here,
-        desliced,
-        crossed,
-        value_t,
-        repeat,
-        tokens,
-        queries,
-        scores,
-        probs,
-        arrived,
-    ) = refs[extra:]
-    head_size = q_weight.shape[0]
-    slices = mine.shape[1]
-    span = mine.shape[0]
-    half = span // head_size
-    heads = 2 * half
+    mixed, finished, spread, desliced, arrived = refs[extra:]
+    span, slices = mine.shape
     rows, width = points.shape
+    heads = stored.shape[1] // slices
+    head_size = width // heads
     piece = up.shape[1] // 2
     live = sizes[place[0]]
     low = place[0] % 2 == 0
+    near = lax.div(place[0], zunit) % 2 == 0
     blocks = rows // BACK_ROWS
     def leave(i):
         here = pl.ds(pl.multiple_of(i * BACK_ROWS, BACK_ROWS), BACK_ROWS)
@@ -244,11 +231,12 @@
     def own(h):
         return slice(h * head_size, (h + 1) * head_size)
 
-    mix_weights(q_weight, k_weight, v_weight, crossed, value_t, repeat, queries)
-    mix_tokens(theirs, crossed, value_t, repeat, tokens, queries, scores, probs, mixed_here, 0)
-    own_side, other_side = mine[...].astype(f32), mixed_here[...].astype(f32)
-    spread[:span, :] = jnp.where(low, own_side, other_side).astype(bf16)
-    spread[span:, :] = jnp.where(low, other_side, own_side).astype(bf16)
+    wide = [piece[...].astype(f32) for piece in (mine, across, along, corner)]
+    for side in range(2):
+        here = [jnp.where(low, wide[n + side], wide[n + 1 - side]) for n in (0, 2)]
+        for part in range(2):
+            at = (2 * side + part) * span
+            spread[at : at + span, :] = jnp.where(near, here[part], here[1 - part]).astype(bf16)
 
     pieces = [
         (up.at[:, pl.ds(c * piece, piece)], down.at[pl.ds(c * piece, piece), :]) for c in range(2)
@@ -300,19 +288,19 @@
 HBM = pl.BlockSpec(memory_space=pltpu.HBM)
 
 
-def front_call(sizes, place, points, gain, fx_weight, x_weight, slice_weight, temp_vector):
+def front_call(zunit, sizes, place, points, gain, fx_weight, x_weight, slice_weight, temp_vector):
     rows, width = points.shape
     head_size, slices = slice_weight.shape
     heads = width // head_size
-    sums_rows = heads // 2 * (head_size + 1)
+    sums_rows = -(-(heads // 4 * (head_size + 1)) // 8) * 8
     return pl.pallas_call(
-        front_kernel,
+        functools.partial(front_kernel, zunit),
         in_specs=[SMEM, SMEM] + [VMEM] * 6,
         out_specs=[VMEM, VMEM, VMEM],
         out_shape=[
             jax.ShapeDtypeStruct((rows // FRONT_ROWS, heads * slices, FRONT_ROWS), bf16),
-            jax.ShapeDtypeStruct((sums_rows, slices), f32),
-            jax.ShapeDtypeStruct((sums_rows, slices), f32),
+            jax.ShapeDtypeStruct((2, sums_rows, slices), f32),
+            jax.ShapeDtypeStruct((2, sums_rows, slices), f32),
         ],
         scratch_shapes=[
             pltpu.VMEM((width, width), bf16),
@@ -321,7 +309,7 @@
             pltpu.VMEM((3 * heads, width), bf16),
             pltpu.VMEM((width, FRONT_ROWS), bf16),
             pltpu.VMEM((width, FRONT_ROWS), bf16),
-            pltpu.VMEM((2, sums_rows, slices), f32),
+            pltpu.VMEM((4, sums_rows, slices), f32),
         ],
         compiler_params=pltpu.CompilerParams(vmem_limit_bytes=32 * MIB),
         name="front",
@@ -353,26 +341,19 @@
     )(sums, q_weight, k_weight, v_weight)
 
 
-def back_call(
-    sizes, place, stored, mine, theirs, q_weight, k_weight, v_weight, gain, points, out_weight, up, down, sent
-):
+def back_call(zunit, sizes, place, stored, tokens, gain, points, out_weight, up, down, sent):
     rows, width = points.shape
-    head_size = q_weight.shape[0]
-    slices = mine.shape[1]
-    span = mine.shape[0]
-    half = span // head_size
+    slices = tokens[0].shape[1]
     blocks = rows // BACK_ROWS
     return pl.pallas_call(
-        back_kernel,
-        in_specs=[SMEM, SMEM] + [VMEM] * (11 + len(sent)),
+        functools.partial(back_kernel, zunit),
+        in_specs=[SMEM, SMEM] + [VMEM] * (10 + len(sent)),
         out_specs=HBM,
         out_shape=jax.ShapeDtypeStruct((rows, width), bf16),
         scratch_shapes=[
             pltpu.VMEM((blocks, BACK_ROWS, width), bf16),
-            pltpu.VMEM((2 * span, slices), bf16),
-            pltpu.VMEM((span, slices), bf16),
+            pltpu.VMEM((width, slices), bf16),
             pltpu.VMEM((width, BACK_ROWS), f32),
-            *mix_scratch(half, head_size, slices),
             pltpu.SemaphoreType.DMA((blocks,)),
         ],
         compiler_params=pltpu.CompilerParams(vmem_limit_bytes=36 * MIB),
@@ -381,11 +362,7 @@
         sizes,
         place,
         stored,
-        mine,
-        theirs,
-        q_weight,
-        k_weight,
-        v_weight,
+        *tokens,
         gain[None, :],
         points,
         out_weight,
@@ -430,33 +407,34 @@
         for turn in range(1, shards)
         for half in halves
     ]
+    zunit = 2 * shards
     stored, keep, send = front_call(
-        part_sizes, place, points, norm1_gain, fx_weight, x_weight, slice_weight, temp_vector
+        zunit, part_sizes, place, points, norm1_gain, fx_weight, x_weight, slice_weight, temp_vector
     )
     received = lax.ppermute(send, "sub", [(0, 1), (1, 0)])
     bits = [2 << b for b in range((devices // 2).bit_length() - 1)]
-    zs = [b for b in bits if b >= 2 * shards]
-    xs = [b for b in bits if b < 2 * shards]
-    even_order, odd_order = zs[1:] + xs + zs[:1], zs + xs
-    sums = keep + received
-    for n, (even, odd) in enumerate(zip(even_order, odd_order)):
-        if n == 2:
+    zs = [b for b in bits if b > zunit]
+    xs = [b for b in bits if b < zunit]
+
+    def swap(x, even, odd):
+        return lax.ppermute(x, axes, [(i, i ^ (odd if i & 1 else even)) for i in range(devices)])
+
+    sums = keep[0] + received[0] + swap(keep[1] + received[1], zunit, zunit)
+    for n, (even, odd) in enumerate(zip(zs + xs, xs + zs)):
+        if n == len(zs + xs) - 1:
             ready = lax.optimization_barrier((tuple(far_pieces), sums))[0]
             hops = [lax.ppermute(piece, "sub", [(0, 1), (1, 0)]) for piece in ready]
-        sums = sums + lax.ppermute(
-            sums, axes, [(i, i ^ (odd if i & 1 else even)) for i in range(devices)]
-        )
-    theirs = lax.ppermute(sums, "sub", [(0, 1), (1, 0)])
+        sums = sums + swap(sums, even, odd)
     mine = mix_call(sums, q_weight, k_weight, v_weight)
+    along = swap(mine, zunit, zunit)
+    pair = lax.ppermute(jnp.stack([mine, along]), "sub", [(0, 1), (1, 0)])
+    tokens = [mine, pair[0], along, pair[1]]
     return back_call(
+        zunit,
         part_sizes,
         place,
         stored,
-        mine,
-        theirs,
-        q_weight,
-        k_weight,
-        v_weight,
+        tokens,
         norm2_gain,
         points,
         out_weight,

time: 52.1 us -> 51.4 us (0.987)
  the two profiles are of different devices: /device:TPU:1 before, /device:TPU:17 now
where the time goes in v5:
time: 51.4 us; the launch traced here: 50.8 us
  waiting for transfers between devices  21.4 us (42%)
  Pallas kernels  19.7 us (38%)
  starting transfers between devices  6.87 us (13%)
  local copies, waits for them, and re-layouts  1.49 us (3%)
  other arithmetic  1.14 us (2%)
    ppermute x4, waiting for transfers between devices, swap(): lax.ppermute(x, axes, [(i, i ^ (odd if i & 1 else even)) for i in range(d...  18.8 us
    pallas_call x1, Pallas kernels, front_call(): pl.pallas_call(functools.partial(front_kernel, zunit), in_specs=[SMEM, SM...  9.65 us
    pallas_call x1, Pallas kernels, back_call(): pl.pallas_call(functools.partial(back_kernel, zunit), in_specs=[SMEM, SME...  8.99 us
    ppermute x4, starting transfers between devices, swap(): lax.ppermute(x, axes, [(i, i ^ (odd if i & 1 else even)) for i in range(d...  4.82 us
    ppermute x1, waiting for transfers between devices, per_device(): received = lax.ppermute(send, 'sub', [(0, 1), (1, 0)])  1.55 us
    dynamic_slice x1, local copies, waits for them, and re-layouts, per_device(): lax.dynamic_slice_in_dim(down_weight, core * piece, piece, 0)  1.41 us
    ppermute x1, starting transfers between devices, per_device(): lax.ppermute(half, 'ffn', [(i, (i + turn) % shards) for i in range(shards)])  1.21 us
    concatenate x1, other arithmetic, per_device(): halves = (jnp.concatenate(halves, 0),)  1.04 us
  transfers between devices with their start and end apart: 8, of which 6 were waited for; matrix products, arithmetic and copies ran while one was open for 0% of the time, Pallas kernels for 21%

profile of v5, /device:TPU:17, one launch (start us, length us, event | category | flops | bytes accessed | tf_op | source)
XLA Modules:
  0.0 50.8 jit_solution(11242965250614991162)
XLA Ops:
  0.0 0.0 copy-start.6
  0.0 0.0 copy-start.7
  0.0 0.0 copy-start.9
  0.0 0.0 copy-start.10
  0.0 1.4 %constant_dynamic-slice_fusion = (bf16[512,512]{1,0:T(8,128)(2,1)S(1)}, bf16[512,512]{1,0:T(8,128)(2,1)S(1)}) fusion(bf16[1024,512]{1,0:T(8,128)(2,1)} %down.1, s32[]{:T(128)S(6)} %select_n.4, bf16[512,1024]{1,0:T(8,128)(2,1)} %up.1), kind=kLoop, calls=%fused_computation.9 | loop fusion | bytes 2097156 | tf_op jit(solution)/shard_map/dynamic_slice | solution.py:401
  1.5 1.0 %pad_maximum_fusion = bf16[1024,512]{1,0:T(8,128)(2,1)} fusion(bf16[512,512]{1,0:T(8,128)(2,1)S(1)} %get-tuple-element.15, bf16[512,512]{1,0:T(8,128)(2,1)S(1)} %get-tuple-element.16), kind=kLoop, calls=%fused_computation | loop fusion | flops 2097152 | bytes 2097152 | tf_op jit(solution)/shard_map/concatenate | solution.py:404
  2.5 1.2 %collective-permute-start.6 = (bf16[1024,512]{1,0:T(8,128)(2,1)}, bf16[1024,512]{1,0:T(8,128)(2,1)S(1)}, u32[]{:S(2)}, u32[]{:S(2)}) collective-permute-start(bf16[1024,512]{1,0:T(8,128)(2,1)} %pad_maximum_fusion), channel_id=1, source_target_pairs={{0,2},{2,0},{1,3},{3,1},{4,6},{6,4},{5,7},{7,5},{8,10},{10,8},{9,1... | collective-permute-start | bytes 3145736 | tf_op jit(solution)/shard_map/ppermute | solution.py:406
  3.7 0.0 copy-done.3
  3.8 9.7 %front.1 = (bf16[2,4096,512]{2,1,0:T(8,128)(2,1)S(1)}, f32[2,136,256]{2,1,0:T(8,128)S(1)}, f32[2,136,256]{2,1,0:T(8,128)S(1)}) custom-call(s32[16]{0:T(128)S(1)} %copy-done.9, s32[1]{0:T(128)} %bitcast.place, f32[1,512]{1,0:T(1,128)S(1)} %bitcast.18, bf16[32,256]{1,0:T(8,128)(2,1)S(1)} %copy-done.6, f32[1,32]{1,0:T(1,128)S(1)} %bitcast.20, ...), custom_call_target="tpu_custom_call" | custom-call | tf_op jit(solution)/shard_map/front/pallas_call | solution.py:296
  13.4 0.0 copy-start.1
  13.4 0.0 copy-start.2
  13.5 0.0 copy-start.5
  13.5 0.0 copy-start.8
  13.5 0.1 collective-permute-start
  13.6 1.5 %collective-permute-done = f32[2,136,256]{2,1,0:T(8,128)S(1)} collective-permute-done((f32[2,136,256]{2,1,0:T(8,128)S(1)}, f32[2,136,256]{2,1,0:T(8,128)S(1)}, u32[]{:S(2)}, u32[]{:S(2)}) %collective-permute-start) | collective-permute-done | bytes 278560 | tf_op jit(solution)/shard_map/ppermute | solution.py:414
  15.1 1.4 %collective-permute-start.1 = (f32[136,256]{1,0:T(8,128)S(1)}, f32[136,256]{1,0:T(8,128)S(1)}, u32[]{:S(2)}, u32[]{:S(2)}) collective-permute-start(f32[136,256]{1,0:T(8,128)S(1)} %fusion), channel_id=1, source_target_pairs={{0,4},{1,5},{2,6},{3,7},{4,0},{5,1},{6,2},{7,3},{8,12},{9,13},{10,... | collective-permute-start | bytes 417800 | tf_op jit(solution)/shard_map/ppermute | solution.py:420
  16.5 3.8 %collective-permute-done.1 = f32[136,256]{1,0:T(8,128)S(1)} collective-permute-done((f32[136,256]{1,0:T(8,128)S(1)}, f32[136,256]{1,0:T(8,128)S(1)}, u32[]{:S(2)}, u32[]{:S(2)}) %collective-permute-start.1) | collective-permute-done | bytes 139296 | tf_op jit(solution)/shard_map/ppermute | solution.py:420
  20.4 0.8 %collective-permute-start.2 = (f32[136,256]{1,0:T(8,128)S(1)}, f32[136,256]{1,0:T(8,128)S(1)}, u32[]{:S(2)}, u32[]{:S(2)}) collective-permute-start(f32[136,256]{1,0:T(8,128)S(1)} %fusion.2), channel_id=1, source_target_pairs={{0,8},{1,3},{2,10},{3,1},{4,12},{5,7},{6,14},{7,5},{8,0},{9,11},{1... | collective-permute-start | bytes 417800 | tf_op jit(solution)/shard_map/ppermute | solution.py:420
  21.2 7.9 %collective-permute-done.2 = f32[136,256]{1,0:T(8,128)S(1)} collective-permute-done((f32[136,256]{1,0:T(8,128)S(1)}, f32[136,256]{1,0:T(8,128)S(1)}, u32[]{:S(2)}, u32[]{:S(2)}) %collective-permute-start.2) | collective-permute-done | bytes 139296 | tf_op jit(solution)/shard_map/ppermute | solution.py:420
  29.1 0.0 collective-permute-done.6.refs_0_
  29.1 0.3 collective-permute-start.7
  29.4 0.0 collective-permute-start.3
  29.4 4.9 %collective-permute-done.3 = f32[136,256]{1,0:T(8,128)S(1)} collective-permute-done((f32[136,256]{1,0:T(8,128)S(1)}, f32[136,256]{1,0:T(8,128)S(1)}, u32[]{:S(2)}, u32[]{:S(2)}) %collective-permute-start.3) | collective-permute-done | bytes 139296 | tf_op jit(solution)/shard_map/ppermute | solution.py:420
  34.4 0.0 copy-done.12
  34.4 0.0 copy-done.13
  34.4 1.0 %mix.1.mine = bf16[128,256]{1,0:T(8,128)(2,1)S(1)} custom-call(f32[136,256]{1,0:T(8,128)S(1)} %add.39.sums, bf16[32,32]{1,0:T(8,128)(2,1)S(1)} %copy-done.11, bf16[32,32]{1,0:T(8,128)(2,1)S(1)} %copy-done.12, bf16[32,32]{1,0:T(8,128)(2,1)S(1)} %copy-done.13), custom_call_target="tpu_custom_call" | custom-call | flops 300000000 | bytes 500000 | tf_op jit(solution)/shard_map/mix/pallas_call | solution.py:332
  35.4 2.6 %collective-permute-start.4 = (bf16[128,256]{1,0:T(8,128)(2,1)S(1)}, bf16[128,256]{1,0:T(8,128)(2,1)S(1)}, u32[]{:S(2)}, u32[]{:S(2)}) collective-permute-start(bf16[128,256]{1,0:T(8,128)(2,1)S(1)} %mix.1.mine), channel_id=1, source_target_pairs={{0,4},{1,5},{2,6},{3,7},{4,0},{5,1},{6,2},{7,3},{8,12},{9,13},{10,... | collective-permute-start | bytes 196616 | tf_op jit(solution)/shard_map/ppermute | solution.py:420
  38.1 2.2 %collective-permute-done.4.along = bf16[128,256]{1,0:T(8,128)(2,1)S(1)} collective-permute-done((bf16[128,256]{1,0:T(8,128)(2,1)S(1)}, bf16[128,256]{1,0:T(8,128)(2,1)S(1)}, u32[]{:S(2)}, u32[]{:S(2)}) %collective-permute-start.4) | collective-permute-done | bytes 65568 | tf_op jit(solution)/shard_map/ppermute | solution.py:420
  40.3 0.5 collective-permute-start.5
  40.7 1.0 %collective-permute-done.5 = bf16[2,128,256]{2,1,0:T(8,128)(2,1)S(1)} collective-permute-done((bf16[2,128,256]{2,1,0:T(8,128)(2,1)S(1)}, bf16[2,128,256]{2,1,0:T(8,128)(2,1)S(1)}, u32[]{:S(2)}, u32[]{:S(2)}) %collective-permute-start.5) | collective-permute-done | bytes 131104 | tf_op jit(solution)/shard_map/ppermute | solution.py:430
  41.7 0.0 collective-permute-done.7.refs_1_
  41.8 9.0 %back.1 = bf16[1024,512]{1,0:T(8,128)(2,1)} custom-call(s32[16]{0:T(128)S(1)} %copy-done.9, s32[1]{0:T(128)} %bitcast.place, bf16[2,4096,512]{2,1,0:T(8,128)(2,1)S(1)} %get-tuple-element.9.stored, bf16[128,256]{1,0:T(8,128)(2,1)S(1)} %mix.1.mine, bf16[128,256]{1,0:T(8,128)(2,1)S(1)} %get-tuple-element.14.across, ...), custom_call_target="tpu_custom_call" | custom-call | tf_op jit(solution)/shard_map/back/pallas_call | solution.py:348
  (23 shorter events, 0.1 us)
Async XLA Ops:
  0.0 3.7 %copy-start = (bf16[1024,512]{1,0:T(8,128)(2,1)S(1)}, bf16[1024,512]{1,0:T(8,128)(2,1)}, u32[]{:S(2)}) copy-start(bf16[1024,512]{1,0:T(8,128)(2,1)} %points.3) | copy-start | bytes 3145732
  0.0 3.7 %copy-start.3 = (bf16[512,512]{1,0:T(8,128)(2,1)S(1)}, bf16[512,512]{1,0:T(8,128)(2,1)}, u32[]{:S(2)}) copy-start(bf16[512,512]{1,0:T(8,128)(2,1)} %fx_weight.1) | copy-start | bytes 1572868
  0.0 3.7 %copy-start.4 = (bf16[512,512]{1,0:T(8,128)(2,1)S(1)}, bf16[512,512]{1,0:T(8,128)(2,1)}, u32[]{:S(2)}) copy-start(bf16[512,512]{1,0:T(8,128)(2,1)} %x_weight.1) | copy-start | bytes 1572868
  0.0 3.7 %copy-start.6 = (bf16[32,256]{1,0:T(8,128)(2,1)S(1)}, bf16[32,256]{1,0:T(8,128)(2,1)}, u32[]{:S(2)}) copy-start(bf16[32,256]{1,0:T(8,128)(2,1)} %slice_weight.1) | copy-start | bytes 49156
  0.0 3.7 %copy-start.7 = (f32[512]{0:T(512)S(1)}, f32[512]{0:T(512)}, u32[]{:S(2)}) copy-start(f32[512]{0:T(512)} %param.16) | copy-start | bytes 6148
  0.0 3.7 %copy-start.9 = (s32[16]{0:T(128)S(1)}, s32[16]{0:T(128)}, u32[]{:S(2)}) copy-start(s32[16]{0:T(128)} %sizes.3) | copy-start | bytes 196
  0.0 3.7 %copy-start.10 = (f32[32]{0:T(128)S(1)}, f32[32]{0:T(128)}, u32[]{:S(2)}) copy-start(f32[32]{0:T(128)} %param.20) | copy-start | bytes 388
  2.5 31.9 %copy-start.11 = (bf16[32,32]{1,0:T(8,128)(2,1)S(1)}, bf16[32,32]{1,0:T(8,128)(2,1)}, u32[]{:S(2)}) copy-start(bf16[32,32]{1,0:T(8,128)(2,1)} %q_weight.1) | copy-start | bytes 6148
  2.5 31.9 %copy-start.12 = (bf16[32,32]{1,0:T(8,128)(2,1)S(1)}, bf16[32,32]{1,0:T(8,128)(2,1)}, u32[]{:S(2)}) copy-start(bf16[32,32]{1,0:T(8,128)(2,1)} %k_weight.1) | copy-start | bytes 6148
  2.5 31.9 %copy-start.13 = (bf16[32,32]{1,0:T(8,128)(2,1)S(1)}, bf16[32,32]{1,0:T(8,128)(2,1)}, u32[]{:S(2)}) copy-start(bf16[32,32]{1,0:T(8,128)(2,1)} %v_weight.1) | copy-start | bytes 6148
  2.5 26.6 %collective-permute-start.6 = (bf16[1024,512]{1,0:T(8,128)(2,1)}, bf16[1024,512]{1,0:T(8,128)(2,1)S(1)}, u32[]{:S(2)}, u32[]{:S(2)}) collective-permute-start(bf16[1024,512]{1,0:T(8,128)(2,1)} %pad_maximum_fusion), channel_id=1, source_target_pairs={{0,2},{2,0},{1,3},{3,1},{4,6},{6,4},{5,7},{7,5},{8,10},{10,8},{9,1... | collective-permute-start | bytes 3145736 | tf_op jit(solution)/shard_map/ppermute | solution.py:406
  13.4 28.3 %copy-start.1 = (bf16[512,1024]{1,0:T(8,128)(2,1)S(1)}, bf16[512,1024]{1,0:T(8,128)(2,1)}, u32[]{:S(2)}) copy-start(bf16[512,1024]{1,0:T(8,128)(2,1)} %up.1) | copy-start | bytes 3145732
  13.4 28.3 %copy-start.2 = (bf16[1024,512]{1,0:T(8,128)(2,1)S(1)}, bf16[1024,512]{1,0:T(8,128)(2,1)}, u32[]{:S(2)}) copy-start(bf16[1024,512]{1,0:T(8,128)(2,1)} %down.1) | copy-start | bytes 3145732
  13.5 28.3 %copy-start.5 = (bf16[512,512]{1,0:T(8,128)(2,1)S(1)}, bf16[512,512]{1,0:T(8,128)(2,1)}, u32[]{:S(2)}) copy-start(bf16[512,512]{1,0:T(8,128)(2,1)} %out_weight.1) | copy-start | bytes 1572868
  13.5 28.3 %copy-start.8 = (f32[512]{0:T(512)S(1)}, f32[512]{0:T(512)}, u32[]{:S(2)}) copy-start(f32[512]{0:T(512)} %param.25) | copy-start | bytes 6148
  13.5 1.6 %collective-permute-start = (f32[2,136,256]{2,1,0:T(8,128)S(1)}, f32[2,136,256]{2,1,0:T(8,128)S(1)}, u32[]{:S(2)}, u32[]{:S(2)}) collective-permute-start(f32[2,136,256]{2,1,0:T(8,128)S(1)} %get-tuple-element.11), channel_id=1, source_target_pairs={{0,1},{1,0},{2,3},{3,2},{4,5},{5,4},{6,7},{7,6},{8,9},{9,8},{10,11... | collective-permute-start | bytes 835592 | tf_op jit(solution)/shard_map/ppermute | solution.py:414
  15.1 5.2 %collective-permute-start.1 = (f32[136,256]{1,0:T(8,128)S(1)}, f32[136,256]{1,0:T(8,128)S(1)}, u32[]{:S(2)}, u32[]{:S(2)}) collective-permute-start(f32[136,256]{1,0:T(8,128)S(1)} %fusion), channel_id=1, source_target_pairs={{0,4},{1,5},{2,6},{3,7},{4,0},{5,1},{6,2},{7,3},{8,12},{9,13},{10,... | collective-permute-start | bytes 417800 | tf_op jit(solution)/shard_map/ppermute | solution.py:420
  20.4 8.7 %collective-permute-start.2 = (f32[136,256]{1,0:T(8,128)S(1)}, f32[136,256]{1,0:T(8,128)S(1)}, u32[]{:S(2)}, u32[]{:S(2)}) collective-permute-start(f32[136,256]{1,0:T(8,128)S(1)} %fusion.2), channel_id=1, source_target_pairs={{0,8},{1,3},{2,10},{3,1},{4,12},{5,7},{6,14},{7,5},{8,0},{9,11},{1... | collective-permute-start | bytes 417800 | tf_op jit(solution)/shard_map/ppermute | solution.py:420
  29.1 12.6 %collective-permute-start.7 = (bf16[1024,512]{1,0:T(8,128)(2,1)S(1)}, bf16[1024,512]{1,0:T(8,128)(2,1)S(1)}, u32[]{:S(2)}, u32[]{:S(2)}) collective-permute-start(bf16[1024,512]{1,0:T(8,128)(2,1)S(1)} %collective-permute-done.6.refs_0_), channel_id=1, source_target_pairs={{0,1},{1,0},{2,3},{3,2},{4,5},{5,4},{6,7},{7,6},{8,9},{9,8},{10,11... | collective-permute-start | bytes 3145736 | tf_op jit(solution)/shard_map/ppermute | solution.py:426
  29.4 4.9 %collective-permute-start.3 = (f32[136,256]{1,0:T(8,128)S(1)}, f32[136,256]{1,0:T(8,128)S(1)}, u32[]{:S(2)}, u32[]{:S(2)}) collective-permute-start(f32[136,256]{1,0:T(8,128)S(1)} %add.38), channel_id=1, source_target_pairs={{0,2},{1,9},{2,0},{3,11},{4,6},{5,13},{6,4},{7,15},{8,10},{9,1},{1... | collective-permute-start | bytes 417800 | tf_op jit(solution)/shard_map/ppermute | solution.py:420
  35.4 4.8 %collective-permute-start.4 = (bf16[128,256]{1,0:T(8,128)(2,1)S(1)}, bf16[128,256]{1,0:T(8,128)(2,1)S(1)}, u32[]{:S(2)}, u32[]{:S(2)}) collective-permute-start(bf16[128,256]{1,0:T(8,128)(2,1)S(1)} %mix.1.mine), channel_id=1, source_target_pairs={{0,4},{1,5},{2,6},{3,7},{4,0},{5,1},{6,2},{7,3},{8,12},{9,13},{10,... | collective-permute-start | bytes 196616 | tf_op jit(solution)/shard_map/ppermute | solution.py:420
  40.3 1.4 %collective-permute-start.5 = (bf16[2,128,256]{2,1,0:T(8,128)(2,1)S(1)}, bf16[2,128,256]{2,1,0:T(8,128)(2,1)S(1)}, u32[]{:S(2)}, u32[]{:S(2)}) collective-permute-start(bf16[2,128,256]{2,1,0:T(8,128)(2,1)S(1)} %pad_maximum_fusion.1), channel_id=1, source_target_pairs={{0,1},{1,0},{2,3},{3,2},{4,5},{5,4},{6,7},{7,6},{8,9},{9,8},{10,11... | collective-permute-start | bytes 393224 | tf_op jit(solution)/shard_map/ppermute | solution.py:430

commit v6 on v5

--- a/solution.py
+++ b/solution.py
@@ -88,8 +88,8 @@
     block = jnp.where(lax.div(col, head_size) == row, jnp.broadcast_to(wide, (heads, width)), 0.0)
     for i, part in enumerate(split3(block)):
         temp_t[i * heads : (i + 1) * heads, :] = part
-    x_t[...] = x_weight[...].astype(f32).T.astype(bf16)
-    fx_t[...] = fx_weight[...].astype(f32).T.astype(bf16)
+    x_t[...] = x_weight[...].T
+    fx_t[...] = fx_weight[...].T
 
     def own(h):
         return slice(h * head_size, (h + 1) * head_size)
@@ -160,7 +160,7 @@
         for h in range(half):
             queries[h, own(i), :] = part[own(h), :]
     values = dot(value_t[...], narrow).astype(bf16)
-    tokens[...] = dot(narrow.astype(f32).T.astype(bf16), repeat[...]).astype(bf16)
+    tokens[...] = dot(narrow.T, repeat[...]).astype(bf16)
     for h in range(half):
         scores[h] = dot(tokens[:, h * 128 : (h + 1) * 128], queries[h])
     for h in range(half):

time: 51.4 us -> 51.5 us (level)
  the two profiles are of different devices: /device:TPU:17 before, /device:TPU:25 now
where the time goes in v6:
time: 51.5 us; the launch traced here: 50.7 us
  waiting for transfers between devices  25.1 us (49%)
  Pallas kernels  19.6 us (38%)
  starting transfers between devices  3.05 us (6%)
  local copies, waits for them, and re-layouts  1.49 us (3%)
  other arithmetic  1.14 us (2%)
    ppermute x4, waiting for transfers between devices, swap(): lax.ppermute(x, axes, [(i, i ^ (odd if i & 1 else even)) for i in range(d...  22.6 us
    pallas_call x1, Pallas kernels, front_call(): pl.pallas_call(functools.partial(front_kernel, zunit), in_specs=[SMEM, SM...  9.61 us
    pallas_call x1, Pallas kernels, back_call(): pl.pallas_call(functools.partial(back_kernel, zunit), in_specs=[SMEM, SME...  9 us
    ppermute x1, waiting for transfers between devices, per_device(): received = lax.ppermute(send, 'sub', [(0, 1), (1, 0)])  1.55 us
    dynamic_slice x1, local copies, waits for them, and re-layouts, per_device(): lax.dynamic_slice_in_dim(down_weight, core * piece, piece, 0)  1.41 us
    ppermute x1, starting transfers between devices, per_device(): lax.ppermute(half, 'ffn', [(i, (i + turn) % shards) for i in range(shards)])  1.21 us
    concatenate x1, other arithmetic, per_device(): halves = (jnp.concatenate(halves, 0),)  1.04 us
  transfers between devices with their start and end apart: 8, of which 6 were waited for; matrix products, arithmetic and copies ran while one was open for 0% of the time, Pallas kernels for 21%

profile of v6, /device:TPU:25, one launch (start us, length us, event | category | flops | bytes accessed | tf_op | source)
XLA Modules:
  0.0 50.7 jit_solution(6456323123183587368)
XLA Ops:
  0.0 0.0 copy-start.6
  0.0 0.0 copy-start.7
  0.0 0.0 copy-start.9
  0.0 0.0 copy-start.10
  0.0 1.4 %constant_dynamic-slice_fusion = (bf16[512,512]{1,0:T(8,128)(2,1)S(1)}, bf16[512,512]{1,0:T(8,128)(2,1)S(1)}) fusion(bf16[1024,512]{1,0:T(8,128)(2,1)} %down.1, s32[]{:T(128)S(6)} %select_n.4, bf16[512,1024]{1,0:T(8,128)(2,1)} %up.1), kind=kLoop, calls=%fused_computation.9 | loop fusion | bytes 2097156 | tf_op jit(solution)/shard_map/dynamic_slice | solution.py:401
  1.5 1.0 %pad_maximum_fusion = bf16[1024,512]{1,0:T(8,128)(2,1)} fusion(bf16[512,512]{1,0:T(8,128)(2,1)S(1)} %get-tuple-element.15, bf16[512,512]{1,0:T(8,128)(2,1)S(1)} %get-tuple-element.16), kind=kLoop, calls=%fused_computation | loop fusion | flops 2097152 | bytes 2097152 | tf_op jit(solution)/shard_map/concatenate | solution.py:404
  2.5 1.2 %collective-permute-start.6 = (bf16[1024,512]{1,0:T(8,128)(2,1)}, bf16[1024,512]{1,0:T(8,128)(2,1)S(1)}, u32[]{:S(2)}, u32[]{:S(2)}) collective-permute-start(bf16[1024,512]{1,0:T(8,128)(2,1)} %pad_maximum_fusion), channel_id=1, source_target_pairs={{0,2},{2,0},{1,3},{3,1},{4,6},{6,4},{5,7},{7,5},{8,10},{10,8},{9,1... | collective-permute-start | bytes 3145736 | tf_op jit(solution)/shard_map/ppermute | solution.py:406
  3.7 0.0 copy-done
  3.7 0.0 copy-done.3
  3.7 0.0 copy-done.6
  3.8 9.6 %front.1 = (bf16[2,4096,512]{2,1,0:T(8,128)(2,1)S(1)}, f32[2,136,256]{2,1,0:T(8,128)S(1)}, f32[2,136,256]{2,1,0:T(8,128)S(1)}) custom-call(s32[16]{0:T(128)S(1)} %copy-done.9, s32[1]{0:T(128)} %bitcast.place, f32[1,512]{1,0:T(1,128)S(1)} %bitcast.18, bf16[32,256]{1,0:T(8,128)(2,1)S(1)} %copy-done.6, f32[1,32]{1,0:T(1,128)S(1)} %bitcast.20, ...), custom_call_target="tpu_custom_call" | custom-call | tf_op jit(solution)/shard_map/front/pallas_call | solution.py:296
  13.4 0.0 copy-start.1
  13.4 0.0 copy-start.2
  13.4 0.0 copy-start.5
  13.4 0.0 copy-start.8
  13.4 0.1 collective-permute-start
  13.5 1.5 %collective-permute-done = f32[2,136,256]{2,1,0:T(8,128)S(1)} collective-permute-done((f32[2,136,256]{2,1,0:T(8,128)S(1)}, f32[2,136,256]{2,1,0:T(8,128)S(1)}, u32[]{:S(2)}, u32[]{:S(2)}) %collective-permute-start) | collective-permute-done | bytes 278560 | tf_op jit(solution)/shard_map/ppermute | solution.py:414
  15.1 0.8 %collective-permute-start.1 = (f32[136,256]{1,0:T(8,128)S(1)}, f32[136,256]{1,0:T(8,128)S(1)}, u32[]{:S(2)}, u32[]{:S(2)}) collective-permute-start(f32[136,256]{1,0:T(8,128)S(1)} %fusion), channel_id=1, source_target_pairs={{0,4},{1,5},{2,6},{3,7},{4,0},{5,1},{6,2},{7,3},{8,12},{9,13},{10,... | collective-permute-start | bytes 417800 | tf_op jit(solution)/shard_map/ppermute | solution.py:420
  15.9 4.4 %collective-permute-done.1 = f32[136,256]{1,0:T(8,128)S(1)} collective-permute-done((f32[136,256]{1,0:T(8,128)S(1)}, f32[136,256]{1,0:T(8,128)S(1)}, u32[]{:S(2)}, u32[]{:S(2)}) %collective-permute-start.1) | collective-permute-done | bytes 139296 | tf_op jit(solution)/shard_map/ppermute | solution.py:420
  20.3 0.1 collective-permute-start.2
  20.4 8.7 %collective-permute-done.2 = f32[136,256]{1,0:T(8,128)S(1)} collective-permute-done((f32[136,256]{1,0:T(8,128)S(1)}, f32[136,256]{1,0:T(8,128)S(1)}, u32[]{:S(2)}, u32[]{:S(2)}) %collective-permute-start.2) | collective-permute-done | bytes 139296 | tf_op jit(solution)/shard_map/ppermute | solution.py:420
  29.1 0.0 collective-permute-done.6.refs_0_
  29.1 0.3 collective-permute-start.7
  29.4 0.1 collective-permute-start.3
  29.5 6.1 %collective-permute-done.3 = f32[136,256]{1,0:T(8,128)S(1)} collective-permute-done((f32[136,256]{1,0:T(8,128)S(1)}, f32[136,256]{1,0:T(8,128)S(1)}, u32[]{:S(2)}, u32[]{:S(2)}) %collective-permute-start.3) | collective-permute-done | bytes 139296 | tf_op jit(solution)/shard_map/ppermute | solution.py:420
  35.7 1.0 %mix.1.mine = bf16[128,256]{1,0:T(8,128)(2,1)S(1)} custom-call(f32[136,256]{1,0:T(8,128)S(1)} %add.39.sums, bf16[32,32]{1,0:T(8,128)(2,1)S(1)} %copy-done.11, bf16[32,32]{1,0:T(8,128)(2,1)S(1)} %copy-done.12, bf16[32,32]{1,0:T(8,128)(2,1)S(1)} %copy-done.13), custom_call_target="tpu_custom_call" | custom-call | flops 300000000 | bytes 500000 | tf_op jit(solution)/shard_map/mix/pallas_call | solution.py:332
  36.7 0.1 collective-permute-start.4
  36.8 3.4 %collective-permute-done.4.along = bf16[128,256]{1,0:T(8,128)(2,1)S(1)} collective-permute-done((bf16[128,256]{1,0:T(8,128)(2,1)S(1)}, bf16[128,256]{1,0:T(8,128)(2,1)S(1)}, u32[]{:S(2)}, u32[]{:S(2)}) %collective-permute-start.4) | collective-permute-done | bytes 65568 | tf_op jit(solution)/shard_map/ppermute | solution.py:420
  40.2 0.4 collective-permute-start.5
  40.6 1.0 %collective-permute-done.5 = bf16[2,128,256]{2,1,0:T(8,128)(2,1)S(1)} collective-permute-done((bf16[2,128,256]{2,1,0:T(8,128)(2,1)S(1)}, bf16[2,128,256]{2,1,0:T(8,128)(2,1)S(1)}, u32[]{:S(2)}, u32[]{:S(2)}) %collective-permute-start.5) | collective-permute-done | bytes 131104 | tf_op jit(solution)/shard_map/ppermute | solution.py:430
  41.6 0.0 collective-permute-done.7.refs_1_
  41.7 9.0 %back.1 = bf16[1024,512]{1,0:T(8,128)(2,1)} custom-call(s32[16]{0:T(128)S(1)} %copy-done.9, s32[1]{0:T(128)} %bitcast.place, bf16[2,4096,512]{2,1,0:T(8,128)(2,1)S(1)} %get-tuple-element.9.stored, bf16[128,256]{1,0:T(8,128)(2,1)S(1)} %mix.1.mine, bf16[128,256]{1,0:T(8,128)(2,1)S(1)} %get-tuple-element.14.across, ...), custom_call_target="tpu_custom_call" | custom-call | tf_op jit(solution)/shard_map/back/pallas_call | solution.py:348
  (23 shorter events, 0.1 us)
Async XLA Ops:
  0.0 3.7 %copy-start = (bf16[1024,512]{1,0:T(8,128)(2,1)S(1)}, bf16[1024,512]{1,0:T(8,128)(2,1)}, u32[]{:S(2)}) copy-start(bf16[1024,512]{1,0:T(8,128)(2,1)} %points.3) | copy-start | bytes 3145732
  0.0 3.7 %copy-start.3 = (bf16[512,512]{1,0:T(8,128)(2,1)S(1)}, bf16[512,512]{1,0:T(8,128)(2,1)}, u32[]{:S(2)}) copy-start(bf16[512,512]{1,0:T(8,128)(2,1)} %fx_weight.1) | copy-start | bytes 1572868
  0.0 3.7 %copy-start.4 = (bf16[512,512]{1,0:T(8,128)(2,1)S(1)}, bf16[512,512]{1,0:T(8,128)(2,1)}, u32[]{:S(2)}) copy-start(bf16[512,512]{1,0:T(8,128)(2,1)} %x_weight.1) | copy-start | bytes 1572868
  0.0 3.7 %copy-start.6 = (bf16[32,256]{1,0:T(8,128)(2,1)S(1)}, bf16[32,256]{1,0:T(8,128)(2,1)}, u32[]{:S(2)}) copy-start(bf16[32,256]{1,0:T(8,128)(2,1)} %slice_weight.1) | copy-start | bytes 49156
  0.0 3.7 %copy-start.7 = (f32[512]{0:T(512)S(1)}, f32[512]{0:T(512)}, u32[]{:S(2)}) copy-start(f32[512]{0:T(512)} %param.16) | copy-start | bytes 6148
  0.0 3.7 %copy-start.9 = (s32[16]{0:T(128)S(1)}, s32[16]{0:T(128)}, u32[]{:S(2)}) copy-start(s32[16]{0:T(128)} %sizes.3) | copy-start | bytes 196
  0.0 3.7 %copy-start.10 = (f32[32]{0:T(128)S(1)}, f32[32]{0:T(128)}, u32[]{:S(2)}) copy-start(f32[32]{0:T(128)} %param.20) | copy-start | bytes 388
  2.5 33.1 %copy-start.11 = (bf16[32,32]{1,0:T(8,128)(2,1)S(1)}, bf16[32,32]{1,0:T(8,128)(2,1)}, u32[]{:S(2)}) copy-start(bf16[32,32]{1,0:T(8,128)(2,1)} %q_weight.1) | copy-start | bytes 6148
  2.5 33.2 %copy-start.12 = (bf16[32,32]{1,0:T(8,128)(2,1)S(1)}, bf16[32,32]{1,0:T(8,128)(2,1)}, u32[]{:S(2)}) copy-start(bf16[32,32]{1,0:T(8,128)(2,1)} %k_weight.1) | copy-start | bytes 6148
  2.5 33.2 %copy-start.13 = (bf16[32,32]{1,0:T(8,128)(2,1)S(1)}, bf16[32,32]{1,0:T(8,128)(2,1)}, u32[]{:S(2)}) copy-start(bf16[32,32]{1,0:T(8,128)(2,1)} %v_weight.1) | copy-start | bytes 6148
  2.5 26.6 %collective-permute-start.6 = (bf16[1024,512]{1,0:T(8,128)(2,1)}, bf16[1024,512]{1,0:T(8,128)(2,1)S(1)}, u32[]{:S(2)}, u32[]{:S(2)}) collective-permute-start(bf16[1024,512]{1,0:T(8,128)(2,1)} %pad_maximum_fusion), channel_id=1, source_target_pairs={{0,2},{2,0},{1,3},{3,1},{4,6},{6,4},{5,7},{7,5},{8,10},{10,8},{9,1... | collective-permute-start | bytes 3145736 | tf_op jit(solution)/shard_map/ppermute | solution.py:406
  13.4 28.3 %copy-start.1 = (bf16[512,1024]{1,0:T(8,128)(2,1)S(1)}, bf16[512,1024]{1,0:T(8,128)(2,1)}, u32[]{:S(2)}) copy-start(bf16[512,1024]{1,0:T(8,128)(2,1)} %up.1) | copy-start | bytes 3145732
  13.4 28.3 %copy-start.2 = (bf16[1024,512]{1,0:T(8,128)(2,1)S(1)}, bf16[1024,512]{1,0:T(8,128)(2,1)}, u32[]{:S(2)}) copy-start(bf16[1024,512]{1,0:T(8,128)(2,1)} %down.1) | copy-start | bytes 3145732
  13.4 28.3 %copy-start.5 = (bf16[512,512]{1,0:T(8,128)(2,1)S(1)}, bf16[512,512]{1,0:T(8,128)(2,1)}, u32[]{:S(2)}) copy-start(bf16[512,512]{1,0:T(8,128)(2,1)} %out_weight.1) | copy-start | bytes 1572868
  13.4 28.3 %copy-start.8 = (f32[512]{0:T(512)S(1)}, f32[512]{0:T(512)}, u32[]{:S(2)}) copy-start(f32[512]{0:T(512)} %param.25) | copy-start | bytes 6148
  13.4 1.6 %collective-permute-start = (f32[2,136,256]{2,1,0:T(8,128)S(1)}, f32[2,136,256]{2,1,0:T(8,128)S(1)}, u32[]{:S(2)}, u32[]{:S(2)}) collective-permute-start(f32[2,136,256]{2,1,0:T(8,128)S(1)} %get-tuple-element.11), channel_id=1, source_target_pairs={{0,1},{1,0},{2,3},{3,2},{4,5},{5,4},{6,7},{7,6},{8,9},{9,8},{10,11... | collective-permute-start | bytes 835592 | tf_op jit(solution)/shard_map/ppermute | solution.py:414
  15.1 5.2 %collective-permute-start.1 = (f32[136,256]{1,0:T(8,128)S(1)}, f32[136,256]{1,0:T(8,128)S(1)}, u32[]{:S(2)}, u32[]{:S(2)}) collective-permute-start(f32[136,256]{1,0:T(8,128)S(1)} %fusion), channel_id=1, source_target_pairs={{0,4},{1,5},{2,6},{3,7},{4,0},{5,1},{6,2},{7,3},{8,12},{9,13},{10,... | collective-permute-start | bytes 417800 | tf_op jit(solution)/shard_map/ppermute | solution.py:420
  20.3 8.8 %collective-permute-start.2 = (f32[136,256]{1,0:T(8,128)S(1)}, f32[136,256]{1,0:T(8,128)S(1)}, u32[]{:S(2)}, u32[]{:S(2)}) collective-permute-start(f32[136,256]{1,0:T(8,128)S(1)} %fusion.2), channel_id=1, source_target_pairs={{0,8},{1,3},{2,10},{3,1},{4,12},{5,7},{6,14},{7,5},{8,0},{9,11},{1... | collective-permute-start | bytes 417800 | tf_op jit(solution)/shard_map/ppermute | solution.py:420
  29.1 12.5 %collective-permute-start.7 = (bf16[1024,512]{1,0:T(8,128)(2,1)S(1)}, bf16[1024,512]{1,0:T(8,128)(2,1)S(1)}, u32[]{:S(2)}, u32[]{:S(2)}) collective-permute-start(bf16[1024,512]{1,0:T(8,128)(2,1)S(1)} %collective-permute-done.6.refs_0_), channel_id=1, source_target_pairs={{0,1},{1,0},{2,3},{3,2},{4,5},{5,4},{6,7},{7,6},{8,9},{9,8},{10,11... | collective-permute-start | bytes 3145736 | tf_op jit(solution)/shard_map/ppermute | solution.py:426
  29.4 6.2 %collective-permute-start.3 = (f32[136,256]{1,0:T(8,128)S(1)}, f32[136,256]{1,0:T(8,128)S(1)}, u32[]{:S(2)}, u32[]{:S(2)}) collective-permute-start(f32[136,256]{1,0:T(8,128)S(1)} %add.38), channel_id=1, source_target_pairs={{0,2},{1,9},{2,0},{3,11},{4,6},{5,13},{6,4},{7,15},{8,10},{9,1},{1... | collective-permute-start | bytes 417800 | tf_op jit(solution)/shard_map/ppermute | solution.py:420
  36.7 3.5 %collective-permute-start.4 = (bf16[128,256]{1,0:T(8,128)(2,1)S(1)}, bf16[128,256]{1,0:T(8,128)(2,1)S(1)}, u32[]{:S(2)}, u32[]{:S(2)}) collective-permute-start(bf16[128,256]{1,0:T(8,128)(2,1)S(1)} %mix.1.mine), channel_id=1, source_target_pairs={{0,4},{1,5},{2,6},{3,7},{4,0},{5,1},{6,2},{7,3},{8,12},{9,13},{10,... | collective-permute-start | bytes 196616 | tf_op jit(solution)/shard_map/ppermute | solution.py:420
  40.2 1.4 %collective-permute-start.5 = (bf16[2,128,256]{2,1,0:T(8,128)(2,1)S(1)}, bf16[2,128,256]{2,1,0:T(8,128)(2,1)S(1)}, u32[]{:S(2)}, u32[]{:S(2)}) collective-permute-start(bf16[2,128,256]{2,1,0:T(8,128)(2,1)S(1)} %pad_maximum_fusion.1), channel_id=1, source_target_pairs={{0,1},{1,0},{2,3},{3,2},{4,5},{5,4},{6,7},{7,6},{8,9},{9,8},{10,11... | collective-permute-start | bytes 393224 | tf_op jit(solution)/shard_map/ppermute | solution.py:430

commit v7 on v5

--- a/solution.py
+++ b/solution.py
@@ -426,9 +426,8 @@
             hops = [lax.ppermute(piece, "sub", [(0, 1), (1, 0)]) for piece in ready]
         sums = sums + swap(sums, even, odd)
     mine = mix_call(sums, q_weight, k_weight, v_weight)
-    along = swap(mine, zunit, zunit)
-    pair = lax.ppermute(jnp.stack([mine, along]), "sub", [(0, 1), (1, 0)])
-    tokens = [mine, pair[0], along, pair[1]]
+    across, along = swap(mine, 1, 1), swap(mine, zunit, zunit)
+    tokens = [mine, across, along, swap(along, 1, 1)]
     return back_call(
         zunit,
         part_sizes,

time: 51.4 us -> 51 us (level)
  the two profiles are of different devices: /device:TPU:17 before, /device:TPU:11 now
where the time goes in v7:
time: 51 us; the launch traced here: 50.7 us
  waiting for transfers between devices  22 us (43%)
  Pallas kernels  19.7 us (39%)
  starting transfers between devices  6.24 us (12%)
  local copies, waits for them, and re-layouts  1.48 us (3%)
  other arithmetic  1.13 us (2%)
    ppermute x6, waiting for transfers between devices, swap(): lax.ppermute(x, axes, [(i, i ^ (odd if i & 1 else even)) for i in range(d...  20.8 us
    pallas_call x1, Pallas kernels, front_call(): pl.pallas_call(functools.partial(front_kernel, zunit), in_specs=[SMEM, SM...  9.65 us
    pallas_call x1, Pallas kernels, back_call(): pl.pallas_call(functools.partial(back_kernel, zunit), in_specs=[SMEM, SME...  8.99 us
    ppermute x6, starting transfers between devices, swap(): lax.ppermute(x, axes, [(i, i ^ (odd if i & 1 else even)) for i in range(d...  4.66 us
    dynamic_slice x1, local copies, waits for them, and re-layouts, per_device(): lax.dynamic_slice_in_dim(down_weight, core * piece, piece, 0)  1.41 us
    ppermute x1, waiting for transfers between devices, per_device(): received = lax.ppermute(send, 'sub', [(0, 1), (1, 0)])  1.19 us
    concatenate x1, other arithmetic, per_device(): halves = (jnp.concatenate(halves, 0),)  1.04 us
    ppermute x1, starting transfers between devices, per_device(): received = lax.ppermute(send, 'sub', [(0, 1), (1, 0)])  1.02 us
  transfers between devices with their start and end apart: 9, of which 6 were waited for; matrix products, arithmetic and copies ran while one was open for 0% of the time, Pallas kernels for 21%

profile of v7, /device:TPU:11, one launch (start us, length us, event | category | flops | bytes accessed | tf_op | source)
XLA Modules:
  0.0 50.7 jit_solution(9663394390496029341)
XLA Ops:
  0.0 0.0 copy-start.6
  0.0 1.4 %constant_dynamic-slice_fusion = (bf16[512,512]{1,0:T(8,128)(2,1)S(1)}, bf16[512,512]{1,0:T(8,128)(2,1)S(1)}) fusion(bf16[1024,512]{1,0:T(8,128)(2,1)} %down.1, s32[]{:T(128)S(6)} %select_n.4, bf16[512,1024]{1,0:T(8,128)(2,1)} %up.1), kind=kLoop, calls=%fused_computation.6 | loop fusion | bytes 2097156 | tf_op jit(solution)/shard_map/dynamic_slice | solution.py:401
  1.5 1.0 %pad_maximum_fusion = bf16[1024,512]{1,0:T(8,128)(2,1)} fusion(bf16[512,512]{1,0:T(8,128)(2,1)S(1)} %get-tuple-element.13, bf16[512,512]{1,0:T(8,128)(2,1)S(1)} %get-tuple-element.14), kind=kLoop, calls=%fused_computation | loop fusion | flops 2097152 | bytes 2097152 | tf_op jit(solution)/shard_map/concatenate | solution.py:404
  2.5 0.3 collective-permute-start.7
  2.8 0.0 copy-done
  2.8 0.0 copy-done.7
  2.8 0.0 copy-done.9
  2.8 0.0 copy-done.10
  2.8 0.0 copy-start.1
  2.8 0.0 copy-start.2
  2.8 0.0 copy-start.5
  2.8 0.0 copy-start.8
  2.9 9.7 %front.1 = (bf16[2,4096,512]{2,1,0:T(8,128)(2,1)S(1)}, f32[2,136,256]{2,1,0:T(8,128)S(1)}, f32[2,136,256]{2,1,0:T(8,128)S(1)}) custom-call(s32[16]{0:T(128)S(1)} %copy-done.9, s32[1]{0:T(128)} %bitcast.place, f32[1,512]{1,0:T(1,128)S(1)} %bitcast.10, bf16[32,256]{1,0:T(8,128)(2,1)S(1)} %copy-done.6, f32[1,32]{1,0:T(1,128)S(1)} %bitcast.12, ...), custom_call_target="tpu_custom_call" | custom-call | tf_op jit(solution)/shard_map/front/pallas_call | solution.py:296
  12.5 1.0 %collective-permute-start = (f32[2,136,256]{2,1,0:T(8,128)S(1)}, f32[2,136,256]{2,1,0:T(8,128)S(1)}, u32[]{:S(2)}, u32[]{:S(2)}) collective-permute-start(f32[2,136,256]{2,1,0:T(8,128)S(1)} %get-tuple-element.11), channel_id=1, source_target_pairs={{0,1},{1,0},{2,3},{3,2},{4,5},{5,4},{6,7},{7,6},{8,9},{9,8},{10,11... | collective-permute-start | bytes 835592 | tf_op jit(solution)/shard_map/ppermute | solution.py:414
  13.5 1.2 %collective-permute-done = f32[2,136,256]{2,1,0:T(8,128)S(1)} collective-permute-done((f32[2,136,256]{2,1,0:T(8,128)S(1)}, f32[2,136,256]{2,1,0:T(8,128)S(1)}, u32[]{:S(2)}, u32[]{:S(2)}) %collective-permute-start) | collective-permute-done | bytes 278560 | tf_op jit(solution)/shard_map/ppermute | solution.py:414
  14.7 0.1 collective-permute-start.1
  14.8 4.9 %collective-permute-done.1 = f32[136,256]{1,0:T(8,128)S(1)} collective-permute-done((f32[136,256]{1,0:T(8,128)S(1)}, f32[136,256]{1,0:T(8,128)S(1)}, u32[]{:S(2)}, u32[]{:S(2)}) %collective-permute-start.1) | collective-permute-done | bytes 139296 | tf_op jit(solution)/shard_map/ppermute | solution.py:420
  19.7 0.9 %collective-permute-start.2 = (f32[136,256]{1,0:T(8,128)S(1)}, f32[136,256]{1,0:T(8,128)S(1)}, u32[]{:S(2)}, u32[]{:S(2)}) collective-permute-start(f32[136,256]{1,0:T(8,128)S(1)} %fusion.2), channel_id=1, source_target_pairs={{0,8},{1,3},{2,10},{3,1},{4,12},{5,7},{6,14},{7,5},{8,0},{9,11},{1... | collective-permute-start | bytes 417800 | tf_op jit(solution)/shard_map/ppermute | solution.py:420
  20.7 8.4 %collective-permute-done.2 = f32[136,256]{1,0:T(8,128)S(1)} collective-permute-done((f32[136,256]{1,0:T(8,128)S(1)}, f32[136,256]{1,0:T(8,128)S(1)}, u32[]{:S(2)}, u32[]{:S(2)}) %collective-permute-start.2) | collective-permute-done | bytes 139296 | tf_op jit(solution)/shard_map/ppermute | solution.py:420
  29.1 0.0 collective-permute-done.7.refs_0_
  29.1 0.3 collective-permute-start.8
  29.4 2.3 %collective-permute-start.3 = (f32[136,256]{1,0:T(8,128)S(1)}, f32[136,256]{1,0:T(8,128)S(1)}, u32[]{:S(2)}, u32[]{:S(2)}) collective-permute-start(f32[136,256]{1,0:T(8,128)S(1)} %add.38), channel_id=1, source_target_pairs={{0,2},{1,9},{2,0},{3,11},{4,6},{5,13},{6,4},{7,15},{8,10},{9,1},{1... | collective-permute-start | bytes 417800 | tf_op jit(solution)/shard_map/ppermute | solution.py:420
  31.8 3.4 %collective-permute-done.3 = f32[136,256]{1,0:T(8,128)S(1)} collective-permute-done((f32[136,256]{1,0:T(8,128)S(1)}, f32[136,256]{1,0:T(8,128)S(1)}, u32[]{:S(2)}, u32[]{:S(2)}) %collective-permute-start.3) | collective-permute-done | bytes 139296 | tf_op jit(solution)/shard_map/ppermute | solution.py:420
  35.2 1.0 %mix.1.mine = bf16[128,256]{1,0:T(8,128)(2,1)S(1)} custom-call(f32[136,256]{1,0:T(8,128)S(1)} %add.39.sums, bf16[32,32]{1,0:T(8,128)(2,1)S(1)} %copy-done.11, bf16[32,32]{1,0:T(8,128)(2,1)S(1)} %copy-done.12, bf16[32,32]{1,0:T(8,128)(2,1)S(1)} %copy-done.13), custom_call_target="tpu_custom_call" | custom-call | flops 300000000 | bytes 500000 | tf_op jit(solution)/shard_map/mix/pallas_call | solution.py:332
  36.2 0.8 %collective-permute-start.5 = (bf16[128,256]{1,0:T(8,128)(2,1)S(1)}, bf16[128,256]{1,0:T(8,128)(2,1)S(1)}, u32[]{:S(2)}, u32[]{:S(2)}) collective-permute-start(bf16[128,256]{1,0:T(8,128)(2,1)S(1)} %mix.1.mine), channel_id=1, source_target_pairs={{0,4},{1,5},{2,6},{3,7},{4,0},{5,1},{6,2},{7,3},{8,12},{9,13},{10,... | collective-permute-start | bytes 196616 | tf_op jit(solution)/shard_map/ppermute | solution.py:420
  37.1 0.0 collective-permute-start.4
  37.1 3.2 %collective-permute-done.5.along = bf16[128,256]{1,0:T(8,128)(2,1)S(1)} collective-permute-done((bf16[128,256]{1,0:T(8,128)(2,1)S(1)}, bf16[128,256]{1,0:T(8,128)(2,1)S(1)}, u32[]{:S(2)}, u32[]{:S(2)}) %collective-permute-start.5) | collective-permute-done | bytes 65568 | tf_op jit(solution)/shard_map/ppermute | solution.py:420
  40.3 0.5 collective-permute-start.6
  40.8 0.0 collective-permute-done.4.across
  40.8 0.9 %collective-permute-done.6.corner = bf16[128,256]{1,0:T(8,128)(2,1)S(1)} collective-permute-done((bf16[128,256]{1,0:T(8,128)(2,1)S(1)}, bf16[128,256]{1,0:T(8,128)(2,1)S(1)}, u32[]{:S(2)}, u32[]{:S(2)}) %collective-permute-start.6) | collective-permute-done | bytes 65568 | tf_op jit(solution)/shard_map/ppermute | solution.py:420
  41.7 0.0 collective-permute-done.8.refs_1_
  41.7 9.0 %back.1 = bf16[1024,512]{1,0:T(8,128)(2,1)} custom-call(s32[16]{0:T(128)S(1)} %copy-done.9, s32[1]{0:T(128)} %bitcast.place, bf16[2,4096,512]{2,1,0:T(8,128)(2,1)S(1)} %get-tuple-element.9.stored, bf16[128,256]{1,0:T(8,128)(2,1)S(1)} %mix.1.mine, bf16[128,256]{1,0:T(8,128)(2,1)S(1)} %collective-permute-done.4.across, ...), custom_call_target="tpu_custom_call" | custom-call | tf_op jit(solution)/shard_map/back/pallas_call | solution.py:348
  (23 shorter events, 0.1 us)
Async XLA Ops:
  0.0 2.8 %copy-start = (bf16[1024,512]{1,0:T(8,128)(2,1)S(1)}, bf16[1024,512]{1,0:T(8,128)(2,1)}, u32[]{:S(2)}) copy-start(bf16[1024,512]{1,0:T(8,128)(2,1)} %points.3) | copy-start | bytes 3145732
  0.0 2.8 %copy-start.3 = (bf16[512,512]{1,0:T(8,128)(2,1)S(1)}, bf16[512,512]{1,0:T(8,128)(2,1)}, u32[]{:S(2)}) copy-start(bf16[512,512]{1,0:T(8,128)(2,1)} %fx_weight.1) | copy-start | bytes 1572868
  0.0 2.8 %copy-start.4 = (bf16[512,512]{1,0:T(8,128)(2,1)S(1)}, bf16[512,512]{1,0:T(8,128)(2,1)}, u32[]{:S(2)}) copy-start(bf16[512,512]{1,0:T(8,128)(2,1)} %x_weight.1) | copy-start | bytes 1572868
  0.0 2.8 %copy-start.6 = (bf16[32,256]{1,0:T(8,128)(2,1)S(1)}, bf16[32,256]{1,0:T(8,128)(2,1)}, u32[]{:S(2)}) copy-start(bf16[32,256]{1,0:T(8,128)(2,1)} %slice_weight.1) | copy-start | bytes 49156
  0.0 2.8 %copy-start.7 = (f32[512]{0:T(512)S(1)}, f32[512]{0:T(512)}, u32[]{:S(2)}) copy-start(f32[512]{0:T(512)} %param.16) | copy-start | bytes 6148
  0.0 2.8 %copy-start.9 = (s32[16]{0:T(128)S(1)}, s32[16]{0:T(128)}, u32[]{:S(2)}) copy-start(s32[16]{0:T(128)} %sizes.3) | copy-start | bytes 196
  0.0 2.8 %copy-start.10 = (f32[32]{0:T(128)S(1)}, f32[32]{0:T(128)}, u32[]{:S(2)}) copy-start(f32[32]{0:T(128)} %param.20) | copy-start | bytes 388
  2.5 32.7 %copy-start.11 = (bf16[32,32]{1,0:T(8,128)(2,1)S(1)}, bf16[32,32]{1,0:T(8,128)(2,1)}, u32[]{:S(2)}) copy-start(bf16[32,32]{1,0:T(8,128)(2,1)} %q_weight.1) | copy-start | bytes 6148
  2.5 32.7 %copy-start.12 = (bf16[32,32]{1,0:T(8,128)(2,1)S(1)}, bf16[32,32]{1,0:T(8,128)(2,1)}, u32[]{:S(2)}) copy-start(bf16[32,32]{1,0:T(8,128)(2,1)} %k_weight.1) | copy-start | bytes 6148
  2.5 32.7 %copy-start.13 = (bf16[32,32]{1,0:T(8,128)(2,1)S(1)}, bf16[32,32]{1,0:T(8,128)(2,1)}, u32[]{:S(2)}) copy-start(bf16[32,32]{1,0:T(8,128)(2,1)} %v_weight.1) | copy-start | bytes 6148
  2.5 26.6 %collective-permute-start.7 = (bf16[1024,512]{1,0:T(8,128)(2,1)}, bf16[1024,512]{1,0:T(8,128)(2,1)S(1)}, u32[]{:S(2)}, u32[]{:S(2)}) collective-permute-start(bf16[1024,512]{1,0:T(8,128)(2,1)} %pad_maximum_fusion), channel_id=1, source_target_pairs={{0,2},{2,0},{1,3},{3,1},{4,6},{6,4},{5,7},{7,5},{8,10},{10,8},{9,1... | collective-permute-start | bytes 3145736 | tf_op jit(solution)/shard_map/ppermute | solution.py:406
  2.8 38.9 %copy-start.1 = (bf16[512,1024]{1,0:T(8,128)(2,1)S(1)}, bf16[512,1024]{1,0:T(8,128)(2,1)}, u32[]{:S(2)}) copy-start(bf16[512,1024]{1,0:T(8,128)(2,1)} %up.1) | copy-start | bytes 3145732
  2.8 38.9 %copy-start.2 = (bf16[1024,512]{1,0:T(8,128)(2,1)S(1)}, bf16[1024,512]{1,0:T(8,128)(2,1)}, u32[]{:S(2)}) copy-start(bf16[1024,512]{1,0:T(8,128)(2,1)} %down.1) | copy-start | bytes 3145732
  2.8 38.9 %copy-start.5 = (bf16[512,512]{1,0:T(8,128)(2,1)S(1)}, bf16[512,512]{1,0:T(8,128)(2,1)}, u32[]{:S(2)}) copy-start(bf16[512,512]{1,0:T(8,128)(2,1)} %out_weight.1) | copy-start | bytes 1572868
  2.8 38.9 %copy-start.8 = (f32[512]{0:T(512)S(1)}, f32[512]{0:T(512)}, u32[]{:S(2)}) copy-start(f32[512]{0:T(512)} %param.25) | copy-start | bytes 6148
  12.5 2.2 %collective-permute-start = (f32[2,136,256]{2,1,0:T(8,128)S(1)}, f32[2,136,256]{2,1,0:T(8,128)S(1)}, u32[]{:S(2)}, u32[]{:S(2)}) collective-permute-start(f32[2,136,256]{2,1,0:T(8,128)S(1)} %get-tuple-element.11), channel_id=1, source_target_pairs={{0,1},{1,0},{2,3},{3,2},{4,5},{5,4},{6,7},{7,6},{8,9},{9,8},{10,11... | collective-permute-start | bytes 835592 | tf_op jit(solution)/shard_map/ppermute | solution.py:414
  14.7 5.0 %collective-permute-start.1 = (f32[136,256]{1,0:T(8,128)S(1)}, f32[136,256]{1,0:T(8,128)S(1)}, u32[]{:S(2)}, u32[]{:S(2)}) collective-permute-start(f32[136,256]{1,0:T(8,128)S(1)} %fusion), channel_id=1, source_target_pairs={{0,4},{1,5},{2,6},{3,7},{4,0},{5,1},{6,2},{7,3},{8,12},{9,13},{10,... | collective-permute-start | bytes 417800 | tf_op jit(solution)/shard_map/ppermute | solution.py:420
  19.7 9.4 %collective-permute-start.2 = (f32[136,256]{1,0:T(8,128)S(1)}, f32[136,256]{1,0:T(8,128)S(1)}, u32[]{:S(2)}, u32[]{:S(2)}) collective-permute-start(f32[136,256]{1,0:T(8,128)S(1)} %fusion.2), channel_id=1, source_target_pairs={{0,8},{1,3},{2,10},{3,1},{4,12},{5,7},{6,14},{7,5},{8,0},{9,11},{1... | collective-permute-start | bytes 417800 | tf_op jit(solution)/shard_map/ppermute | solution.py:420
  29.1 12.6 %collective-permute-start.8 = (bf16[1024,512]{1,0:T(8,128)(2,1)S(1)}, bf16[1024,512]{1,0:T(8,128)(2,1)S(1)}, u32[]{:S(2)}, u32[]{:S(2)}) collective-permute-start(bf16[1024,512]{1,0:T(8,128)(2,1)S(1)} %collective-permute-done.7.refs_0_), channel_id=1, source_target_pairs={{0,1},{1,0},{2,3},{3,2},{4,5},{5,4},{6,7},{7,6},{8,9},{9,8},{10,11... | collective-permute-start | bytes 3145736 | tf_op jit(solution)/shard_map/ppermute | solution.py:426
  29.4 5.7 %collective-permute-start.3 = (f32[136,256]{1,0:T(8,128)S(1)}, f32[136,256]{1,0:T(8,128)S(1)}, u32[]{:S(2)}, u32[]{:S(2)}) collective-permute-start(f32[136,256]{1,0:T(8,128)S(1)} %add.38), channel_id=1, source_target_pairs={{0,2},{1,9},{2,0},{3,11},{4,6},{5,13},{6,4},{7,15},{8,10},{9,1},{1... | collective-permute-start | bytes 417800 | tf_op jit(solution)/shard_map/ppermute | solution.py:420
  36.2 4.1 %collective-permute-start.5 = (bf16[128,256]{1,0:T(8,128)(2,1)S(1)}, bf16[128,256]{1,0:T(8,128)(2,1)S(1)}, u32[]{:S(2)}, u32[]{:S(2)}) collective-permute-start(bf16[128,256]{1,0:T(8,128)(2,1)S(1)} %mix.1.mine), channel_id=1, source_target_pairs={{0,4},{1,5},{2,6},{3,7},{4,0},{5,1},{6,2},{7,3},{8,12},{9,13},{10,... | collective-permute-start | bytes 196616 | tf_op jit(solution)/shard_map/ppermute | solution.py:420
  37.1 3.7 %collective-permute-start.4 = (bf16[128,256]{1,0:T(8,128)(2,1)S(1)}, bf16[128,256]{1,0:T(8,128)(2,1)S(1)}, u32[]{:S(2)}, u32[]{:S(2)}) collective-permute-start(bf16[128,256]{1,0:T(8,128)(2,1)S(1)} %mix.1.mine), channel_id=1, source_target_pairs={{0,1},{1,0},{2,3},{3,2},{4,5},{5,4},{6,7},{7,6},{8,9},{9,8},{10,11... | collective-permute-start | bytes 196616 | tf_op jit(solution)/shard_map/ppermute | solution.py:420
  40.3 1.4 %collective-permute-start.6 = (bf16[128,256]{1,0:T(8,128)(2,1)S(1)}, bf16[128,256]{1,0:T(8,128)(2,1)S(1)}, u32[]{:S(2)}, u32[]{:S(2)}) collective-permute-start(bf16[128,256]{1,0:T(8,128)(2,1)S(1)} %collective-permute-done.5.along), channel_id=1, source_target_pairs={{0,1},{1,0},{2,3},{3,2},{4,5},{5,4},{6,7},{7,6},{8,9},{9,8},{10,11... | collective-permute-start | bytes 196616 | tf_op jit(solution)/shard_map/ppermute | solution.py:420
